TPU v7x, 128 devices: a whole 4x4x4 slice. The times are simulated.
128 devices in a mesh: seed: 4 (over z), tok: 32 (over x, y, core).
Axes of the slice: x: 4, y: 4, z: 4, core: 2. Of those that a mesh axis runs over, the one named last changes fastest.
Arguments:
- atom_single: bfloat16 [32768, 128], P(('seed', 'tok')), parts along dimension 0, may hold values from -6 to 6
- atom_bias: bfloat16 [8192, 512], P('tok'), may hold values from -400 to 400
- atom_token: int32 [8192], P('tok'), may hold values from 0 to 1023, as said below
- atom_counts: int32 [1024], P('tok'), may hold values from 1 to 15, as said below
- pair_rep: bfloat16 [1024, 1024, 128], P('tok'), may hold values from -400 to 400
- atom_qkv_w: bfloat16 [128, 384], replicated, may hold values from -0.5 to 0.5
- atom_out_w: bfloat16 [128, 128], replicated, may hold values from -0.5 to 0.5
- agg_w: bfloat16 [128, 768], replicated, may hold values from -0.5 to 0.5
- tok_qkv_w: bfloat16 [2, 768, 2304], replicated, may hold values from -0.21875 to 0.21875
- tok_out_w: bfloat16 [2, 768, 768], replicated, may hold values from -0.4375 to 0.4375
- pair_w: bfloat16 [128, 32], replicated, may hold values from -0.5 to 0.5
- bcast_w: bfloat16 [768, 128], replicated, may hold values from -0.21875 to 0.21875
Outputs:
- atom_out: bfloat16 [32768, 128], P(('seed', 'tok')), parts along dimension 0
- token_out: bfloat16 [4096, 768], P(('seed', 'tok')), parts along dimension 0
There are 4 independent parts, one for each index of `seed`. A program takes and returns all parts, laid end to end along the dimension named above; an argument that names none is the same for every part. Nothing has to cross between parts.
Inputs may be any that keep to these rules, and one draw needn't show every extreme that they name: `atom_counts`: counts sum to 8192; the counts of the tokens of one index of tok sum to 256; the largest count is 15 and the smallest 1 in every draw. `atom_token`: token t holds exactly atom_counts[t] atoms, and the atoms of one token are consecutive. Along the atoms the tokens come in increasing order, except that at each boundary between neighbouring indices of tok the first token of the upper index comes just before the last token of the lower index; so every atom belongs to a token of its own index of tok or of a neighbouring one.
All inputs are finite; a program needn't handle non-finite values.
Results may differ from a plain program's by a relative error of at most 0.017.
Values may be sent and summed in bfloat16 or wider, within the bound.
No kernel may reach another device: no remote copies, remote signals or barrier semaphores. Data moves between devices by JAX's collectives and lax.ppermute only.
A program may use at most 128 MiB of HBM per device.

v0:
```python
import jax
import jax.numpy as jnp
from jax import lax
from jax.sharding import PartitionSpec as P

C = 768
H = 16
CA = 128
AH = 4
QW = 32
KW = 128
NB = 2
HALO = 48


def with_halo(cells, sides, width):
    for axis, dim in sides:
        count = lax.axis_size(axis)
        ends = count - 1
        head = lax.slice_in_dim(cells, 0, width, axis=dim)
        tail = lax.slice_in_dim(cells, cells.shape[dim] - width, cells.shape[dim], axis=dim)
        cells = jnp.concatenate(
            [
                lax.ppermute(tail, axis, [(i, (i + 1) % count) for i in range(ends)]),
                cells,
                lax.ppermute(head, axis, [((i + 1) % count, i) for i in range(ends)]),
            ],
            axis=dim,
        )
    return cells


def layer_norm(values):
    average = jnp.mean(values, axis=-1, keepdims=True)
    centred = values - average
    variance = jnp.mean(centred * centred, axis=-1, keepdims=True)
    return centred * lax.rsqrt(variance + 1e-05)


def window_attend(queries, keyvals, atom_bias, first_atom, atom_total):
    windows = keyvals.shape[0]
    head_width = CA // AH
    query_heads = queries.reshape(windows, QW, AH, head_width)
    key_heads = keyvals[:, :, :CA].reshape(windows, KW, AH, head_width)
    value_heads = keyvals[:, :, CA:].reshape(windows, KW, AH, head_width)
    scores = jnp.einsum(
        "wqhd,wkhd->whqk", query_heads, key_heads, preferred_element_type=jnp.float32
    ) * head_width ** (-0.5)
    scores = scores + atom_bias.reshape(windows, QW, AH, KW).transpose(0, 2, 1, 3).astype(
        jnp.float32
    )
    position = (
        first_atom
        + QW * jnp.arange(windows, dtype=jnp.int32)[:, None]
        - HALO
        + jnp.arange(KW, dtype=jnp.int32)[None, :]
    )
    inside = (position >= 0) & (position < atom_total)
    scores = jnp.where(inside[:, None, None, :], scores, -1000000000.0)
    maximum = jnp.max(scores, axis=-1, keepdims=True)
    powers = jnp.exp(scores - maximum)
    denominator = jnp.sum(powers, axis=-1)
    weights = powers.astype(jnp.bfloat16)
    mixed_heads = jnp.einsum(
        "whqk,wkhd->wqhd", weights, value_heads, preferred_element_type=jnp.float32
    )
    mixed_heads = mixed_heads / denominator.transpose(0, 2, 1)[..., None]
    return mixed_heads.reshape(windows * QW, CA).astype(jnp.bfloat16)


def member_product(member, lifted):
    upper = lifted.astype(jnp.bfloat16)
    lower = (lifted - upper.astype(jnp.float32)).astype(jnp.bfloat16)
    picker = member.astype(jnp.bfloat16)
    total = jnp.dot(picker, upper, preferred_element_type=jnp.float32)
    return total + jnp.dot(picker, lower, preferred_element_type=jnp.float32)


def local(
    atom_single,
    atom_bias,
    atom_token,
    atom_counts,
    pair_rep,
    atom_qkv_w,
    atom_out_w,
    agg_w,
    tok_qkv_w,
    tok_out_w,
    pair_w,
    bcast_w,
):
    local_atoms = atom_single.shape[0]
    local_tokens = atom_counts.shape[0]
    first_atom = lax.axis_index("tok") * local_atoms
    first_token = lax.axis_index("tok") * local_tokens
    hidden_in = atom_single.astype(jnp.float32)
    normed = layer_norm(hidden_in).astype(jnp.bfloat16)
    projected = jnp.dot(normed, atom_qkv_w, preferred_element_type=jnp.float32).astype(jnp.bfloat16)
    queries = projected[:, :CA]
    padded = with_halo(projected[:, CA:], (("tok", 0),), HALO)
    windows = local_atoms // QW
    gather_index = (
        QW * jnp.arange(windows, dtype=jnp.int32)[:, None]
        + jnp.arange(KW, dtype=jnp.int32)[None, :]
    )
    keyvals = padded[gather_index]
    attended = window_attend(
        queries, keyvals, atom_bias, first_atom, local_atoms * lax.axis_size("tok")
    )
    atom_hidden = (
        hidden_in + jnp.dot(attended, atom_out_w, preferred_element_type=jnp.float32)
    ).astype(jnp.bfloat16)
    lifted = jax.nn.relu(jnp.dot(atom_hidden, agg_w, preferred_element_type=jnp.float32))
    wanted = first_token - local_tokens + jnp.arange(3 * local_tokens, dtype=jnp.int32)
    member = atom_token[None, :] == wanted[:, None]
    partial_sums = member_product(member, lifted)
    outward = jnp.concatenate(
        [partial_sums[:local_tokens], partial_sums[2 * local_tokens :]], axis=0
    )
    received = with_halo(outward.astype(jnp.bfloat16), (("tok", 0),), local_tokens).astype(
        outward.dtype
    )
    token_sums = (
        partial_sums[local_tokens : 2 * local_tokens]
        + received[:local_tokens]
        + received[3 * local_tokens :]
    )
    stream = token_sums / atom_counts.astype(jnp.float32)[:, None]
    pair_bias = jnp.einsum(
        "ijc,ch->hij", pair_rep, pair_w, preferred_element_type=jnp.float32
    ).astype(jnp.bfloat16)
    head_size = C // H
    for layer_index in range(NB):
        normed = layer_norm(stream).astype(jnp.bfloat16)
        projected = jnp.dot(
            normed, tok_qkv_w[layer_index], preferred_element_type=jnp.float32
        ).astype(jnp.bfloat16)
        token_queries = projected[:, :C].reshape(local_tokens, H, head_size)
        token_keyvals = projected[:, C:]
        bias_layer = pair_bias[layer_index * H : (layer_index + 1) * H]

        def attend(running, shard_rows, offset, token_queries=token_queries, bias_layer=bias_layer):
            maximum, denominator, accumulated = running
            piece_rows = shard_rows.shape[0]
            key_heads = shard_rows[:, :C].reshape(piece_rows, H, head_size)
            value_heads = shard_rows[:, C:].reshape(piece_rows, H, head_size)
            scores = jnp.einsum(
                "qhd,khd->hqk", token_queries, key_heads, preferred_element_type=jnp.float32
            ) * head_size ** (-0.5)
            scores = scores + bias_layer.astype(jnp.float32)
            newmax = jnp.maximum(maximum, jnp.max(scores, axis=-1))
            powers = jnp.exp(scores - newmax[..., None])
            denominator = jnp.sum(powers, axis=-1)
            update = jnp.einsum(
                "hqk,khd->hqd",
                powers.astype(jnp.bfloat16),
                value_heads,
                preferred_element_type=jnp.float32,
            )
            accumulated = update
            return (newmax, denominator, accumulated)

        initial = (
            jnp.full((H, local_tokens), -1e30, jnp.float32),
            jnp.zeros((H, local_tokens), jnp.float32),
            jnp.zeros((H, local_tokens, head_size), jnp.float32),
        )
        maximum, denominator, accumulated = attend(
            initial, lax.all_gather(token_keyvals, "tok", axis=0, tiled=True), jnp.int32(0)
        )
        mixed_heads = (
            (accumulated / denominator[..., None])
            .transpose(1, 0, 2)
            .reshape(local_tokens, C)
            .astype(jnp.bfloat16)
        )
        stream = stream + jnp.dot(
            mixed_heads, tok_out_w[layer_index], preferred_element_type=jnp.float32
        )
    token_out = stream.astype(jnp.bfloat16)
    token_carry = jnp.dot(token_out, bcast_w, preferred_element_type=jnp.float32).astype(
        jnp.bfloat16
    )
    token_table = with_halo(token_carry, (("tok", 0),), local_tokens)
    picked = jnp.take(token_table, atom_token - first_token + local_tokens, axis=0)
    atom_out = (atom_hidden.astype(jnp.float32) + picked.astype(jnp.float32)).astype(jnp.bfloat16)
    return (atom_out, token_out)


def solution(mesh):
    placed = (
        P(("seed", "tok"), None),
        P("tok", None),
        P("tok"),
        P("tok"),
        P("tok", None, None),
        P(),
        P(),
        P(),
        P(),
        P(),
        P(),
        P(),
    )
    return jax.shard_map(
        local,
        mesh=mesh,
        in_specs=placed,
        out_specs=(P(("seed", "tok"), None), P(("seed", "tok"), None)),
        check_vma=False,
    )
```

profile of v0, /device:TPU:2, one launch (start us, length us, event | category | flops | bytes accessed | tf_op | source)
XLA Modules:
  0.0 187.3 jit_solution(11791085652193904835)
XLA Ops:
  10.5 1.9 %collective-permute-start = (bf16[48,256]{1,0:T(8,128)(2,1)S(1)}, bf16[48,256]{1,0:T(8,128)(2,1)S(1)}, u32[]{:S(2)}, u32[]{:S(2)}) collective-permute-start(bf16[48,256]{1,0:T(8,128)(2,1)S(1)} %get-tuple-element.12), channel_id=1, source_target_pairs={{0,1},{1,2},{2,3},{3,4},{4,5},{5,6},{6,7},{7,8},{8,9},{9,10},{10,1... | collective-permute-start | bytes 73736 | tf_op jit(solution)/shard_map/ppermute | solution.py:24
  12.4 5.8 %collective-permute-start.1 = (bf16[48,256]{1,0:T(8,128)(2,1)S(1)}, bf16[48,256]{1,0:T(8,128)(2,1)S(1)}, u32[]{:S(2)}, u32[]{:S(2)}) collective-permute-start(bf16[48,256]{1,0:T(8,128)(2,1)S(1)} %get-tuple-element.13), channel_id=1, source_target_pairs={{1,0},{2,1},{3,2},{4,3},{5,4},{6,5},{7,6},{8,7},{9,8},{10,9},{11,1... | collective-permute-start | bytes 73736 | tf_op jit(solution)/shard_map/ppermute | solution.py:26
  19.7 3.9 %gather_fusion = bf16[1024,256]{1,0:T(8,128)(2,1)S(1)} fusion(bf16[352,256]{1,0:T(8,128)(2,1)S(1)} %pad_maximum_fusion, s32[1024]{0:T(1024)S(1)} %fusion.76), kind=kCustom, calls=%fused_computation | custom fusion | bytes 1052672 | tf_op jit(solution)/shard_map/gather | solution.py:107
  26.7 1.9 %collective-permute-start.2 = (bf16[32,768]{1,0:T(8,128)(2,1)S(1)}, bf16[32,768]{1,0:T(8,128)(2,1)S(1)}, u32[]{:S(2)}, u32[]{:S(2)}) collective-permute-start(bf16[32,768]{1,0:T(8,128)(2,1)S(1)} %get-tuple-element.14), channel_id=1, source_target_pairs={{0,1},{1,2},{2,3},{3,4},{4,5},{5,6},{6,7},{7,8},{8,9},{9,10},{10,1... | collective-permute-start | bytes 147464 | tf_op jit(solution)/shard_map/ppermute | solution.py:24
  28.6 5.8 %collective-permute-start.3 = (bf16[32,768]{1,0:T(8,128)(2,1)S(1)}, bf16[32,768]{1,0:T(8,128)(2,1)S(1)}, u32[]{:S(2)}, u32[]{:S(2)}) collective-permute-start(bf16[32,768]{1,0:T(8,128)(2,1)S(1)} %get-tuple-element.15), channel_id=1, source_target_pairs={{1,0},{2,1},{3,2},{4,3},{5,4},{6,5},{7,6},{8,7},{9,8},{10,9},{11,1... | collective-permute-start | bytes 147464 | tf_op jit(solution)/shard_map/ppermute | solution.py:26
  34.4 1.7 collective-permute-done.3
  36.5 2.8 %fusion.6 = bf16[32,2304]{1,0:T(8,128)(2,1)S(1)} fusion(bf16[2,768,2304]{2,1,0:T(8,128)(2,1)} %param.20, f32[32,768]{1,0:T(8,128)S(1)} %get-tuple-element.5, f32[32]{0:T(128)S(1)} %add_rsqrt_fusion.2, f32[32]{0:T(128)S(1)} %broadcast_multiply_fusion.2), kind=kOutput, calls=%fused_computation.9 | convolution fusion | flops 113393664 | bytes 3784960 | tf_op jit(solution)/shard_map/dot_general | solution.py:136
  40.2 6.4 %fusion.73 = bf16[32,32,1024]{2,0,1:T(8,128)(2,1)S(1)} fusion(bf16[32,1024,128]{2,1,0:T(8,128)(2,1)} %param.16, bf16[128,32]{0,1:T(8,128)(2,1)S(1)} %copy-done.9), kind=kOutput, calls=%fused_computation.91 | convolution fusion | flops 268435456 | bytes 10493952 | tf_op jit(solution)/shard_map/ijc,ch->hij/dot_general | solution.py:130
  47.9 39.6 %all-gather.3.cloned.1.call-done = bf16[1024,1536]{1,0:T(8,128)(2,1)} async-done(((bf16[32,1536]{1,0:T(8,128)(2,1)}), bf16[1024,1536]{1,0:T(8,128)(2,1)}) %all-gather.3.cloned.1.call-update) | async-done | bytes 3145744 | tf_op jit(solution)/shard_map/all_gather | solution.py:170
  87.5 3.8 %fusion.83 = (bf16[1024,768]{1,0:T(8,128)(2,1)}, bf16[1024,768]{1,0:T(8,128)(2,1)}) fusion(bf16[1024,1536]{1,0:T(8,128)(2,1)} %all-gather.3.cloned.1.call-done), kind=kLoop, calls=%fused_computation.115 | loop fusion | bytes 6291456 | tf_op jit(solution)/shard_map/slice | solution.py:146
  91.3 2.6 %copy.29 = bf16[1024,768]{0,1:T(8,128)(2,1)} copy(bf16[1024,768]{1,0:T(8,128)(2,1)} %get-tuple-element.8) | data formatting | bytes 3145728 | tf_op jit(solution)/shard_map/slice | solution.py:146
  93.9 2.6 %copy.32 = bf16[1024,768]{0,1:T(8,128)(2,1)} copy(bf16[1024,768]{1,0:T(8,128)(2,1)} %get-tuple-element.9) | data formatting | bytes 3145728 | tf_op jit(solution)/shard_map/slice | solution.py:147
  96.5 2.1 %fusion.89 = (f32[16,32]{1,0:T(8,128)S(1)}, f32[16,32,1024]{2,1,0:T(8,128)S(1)}) fusion(bf16[32,32,1024]{2,1,0:T(8,128)(2,1)S(1)} %copy.48, bf16[1024,16,48]{0,2,1:T(8,128)(2,1)} %bitcast.81, bf16[32,16,48]{2,1,0:T(8,128)(2,1)S(1)} %reshape.169), kind=kOutput, calls=%fused_computation.121 | convolution fusion | flops 52428288 | bytes 4769792 | tf_op jit(solution)/shard_map/qhd,khd->hqk/dot_general | solution.py:148
  100.9 1.7 fusion.90
  102.8 2.8 %fusion.9 = bf16[32,2304]{1,0:T(8,128)(2,1)S(1)} fusion(bf16[2,768,2304]{2,1,0:T(8,128)(2,1)} %param.20, f32[32,768]{1,0:T(8,128)S(1)} %get-tuple-element.23, f32[32]{0:T(128)S(1)} %add_rsqrt_fusion.1, f32[32]{0:T(128)S(1)} %broadcast_multiply_fusion.1), kind=kOutput, calls=%fused_computation.10 | convolution fusion | flops 113393664 | bytes 3784960 | tf_op jit(solution)/shard_map/dot_general | solution.py:136
  106.5 44.3 %all-gather.5.cloned.1.call-done = bf16[1024,1536]{1,0:T(8,128)(2,1)} async-done(((bf16[32,1536]{1,0:T(8,128)(2,1)}), bf16[1024,1536]{1,0:T(8,128)(2,1)}) %all-gather.5.cloned.1.call-update) | async-done | bytes 3145744 | tf_op jit(solution)/shard_map/all_gather | solution.py:170
  150.7 3.8 %fusion.82 = (bf16[1024,768]{1,0:T(8,128)(2,1)}, bf16[1024,768]{1,0:T(8,128)(2,1)}) fusion(bf16[1024,1536]{1,0:T(8,128)(2,1)} %all-gather.5.cloned.1.call-done), kind=kLoop, calls=%fused_computation.114 | loop fusion | bytes 6291456 | tf_op jit(solution)/shard_map/slice | solution.py:146
  154.5 2.6 %copy.34 = bf16[1024,768]{0,1:T(8,128)(2,1)} copy(bf16[1024,768]{1,0:T(8,128)(2,1)} %get-tuple-element.6) | data formatting | bytes 3145728 | tf_op jit(solution)/shard_map/slice | solution.py:146
  157.1 3.4 %fusion.91 = (f32[16,32]{1,0:T(8,128)S(1)}, f32[16,32,1024]{2,1,0:T(8,128)}) fusion(bf16[32,32,1024]{2,1,0:T(8,128)(2,1)S(1)} %copy.48, bf16[1024,16,48]{0,2,1:T(8,128)(2,1)} %bitcast.82, bf16[32,16,48]{2,1,0:T(8,128)(2,1)S(1)} %reshape.172), kind=kOutput, calls=%fused_computation.123 | convolution fusion | flops 52428288 | bytes 4769792 | tf_op jit(solution)/shard_map/qhd,khd->hqk/dot_general | solution.py:148
  160.4 2.8 %copy.36 = bf16[1024,768]{0,1:T(8,128)(2,1)} copy(bf16[1024,768]{1,0:T(8,128)(2,1)} %get-tuple-element.7) | data formatting | bytes 3145728 | tf_op jit(solution)/shard_map/slice | solution.py:147
  165.5 1.6 fusion.37
  167.3 4.4 %collective-permute-start.5 = (bf16[32,128]{1,0:T(8,128)(2,1)S(1)}, bf16[32,128]{1,0:T(8,128)(2,1)S(1)}, u32[]{:S(2)}, u32[]{:S(2)}) collective-permute-start(bf16[32,128]{1,0:T(8,128)(2,1)S(1)} %convolution_convert_fusion.1), channel_id=1, source_target_pairs={{1,0},{2,1},{3,2},{4,3},{5,4},{6,5},{7,6},{8,7},{9,8},{10,9},{11,1... | collective-permute-start | bytes 24584 | tf_op jit(solution)/shard_map/ppermute | solution.py:26
  171.8 1.9 %collective-permute-start.4 = (bf16[32,128]{1,0:T(8,128)(2,1)S(1)}, bf16[32,128]{1,0:T(8,128)(2,1)S(1)}, u32[]{:S(2)}, u32[]{:S(2)}) collective-permute-start(bf16[32,128]{1,0:T(8,128)(2,1)S(1)} %convolution_convert_fusion.1), channel_id=1, source_target_pairs={{0,1},{1,2},{2,3},{3,4},{4,5},{5,6},{6,7},{7,8},{8,9},{9,10},{10,1... | collective-permute-start | bytes 24584 | tf_op jit(solution)/shard_map/ppermute | solution.py:24
  173.7 5.1 %collective-permute-done.4 = bf16[32,128]{1,0:T(8,128)(2,1)S(1)} collective-permute-done((bf16[32,128]{1,0:T(8,128)(2,1)S(1)}, bf16[32,128]{1,0:T(8,128)(2,1)S(1)}, u32[]{:S(2)}, u32[]{:S(2)}) %collective-permute-start.4) | collective-permute-done | bytes 8224 | tf_op jit(solution)/shard_map/ppermute | solution.py:24
  (90 shorter events, 17.6 us)
Async XLA Ops:
  7.2 18.8 %copy-start = (bf16[128,768]{1,0:T(8,128)(2,1)S(1)}, bf16[128,768]{1,0:T(8,128)(2,1)}, u32[]{:S(2)}) copy-start(bf16[128,768]{1,0:T(8,128)(2,1)} %param.19) | copy-start | bytes 589828
  7.2 80.3 %all-gather.3.cloned.1.call-start = ((), (), s32[]{:S(2)}) async-start(), calls=%async_computation | async-start | bytes 3244032 | tf_op jit(solution)/shard_map/all_gather | solution.py:170
  10.5 9.2 %collective-permute-start = (bf16[48,256]{1,0:T(8,128)(2,1)S(1)}, bf16[48,256]{1,0:T(8,128)(2,1)S(1)}, u32[]{:S(2)}, u32[]{:S(2)}) collective-permute-start(bf16[48,256]{1,0:T(8,128)(2,1)S(1)} %get-tuple-element.12), channel_id=1, source_target_pairs={{0,1},{1,2},{2,3},{3,4},{4,5},{5,6},{6,7},{7,8},{8,9},{9,10},{10,1... | collective-permute-start | bytes 73736 | tf_op jit(solution)/shard_map/ppermute | solution.py:24
  12.4 7.3 %collective-permute-start.1 = (bf16[48,256]{1,0:T(8,128)(2,1)S(1)}, bf16[48,256]{1,0:T(8,128)(2,1)S(1)}, u32[]{:S(2)}, u32[]{:S(2)}) collective-permute-start(bf16[48,256]{1,0:T(8,128)(2,1)S(1)} %get-tuple-element.13), channel_id=1, source_target_pairs={{1,0},{2,1},{3,2},{4,3},{5,4},{6,5},{7,6},{8,7},{9,8},{10,9},{11,1... | collective-permute-start | bytes 73736 | tf_op jit(solution)/shard_map/ppermute | solution.py:26
  24.5 1.2 copy-start.4
  24.5 1.2 copy-start.7
  25.0 1.2 copy-start.8
  25.7 8.7 %copy-start.10 = (s32[32]{0:T(128)S(1)}, s32[32]{0:T(128)}, u32[]{:S(2)}) copy-start(s32[32]{0:T(128)} %param.15) | copy-start | bytes 388
  26.7 7.7 %collective-permute-start.2 = (bf16[32,768]{1,0:T(8,128)(2,1)S(1)}, bf16[32,768]{1,0:T(8,128)(2,1)S(1)}, u32[]{:S(2)}, u32[]{:S(2)}) collective-permute-start(bf16[32,768]{1,0:T(8,128)(2,1)S(1)} %get-tuple-element.14), channel_id=1, source_target_pairs={{0,1},{1,2},{2,3},{3,4},{4,5},{5,6},{6,7},{7,8},{8,9},{9,10},{10,1... | collective-permute-start | bytes 147464 | tf_op jit(solution)/shard_map/ppermute | solution.py:24
  28.6 7.5 %collective-permute-start.3 = (bf16[32,768]{1,0:T(8,128)(2,1)S(1)}, bf16[32,768]{1,0:T(8,128)(2,1)S(1)}, u32[]{:S(2)}, u32[]{:S(2)}) collective-permute-start(bf16[32,768]{1,0:T(8,128)(2,1)S(1)} %get-tuple-element.15), channel_id=1, source_target_pairs={{1,0},{2,1},{3,2},{4,3},{5,4},{6,5},{7,6},{8,7},{9,8},{10,9},{11,1... | collective-permute-start | bytes 147464 | tf_op jit(solution)/shard_map/ppermute | solution.py:26
  36.3 3.9 %copy-start.9 = (bf16[128,32]{0,1:T(8,128)(2,1)S(1)}, bf16[128,32]{0,1:T(8,128)(2,1)}, u32[]{:S(2)}) copy-start(bf16[128,32]{0,1:T(8,128)(2,1)} %param.22) | copy-start | bytes 24580
  40.0 110.7 %all-gather.5.cloned.1.call-start = ((), (), s32[]{:S(2)}) async-start(), calls=%async_computation.1 | async-start | bytes 3244032 | tf_op jit(solution)/shard_map/all_gather | solution.py:170
  98.6 1.4 copy-start.2
  160.4 2.8 %copy-start.1 = (f32[16,32,1024]{2,1,0:T(8,128)S(1)}, f32[16,32,1024]{2,1,0:T(8,128)}, u32[]{:S(2)}) copy-start(f32[16,32,1024]{2,1,0:T(8,128)} %get-tuple-element.25) | copy-start | bytes 6291460
  163.2 1.4 copy-start.3
  164.6 2.5 %copy-start.6 = (bf16[768,128]{1,0:T(8,128)(2,1)S(1)}, bf16[768,128]{1,0:T(8,128)(2,1)}, u32[]{:S(2)}) copy-start(bf16[768,128]{1,0:T(8,128)(2,1)} %param.23) | copy-start | bytes 589828
  167.1 13.3 %copy-start.5 = (bf16[32,768]{1,0:T(8,128)(2,1)}, bf16[32,768]{1,0:T(8,128)(2,1)S(1)}, u32[]{:S(2)}) copy-start(bf16[32,768]{1,0:T(8,128)(2,1)S(1)} %fusion.37) | copy-start | bytes 147460
  167.3 6.4 %collective-permute-start.5 = (bf16[32,128]{1,0:T(8,128)(2,1)S(1)}, bf16[32,128]{1,0:T(8,128)(2,1)S(1)}, u32[]{:S(2)}, u32[]{:S(2)}) collective-permute-start(bf16[32,128]{1,0:T(8,128)(2,1)S(1)} %convolution_convert_fusion.1), channel_id=1, source_target_pairs={{1,0},{2,1},{3,2},{4,3},{5,4},{6,5},{7,6},{8,7},{9,8},{10,9},{11,1... | collective-permute-start | bytes 24584 | tf_op jit(solution)/shard_map/ppermute | solution.py:26
  171.8 7.1 %collective-permute-start.4 = (bf16[32,128]{1,0:T(8,128)(2,1)S(1)}, bf16[32,128]{1,0:T(8,128)(2,1)S(1)}, u32[]{:S(2)}, u32[]{:S(2)}) collective-permute-start(bf16[32,128]{1,0:T(8,128)(2,1)S(1)} %convolution_convert_fusion.1), channel_id=1, source_target_pairs={{0,1},{1,2},{2,3},{3,4},{4,5},{5,6},{6,7},{7,8},{8,9},{9,10},{10,1... | collective-permute-start | bytes 24584 | tf_op jit(solution)/shard_map/ppermute | solution.py:24
Sparse Core Ops, SparseCore 0:
  40.1 47.3 all-gather.2
  106.4 44.2 all-gather.4
where the time goes:
time: 188 us; the launch traced here: 187 us
  waiting for transfers between devices  90.7 us (48%)
  local copies, waits for them, and re-layouts  30.1 us (16%)
  matrix products  25 us (13%)
  starting transfers between devices  22 us (12%)
  between operations  14.5 us (8%)
  other arithmetic  4.94 us (3%)
    all_gather x2, waiting for transfers between devices, local(): lax.all_gather(token_keyvals, 'tok', axis=0, tiled=True)  83.8 us
    ppermute x3, starting transfers between devices, with_halo(): lax.ppermute(head, axis, [((i + 1) % count, i) for i in range(ends)])  16 us
    slice x4, local copies, waits for them, and re-layouts, attend(): key_heads = shard_rows[:, :C].reshape(piece_rows, H, head_size)  12.7 us
    dot_general x1, matrix products, local(): jnp.einsum('ijc,ch->hij', pair_rep, pair_w, preferred_element_type=jnp.fl...  6.35 us
    ppermute x3, starting transfers between devices, with_halo(): lax.ppermute(tail, axis, [(i, (i + 1) % count) for i in range(ends)])  5.76 us
    dot_general x2, matrix products, local(): jnp.dot(normed, tok_qkv_w[layer_index], preferred_element_type=jnp.float32)  5.57 us
    dot_general x2, matrix products, attend(): jnp.einsum('qhd,khd->hqk', token_queries, key_heads, preferred_element_ty...  5.49 us
    slice x2, local copies, waits for them, and re-layouts, attend(): value_heads = shard_rows[:, C:].reshape(piece_rows, H, head_size)  5.38 us
  transfers between devices with their start and end apart: 8, of which 4 were waited for; matrix products, arithmetic and copies ran while one was open for 5% of the time, Pallas kernels for 0%

commit v1 on v0

v1 whole, which is shorter than its diff:
```python
import functools

import jax
import jax.numpy as jnp
from jax import lax
from jax.experimental import pallas as pl
from jax.experimental.pallas import tpu as pltpu
from jax.sharding import PartitionSpec as P

C = 768
H = 16
HEAD = C // H
CA = 128
AH = 4
QW = 32
KW = 128
HALO = 48
EDGE = 16
REACH = EDGE + 64
TOKD = 32
ATOMD = 256
ROWS = 48
QROWS = 34 * H
KEYS = 1024
HALF = 512
CHUNK = 32
PACK = REACH + 4 * EDGE + 16
F32 = jnp.float32
BF16 = jnp.bfloat16

NT = (((1,), (1,)), ((), ()))


def params(mib):
    return pltpu.CompilerParams(vmem_limit_bytes=mib * 1024 * 1024)


VMEM = pl.BlockSpec(memory_space=pltpu.VMEM)


def layer_norm(values):
    average = jnp.mean(values, axis=-1, keepdims=True)
    centred = values - average
    variance = jnp.mean(centred * centred, axis=-1, keepdims=True)
    return centred * lax.rsqrt(variance + 1e-05)


def chunk_starts(tok):
    core, y, x = lax.rem(tok, 2), lax.rem(tok // 2, 4), tok // 8
    starts = []
    for j in range(32):
        slow, fast = (j % 16) // 4, j % 4
        plane = core if j < 16 else 1 - core
        kx = jnp.where(plane == 0, slow, fast)
        ky = jnp.where(plane == 0, fast, slow)
        starts.append((((x ^ kx) * 4 + (y ^ ky)) * 2 + plane) * CHUNK)
    return starts


def ordered(pair_ref, t, starts):
    return jnp.concatenate(
        [pair_ref[t, pl.ds(pl.multiple_of(s, CHUNK), CHUNK), :] for s in starts], axis=0
    )


def pack_kernel(single_ref, low_bias_ref, high_bias_ref, token_ref, low_pair_ref, high_pair_ref,
                pair_w_ref, down_ref, up_ref, down_bias_ref, up_bias_ref):
    tok = lax.axis_index("tok")
    base = tok * TOKD
    for out_ref, bias_ref, rows, lanes in (
        (down_ref, low_bias_ref, slice(0, REACH), slice(0, 128)),
        (up_ref, high_bias_ref, slice(ATOMD - REACH, ATOMD), slice(128, 256)),
    ):
        out_ref[:REACH] = single_ref[rows, :]
        for h in range(AH):
            out_ref[REACH + EDGE * h : REACH + EDGE * (h + 1)] = bias_ref[:, h * KW : (h + 1) * KW]
        relative = (token_ref[:, lanes] - base).astype(F32)
        out_ref[REACH + AH * EDGE :] = jnp.broadcast_to(relative, (16, 128)).astype(BF16)
    weights = pair_w_ref[...]
    for out_ref, pair_ref, owner in (
        (down_bias_ref, low_pair_ref, jnp.maximum(tok - 1, 0)),
        (up_bias_ref, high_pair_ref, jnp.minimum(tok + 1, 31)),
    ):
        rows = ordered(pair_ref, 0, chunk_starts(owner))
        out_ref[...] = lax.dot_general(weights, rows, NT, preferred_element_type=F32).astype(BF16)


STEP = 4


def bias_kernel(pair_ref, pair_w_ref, bias0_ref, bias1_ref):
    starts = chunk_starts(lax.axis_index("tok"))
    weights = pair_w_ref[...]
    for t in range(STEP):
        rows = ordered(pair_ref, t, starts)
        out = lax.dot_general(weights, rows, NT, preferred_element_type=F32).astype(BF16)
        bias0_ref[t * H : (t + 1) * H] = out[:H]
        bias1_ref[t * H : (t + 1) * H] = out[H:]


def atom_kernel(single_ref, lower_ref, upper_ref, bias_ref, token_ref, qkv_ref, out_w_ref, agg_ref,
                hidden_ref, stream_ref, normed_ref, own_ref, proj_ref, mixed_ref):
    tok = lax.axis_index("tok")
    first_atom = tok * ATOMD
    base = tok * TOKD
    everything = jnp.concatenate(
        [lower_ref[:REACH], single_ref[...], upper_ref[:REACH]], axis=0
    ).astype(F32)
    normed = layer_norm(everything).astype(BF16)
    proj_ref[...] = jnp.dot(normed, qkv_ref[...], preferred_element_type=F32).astype(BF16)
    head_of_lane = lax.broadcasted_iota(jnp.int32, (1, CA), 1) // (CA // AH)
    windows = [(REACH + QW * w, QW, 32 + QW * w, QW * w) for w in range(8)]
    windows += [(REACH + ATOMD, EDGE, 288, ATOMD), (REACH - EDGE, EDGE, 0, 384 - EDGE)]
    mixed_ref[ATOMD + EDGE : 384 - EDGE] = jnp.zeros((384 - 2 * EDGE - ATOMD, CA), BF16)
    for q_row, count, k_row, out_row in windows:
        queries = proj_ref[q_row : q_row + count, :CA]
        keys = proj_ref[k_row : k_row + KW, CA : 2 * CA]
        values = proj_ref[k_row : k_row + KW, 2 * CA :]
        stacked = jnp.concatenate(
            [jnp.where(head_of_lane == h, queries, jnp.zeros_like(queries)) for h in range(AH)], axis=0
        )
        if out_row < ATOMD:
            bias = [bias_ref[out_row : out_row + count, h * KW : (h + 1) * KW] for h in range(AH)]
        else:
            ref = upper_ref if out_row == ATOMD else lower_ref
            bias = [ref[REACH + EDGE * h : REACH + EDGE * (h + 1)] for h in range(AH)]
        scores = lax.dot_general(stacked, keys, NT, preferred_element_type=F32) * (CA // AH) ** (-0.5)
        scores = scores + jnp.concatenate(bias, axis=0).astype(F32)
        position = (
            first_atom + (k_row - REACH) + lax.broadcasted_iota(jnp.int32, (1, KW), 1)
        )
        inside = (position >= 0) & (position < 32 * ATOMD)
        scores = jnp.where(inside, scores, -1000000000.0)
        powers = jnp.exp(scores - jnp.max(scores, axis=-1, keepdims=True))
        total = jnp.sum(powers, axis=-1, keepdims=True)
        mixed = jnp.dot(powers.astype(BF16), values, preferred_element_type=F32) / total
        merged = jnp.where(head_of_lane == 0, mixed[:count], 0.0)
        for h in range(1, AH):
            merged = jnp.where(head_of_lane == h, mixed[h * count : (h + 1) * count], merged)
        mixed_ref[out_row : out_row + count] = merged.astype(BF16)
    hidden_in = jnp.concatenate(
        [
            single_ref[...],
            upper_ref[:EDGE],
            jnp.zeros((384 - 2 * EDGE - ATOMD, CA), BF16),
            lower_ref[REACH - EDGE : REACH],
        ],
        axis=0,
    ).astype(F32)
    hidden = (
        hidden_in + jnp.dot(mixed_ref[...], out_w_ref[...], preferred_element_type=F32)
    ).astype(BF16)
    hidden_ref[...] = hidden[:ATOMD]
    lifted = jnp.maximum(jnp.dot(hidden, agg_ref[...], preferred_element_type=F32), 0.0)
    lane = lax.broadcasted_iota(jnp.int32, (1, 128), 1)
    after = upper_ref[REACH + AH * EDGE :][:1].astype(F32).astype(jnp.int32) + TOKD
    before = lower_ref[REACH + AH * EDGE :][:1].astype(F32).astype(jnp.int32) - TOKD
    near = jnp.where(lane < EDGE, after, jnp.where(lane >= 128 - EDGE, before, -100))
    relative = jnp.concatenate([token_ref[...] - base, near], axis=1)
    row = lax.broadcasted_iota(jnp.int32, (ROWS, 1), 0)
    wanted = jnp.where(row < TOKD, row, jnp.where(row == TOKD, -1, jnp.where(row == TOKD + 1, TOKD, -200)))
    member = (relative == wanted).astype(F32)
    counts = jnp.maximum(jnp.sum(member, axis=-1, keepdims=True), 1.0)
    picker = member.astype(BF16)
    upper = lifted.astype(BF16)
    lower = (lifted - upper.astype(F32)).astype(BF16)
    sums = jnp.dot(picker, upper, preferred_element_type=F32)
    sums = sums + jnp.dot(picker, lower, preferred_element_type=F32)
    stream = sums / counts
    stream_ref[...] = stream
    out = layer_norm(stream).astype(BF16)
    normed_ref[...] = out
    own_ref[...] = out[:TOKD]


def head_mask():
    row = lax.broadcasted_iota(jnp.int32, (QROWS, 1), 0)
    lane = lax.broadcasted_iota(jnp.int32, (1, C), 1)
    start = (row & (H - 1)) * HEAD
    return (lane >= start) & (lane < start + HEAD)


def query_kernel(normed_ref, q_ref, k_ref, out_ref):
    queries = jnp.dot(normed_ref[...], q_ref[...], preferred_element_type=F32).astype(BF16)
    row = lax.broadcasted_iota(jnp.int32, (QROWS, ROWS), 0)
    column = lax.broadcasted_iota(jnp.int32, (QROWS, ROWS), 1)
    spread = ((row >> 4) == column).astype(F32).astype(BF16)
    repeated = jnp.dot(spread, queries, preferred_element_type=F32)
    repeated = jnp.where(head_mask(), repeated, 0.0).astype(BF16)
    lifted = lax.dot_general(repeated, k_ref[...], NT, preferred_element_type=F32)
    out_ref[...] = (lifted * HEAD ** (-0.5)).astype(BF16)


def attend(query_ref, near_ref, far_ref, bias_ref, edge_bias_ref, v_ref, out_w_ref, stream_ref):
    queries = query_ref[...]
    halves = []
    for i, ref in enumerate((near_ref, far_ref)):
        scores = lax.dot_general(queries, ref[...], NT, preferred_element_type=F32)
        bias = jnp.concatenate(
            [bias_ref[:, i * HALF : (i + 1) * HALF], edge_bias_ref[:, i * HALF : (i + 1) * HALF]], axis=0
        )
        halves.append(scores + bias.astype(F32))
    maximum = jnp.maximum(
        jnp.max(halves[0], axis=-1, keepdims=True), jnp.max(halves[1], axis=-1, keepdims=True)
    )
    total = 0.0
    mixed = 0.0
    for scores, ref in zip(halves, (near_ref, far_ref)):
        powers = jnp.exp(scores - maximum)
        total = total + jnp.sum(powers, axis=-1, keepdims=True)
        mixed = mixed + jnp.dot(powers.astype(BF16), ref[...], preferred_element_type=F32)
    mixed = (mixed / total).astype(BF16)
    valued = jnp.dot(mixed, v_ref[...], preferred_element_type=F32)
    valued = jnp.where(head_mask(), valued, 0.0).astype(BF16)
    row = lax.broadcasted_iota(jnp.int32, (ROWS, QROWS), 0)
    column = lax.broadcasted_iota(jnp.int32, (ROWS, QROWS), 1)
    gather = ((column >> 4) == row).astype(F32).astype(BF16)
    heads = jnp.dot(gather, valued, preferred_element_type=F32).astype(BF16)
    return stream_ref[...] + jnp.dot(heads, out_w_ref[...], preferred_element_type=F32)


def middle_kernel(*refs):
    stream_ref, normed_ref, own_ref = refs[8:]
    stream = attend(*refs[:8])
    stream_ref[...] = stream
    out = layer_norm(stream).astype(BF16)
    normed_ref[...] = out
    own_ref[...] = out[:TOKD]


def last_kernel(*refs):
    bcast_ref, token_ref, hidden_ref, atom_out_ref, token_out_ref = refs[8:]
    token_out = attend(*refs[:8]).astype(BF16)
    token_out_ref[...] = token_out[:TOKD]
    carry = jnp.dot(token_out, bcast_ref[...], preferred_element_type=F32).astype(BF16)
    relative = token_ref[...] - lax.axis_index("tok") * TOKD
    row = lax.broadcasted_iota(jnp.int32, (ROWS, 1), 0)
    wanted = jnp.where(row < TOKD, row, jnp.where(row == TOKD, -1, jnp.where(row == TOKD + 1, TOKD, -200)))
    member = (relative == wanted).astype(F32).astype(BF16)
    picked = lax.dot_general(member, carry, (((0,), (0,)), ((), ())), preferred_element_type=F32)
    atom_out_ref[...] = (hidden_ref[...].astype(F32) + picked).astype(BF16)


def flips(dx, dy, dc):
    pairs = []
    for tok in range(32):
        core, y, x = tok % 2, (tok // 2) % 4, tok // 8
        pairs.append((tok, ((x ^ dx) * 4 + (y ^ dy)) * 2 + (core ^ dc)))
    return pairs


def crossed(k, first):
    along_y, along_x = flips(0, k, 0), flips(k, 0, 0)
    return [
        (along_y if (tok % 2 == 0) == first else along_x)[tok] for tok in range(32)
    ]


def gather(own):
    for first in (True, False):
        own = jnp.concatenate(
            [own] + [lax.ppermute(own, "tok", crossed(k, first)) for k in (1, 2, 3)], axis=0
        )
    return own, lax.ppermute(own, "tok", flips(0, 0, 1))


def shape(rows, columns, dtype=BF16):
    return jax.ShapeDtypeStruct((rows, columns), dtype)


def local(atom_single, atom_bias, atom_token, atom_counts, pair_rep, atom_qkv_w, atom_out_w, agg_w,
          tok_qkv_w, tok_out_w, pair_w, bcast_w):
    tokens = atom_token.reshape(1, ATOMD)
    pair_wt = pair_w.T
    down = [(i + 1, i) for i in range(31)]
    up = [(i, i + 1) for i in range(31)]

    to_down, to_up, bias_down, bias_up = pl.pallas_call(
        pack_kernel,
        grid=(1,),
        in_specs=[
            pl.BlockSpec((ATOMD, CA), lambda i: (0, 0)),
            pl.BlockSpec((EDGE, AH * KW), lambda i: (0, 0)),
            pl.BlockSpec((EDGE, AH * KW), lambda i: (ATOMD // EDGE - 1, 0)),
            pl.BlockSpec((1, ATOMD), lambda i: (0, 0)),
            pl.BlockSpec((1, KEYS, 128), lambda i: (0, 0, 0)),
            pl.BlockSpec((1, KEYS, 128), lambda i: (TOKD - 1, 0, 0)),
            pl.BlockSpec((32, 128), lambda i: (0, 0)),
        ],
        out_specs=[pl.BlockSpec((PACK, CA), lambda i: (0, 0))] * 2 + [pl.BlockSpec((32, KEYS), lambda i: (0, 0))] * 2,
        out_shape=[shape(PACK, CA)] * 2 + [shape(32, KEYS)] * 2,
        compiler_params=params(8),
        name="pack",
    )(atom_single, atom_bias, atom_bias, tokens, pair_rep, pair_rep, pair_wt)
    from_upper = lax.ppermute(to_down, "tok", down)
    from_lower = lax.ppermute(to_up, "tok", up)
    upper_bias = lax.ppermute(bias_down, "tok", down)
    lower_bias = lax.ppermute(bias_up, "tok", up)

    bias = pl.pallas_call(
        bias_kernel,
        grid=(TOKD // STEP,),
        in_specs=[
            pl.BlockSpec((STEP, KEYS, 128), lambda i: (i, 0, 0)),
            pl.BlockSpec((32, 128), lambda i: (0, 0)),
        ],
        out_specs=[pl.BlockSpec((STEP * H, KEYS), lambda i: (i, 0))] * 2,
        out_shape=[shape(TOKD * H, KEYS)] * 2,
        compiler_params=params(12),
        cost_estimate=pl.CostEstimate(flops=2 * 32 * 1024 * 128 * 32, bytes_accessed=10 * 2**20, transcendentals=0),
        name="bias",
    )(pair_rep, pair_wt)
    edge_bias = [
        jnp.concatenate([lower_bias[b * H : (b + 1) * H], upper_bias[b * H : (b + 1) * H]], axis=0)
        for b in range(2)
    ]

    hidden, stream, normed, own = pl.pallas_call(
        atom_kernel,
        in_specs=[VMEM] * 8,
        out_specs=[VMEM] * 4,
        out_shape=[shape(ATOMD, CA), shape(ROWS, C, F32), shape(ROWS, C), shape(TOKD, C)],
        scratch_shapes=[pltpu.VMEM((2 * REACH + ATOMD, 3 * CA), BF16), pltpu.VMEM((384, CA), BF16)],
        compiler_params=params(16),
        name="atoms",
    )(atom_single, from_lower, from_upper, atom_bias, tokens, atom_qkv_w, atom_out_w, agg_w)

    for layer in range(2):
        near, far = gather(own)
        queries = pl.pallas_call(
            query_kernel,
            grid=(1,),
            in_specs=[
                pl.BlockSpec((ROWS, C), lambda i: (0, 0)),
                pl.BlockSpec((None, C, C), lambda i, layer=layer: (layer, 0, 0)),
                pl.BlockSpec((None, C, C), lambda i, layer=layer: (layer, 0, 1)),
            ],
            out_specs=pl.BlockSpec((QROWS, C), lambda i: (0, 0)),
            out_shape=shape(QROWS, C),
            compiler_params=params(20),
            cost_estimate=pl.CostEstimate(flops=10**9, bytes_accessed=5 * 2**20, transcendentals=0),
            name="queries",
        )(normed, tok_qkv_w, tok_qkv_w)
        whole = lambda rows, columns: pl.BlockSpec((rows, columns), lambda i: (0, 0))
        in_specs = [
            whole(QROWS, C),
            whole(HALF, C),
            whole(HALF, C),
            whole(TOKD * H, KEYS),
            whole(2 * H, KEYS),
            pl.BlockSpec((None, C, C), lambda i, layer=layer: (layer, 0, 2)),
            pl.BlockSpec((None, C, C), lambda i, layer=layer: (layer, 0, 0)),
            whole(ROWS, C),
        ]
        operands = (queries, near, far, bias[layer], edge_bias[layer], tok_qkv_w, tok_out_w, stream)
        if layer == 0:
            stream, normed, own = pl.pallas_call(
                middle_kernel,
                grid=(1,),
                in_specs=in_specs,
                out_specs=[whole(ROWS, C), whole(ROWS, C), whole(TOKD, C)],
                out_shape=[shape(ROWS, C, F32), shape(ROWS, C), shape(TOKD, C)],
                compiler_params=params(32),
                name="block",
            )(*operands)
        else:
            atom_out, token_out = pl.pallas_call(
                last_kernel,
                grid=(1,),
                in_specs=in_specs + [whole(C, CA), whole(1, ATOMD), whole(ATOMD, CA)],
                out_specs=[whole(ATOMD, CA), whole(TOKD, C)],
                out_shape=[shape(ATOMD, CA), shape(TOKD, C)],
                compiler_params=params(32),
                name="block_and_broadcast",
            )(*operands, bcast_w, tokens, hidden)
    return (atom_out, token_out)


def solution(mesh):
    placed = (
        P(("seed", "tok"), None),
        P("tok", None),
        P("tok"),
        P("tok"),
        P("tok", None, None),
        P(),
        P(),
        P(),
        P(),
        P(),
        P(),
        P(),
    )
    return jax.shard_map(
        local,
        mesh=mesh,
        in_specs=placed,
        out_specs=(P(("seed", "tok"), None), P(("seed", "tok"), None)),
        check_vma=False,
    )
```

time: 188 us -> 83.4 us (0.44)
  the two profiles are of different devices: /device:TPU:2 before, /device:TPU:1 now
where the time goes in v1:
time: 83.4 us; the launch traced here: 83.1 us
  starting transfers between devices  32.1 us (38%)
  waiting for transfers between devices  24.3 us (29%)
  Pallas kernels  18.6 us (22%)
  local copies, waits for them, and re-layouts  7.16 us (9%)
  between operations  0.99 us (1%)
    ppermute x12, waiting for transfers between devices, gather(): lax.ppermute(own, 'tok', crossed(k, first))  20.4 us
    ppermute x12, starting transfers between devices, gather(): lax.ppermute(own, 'tok', crossed(k, first))  15.2 us
    unnamed x44, local copies, waits for them, and re-layouts  7.1 us
    ppermute x2, starting transfers between devices, gather(): return (own, lax.ppermute(own, 'tok', flips(0, 0, 1)))  5.14 us
    ppermute x1, starting transfers between devices, local(): from_lower = lax.ppermute(to_up, 'tok', up)  4.86 us
    pallas_call x1, Pallas kernels, local(): pl.pallas_call(last_kernel, grid=(1,), in_specs=in_specs + [whole(C, CA),...  4.45 us
    pallas_call x1, Pallas kernels, local(): pl.pallas_call(bias_kernel, grid=(TOKD // STEP,), in_specs=[pl.BlockSpec(...  3.91 us
    pallas_call x1, Pallas kernels, local(): pl.pallas_call(middle_kernel, grid=(1,), in_specs=in_specs, out_specs=[wh...  3.69 us
  transfers between devices with their start and end apart: 18, of which 11 were waited for; matrix products, arithmetic and copies ran while one was open for 0% of the time, Pallas kernels for 8%

profile of v1, /device:TPU:1, one launch (start us, length us, event | category | flops | bytes accessed | tf_op | source)
XLA Modules:
  0.0 83.1 jit_solution(11328841385967234743)
XLA Ops:
  0.7 3.5 %copy-done = bf16[32,1024,128]{2,1,0:T(8,128)(2,1)S(1)} copy-done((bf16[32,1024,128]{2,1,0:T(8,128)(2,1)S(1)}, bf16[32,1024,128]{2,1,0:T(8,128)(2,1)}, u32[]{:S(2)}) %copy-start) | copy-done | bytes 8388632
  7.9 4.9 %collective-permute-start = (bf16[160,128]{1,0:T(8,128)(2,1)S(1)}, bf16[160,128]{1,0:T(8,128)(2,1)S(1)}, u32[]{:S(2)}, u32[]{:S(2)}) collective-permute-start(bf16[160,128]{1,0:T(8,128)(2,1)S(1)} %get-tuple-element.15), channel_id=1, source_target_pairs={{0,1},{1,2},{2,3},{3,4},{4,5},{5,6},{6,7},{7,8},{8,9},{9,10},{10,1... | collective-permute-start | bytes 122888 | tf_op jit(solution)/shard_map/ppermute | solution.py:296
  12.7 1.9 %collective-permute-start.1 = (bf16[160,128]{1,0:T(8,128)(2,1)S(1)}, bf16[160,128]{1,0:T(8,128)(2,1)S(1)}, u32[]{:S(2)}, u32[]{:S(2)}) collective-permute-start(bf16[160,128]{1,0:T(8,128)(2,1)S(1)} %get-tuple-element.16), channel_id=1, source_target_pairs={{1,0},{2,1},{3,2},{4,3},{5,4},{6,5},{7,6},{8,7},{9,8},{10,9},{11,1... | collective-permute-start | bytes 122888 | tf_op jit(solution)/shard_map/ppermute | solution.py:295
  14.7 3.4 %collective-permute-done.1.upper_ref = bf16[160,128]{1,0:T(8,128)(2,1)S(1)} collective-permute-done((bf16[160,128]{1,0:T(8,128)(2,1)S(1)}, bf16[160,128]{1,0:T(8,128)(2,1)S(1)}, u32[]{:S(2)}, u32[]{:S(2)}) %collective-permute-start.1) | collective-permute-done | bytes 40992 | tf_op jit(solution)/shard_map/ppermute | solution.py:295
  18.1 3.3 %atoms.1 = (bf16[256,128]{1,0:T(8,128)(2,1)S(1)}, f32[48,768]{1,0:T(8,128)S(1)}, bf16[48,768]{1,0:T(8,128)(2,1)S(1)}, bf16[32,768]{1,0:T(8,128)(2,1)S(1)}) custom-call(bf16[256,128]{1,0:T(8,128)(2,1)S(1)} %copy-done.6, bf16[160,128]{1,0:T(8,128)(2,1)S(1)} %collective-permute-done.lower_ref, bf16[160,128]{1,0:T(8,128)(2,1)S(1)} %collective-permute-done.1.upper_ref, ...), custom_call_target="tpu_custom_call" | custom-call | tf_op jit(solution)/shard_map/atoms/pallas_call | solution.py:318
  21.4 2.6 %collective-permute-start.4 = (bf16[32,768]{1,0:T(8,128)(2,1)S(1)}, bf16[32,768]{1,0:T(8,128)(2,1)S(1)}, u32[]{:S(2)}, u32[]{:S(2)}) collective-permute-start(bf16[32,768]{1,0:T(8,128)(2,1)S(1)} %get-tuple-element.18), channel_id=1, source_target_pairs={{0,6},{1,25},{2,4},{3,27},{4,2},{5,29},{6,0},{7,31},{8,14},{9,17},... | collective-permute-start | bytes 147464 | tf_op jit(solution)/shard_map/ppermute | solution.py:262
  24.8 3.0 %collective-permute-done.2 = bf16[32,768]{1,0:T(8,128)(2,1)S(1)} collective-permute-done((bf16[32,768]{1,0:T(8,128)(2,1)S(1)}, bf16[32,768]{1,0:T(8,128)(2,1)S(1)}, u32[]{:S(2)}, u32[]{:S(2)}) %collective-permute-start.2) | collective-permute-done | bytes 49184 | tf_op jit(solution)/shard_map/ppermute | solution.py:262
  28.7 1.2 %collective-permute-start.5 = (bf16[128,768]{1,0:T(8,128)(2,1)S(1)}, bf16[128,768]{1,0:T(8,128)(2,1)S(1)}, u32[]{:S(2)}, u32[]{:S(2)}) collective-permute-start(bf16[128,768]{1,0:T(8,128)(2,1)S(1)} %get-tuple-element.40), channel_id=1, source_target_pairs={{0,8},{1,3},{2,10},{3,1},{4,12},{5,7},{6,14},{7,5},{8,0},{9,11},{1... | collective-permute-start | bytes 589832 | tf_op jit(solution)/shard_map/ppermute | solution.py:262
  29.9 3.5 %collective-permute-start.6 = (bf16[128,768]{1,0:T(8,128)(2,1)S(1)}, bf16[128,768]{1,0:T(8,128)(2,1)S(1)}, u32[]{:S(2)}, u32[]{:S(2)}) collective-permute-start(bf16[128,768]{1,0:T(8,128)(2,1)S(1)} %get-tuple-element.40), channel_id=1, source_target_pairs={{0,16},{1,5},{2,18},{3,7},{4,20},{5,1},{6,22},{7,3},{8,24},{9,13},... | collective-permute-start | bytes 589832 | tf_op jit(solution)/shard_map/ppermute | solution.py:262
  33.6 5.2 %collective-permute-done.6 = bf16[128,768]{1,0:T(8,128)(2,1)S(1)} collective-permute-done((bf16[128,768]{1,0:T(8,128)(2,1)S(1)}, bf16[128,768]{1,0:T(8,128)(2,1)S(1)}, u32[]{:S(2)}, u32[]{:S(2)}) %collective-permute-start.6) | collective-permute-done | bytes 196640 | tf_op jit(solution)/shard_map/ppermute | solution.py:262
  38.8 2.1 %collective-permute-done.7 = bf16[128,768]{1,0:T(8,128)(2,1)S(1)} collective-permute-done((bf16[128,768]{1,0:T(8,128)(2,1)S(1)}, bf16[128,768]{1,0:T(8,128)(2,1)S(1)}, u32[]{:S(2)}, u32[]{:S(2)}) %collective-permute-start.7) | collective-permute-done | bytes 196640 | tf_op jit(solution)/shard_map/ppermute | solution.py:262
  41.6 3.0 %collective-permute-start.9 = (bf16[32,1024]{1,0:T(8,128)(2,1)S(1)}, bf16[32,1024]{1,0:T(8,128)(2,1)S(1)}, u32[]{:S(2)}, u32[]{:S(2)}) collective-permute-start(bf16[32,1024]{1,0:T(8,128)(2,1)S(1)} %get-tuple-element.20), channel_id=1, source_target_pairs={{0,1},{1,2},{2,3},{3,4},{4,5},{5,6},{6,7},{7,8},{8,9},{9,10},{10,1... | collective-permute-start | bytes 196616 | tf_op jit(solution)/shard_map/ppermute | solution.py:298
  44.6 1.9 %collective-permute-start.10 = (bf16[32,1024]{1,0:T(8,128)(2,1)S(1)}, bf16[32,1024]{1,0:T(8,128)(2,1)S(1)}, u32[]{:S(2)}, u32[]{:S(2)}) collective-permute-start(bf16[32,1024]{1,0:T(8,128)(2,1)S(1)} %get-tuple-element.21), channel_id=1, source_target_pairs={{1,0},{2,1},{3,2},{4,3},{5,4},{6,5},{7,6},{8,7},{9,8},{10,9},{11,1... | collective-permute-start | bytes 196616 | tf_op jit(solution)/shard_map/ppermute | solution.py:297
  46.6 3.9 %bias.1 = (bf16[512,1024]{1,0:T(8,128)(2,1)S(1)}, bf16[512,1024]{1,0:T(8,128)(2,1)S(1)}) custom-call(bf16[32,1024,128]{2,1,0:T(8,128)(2,1)S(1)} %copy-done.1, bf16[32,128]{1,0:T(8,128)(2,1)S(1)} %bitcast.5), custom_call_target="tpu_custom_call" | custom-call | flops 268435456 | bytes 10485760 | tf_op jit(solution)/shard_map/bias/pallas_call | solution.py:300
  50.5 1.4 %queries.2.refs_0_ = bf16[544,768]{1,0:T(8,128)(2,1)S(1)} custom-call(bf16[48,768]{1,0:T(8,128)(2,1)S(1)} %get-tuple-element.17.normed_ref, bf16[2,768,2304]{2,1,0:T(8,128)(2,1)S(1)} %bitcast.3, bf16[2,768,2304]{2,1,0:T(8,128)(2,1)S(1)} %bitcast.3), custom_call_target="tpu_custom_call" | custom-call | flops 1000000000 | bytes 5242880 | tf_op jit(solution)/shard_map/queries/pallas_call | solution.py:330
  52.2 3.7 %block.1 = (f32[48,768]{1,0:T(8,128)S(1)}, bf16[48,768]{1,0:T(8,128)(2,1)S(1)}, bf16[32,768]{1,0:T(8,128)(2,1)S(1)}) custom-call(bf16[544,768]{1,0:T(8,128)(2,1)S(1)} %queries.2.refs_0_, bf16[512,768]{1,0:T(8,128)(2,1)S(1)} %constant_dynamic-update-slice_fusion.4.refs_1_, bf16[512,768]{1,0:T(8,128)(2,1)S(1)} %collective-permute-done.8.refs_2_, ...), custom_call_target="tpu_custom_call" | custom-call | tf_op jit(solution)/shard_map/block/pallas_call | solution.py:357
  57.6 1.6 %collective-permute-start.11 = (bf16[32,768]{1,0:T(8,128)(2,1)S(1)}, bf16[32,768]{1,0:T(8,128)(2,1)S(1)}, u32[]{:S(2)}, u32[]{:S(2)}) collective-permute-start(bf16[32,768]{1,0:T(8,128)(2,1)S(1)} %get-tuple-element.24), channel_id=1, source_target_pairs={{0,2},{1,9},{2,0},{3,11},{4,6},{5,13},{6,4},{7,15},{8,10},{9,1},{1... | collective-permute-start | bytes 147464 | tf_op jit(solution)/shard_map/ppermute | solution.py:262
  59.2 2.0 %collective-permute-done.11 = bf16[32,768]{1,0:T(8,128)(2,1)S(1)} collective-permute-done((bf16[32,768]{1,0:T(8,128)(2,1)S(1)}, bf16[32,768]{1,0:T(8,128)(2,1)S(1)}, u32[]{:S(2)}, u32[]{:S(2)}) %collective-permute-start.11) | collective-permute-done | bytes 49184 | tf_op jit(solution)/shard_map/ppermute | solution.py:262
  61.9 2.8 %collective-permute-start.15 = (bf16[128,768]{1,0:T(8,128)(2,1)S(1)}, bf16[128,768]{1,0:T(8,128)(2,1)S(1)}, u32[]{:S(2)}, u32[]{:S(2)}) collective-permute-start(bf16[128,768]{1,0:T(8,128)(2,1)S(1)} %get-tuple-element.32), channel_id=1, source_target_pairs={{0,16},{1,5},{2,18},{3,7},{4,20},{5,1},{6,22},{7,3},{8,24},{9,13},... | collective-permute-start | bytes 589832 | tf_op jit(solution)/shard_map/ppermute | solution.py:262
  65.9 4.1 %collective-permute-done.15 = bf16[128,768]{1,0:T(8,128)(2,1)S(1)} collective-permute-done((bf16[128,768]{1,0:T(8,128)(2,1)S(1)}, bf16[128,768]{1,0:T(8,128)(2,1)S(1)}, u32[]{:S(2)}, u32[]{:S(2)}) %collective-permute-start.15) | collective-permute-done | bytes 196640 | tf_op jit(solution)/shard_map/ppermute | solution.py:262
  70.0 2.3 %collective-permute-done.16 = bf16[128,768]{1,0:T(8,128)(2,1)S(1)} collective-permute-done((bf16[128,768]{1,0:T(8,128)(2,1)S(1)}, bf16[128,768]{1,0:T(8,128)(2,1)S(1)}, u32[]{:S(2)}, u32[]{:S(2)}) %collective-permute-start.16) | collective-permute-done | bytes 196640 | tf_op jit(solution)/shard_map/ppermute | solution.py:262
  72.3 4.5 %collective-permute-start.17 = (bf16[512,768]{1,0:T(8,128)(2,1)S(1)}, bf16[512,768]{1,0:T(8,128)(2,1)S(1)}, u32[]{:S(2)}, u32[]{:S(2)}) collective-permute-start(bf16[512,768]{1,0:T(8,128)(2,1)S(1)} %constant_dynamic-update-slice_fusion.15.refs_1_), channel_id=1, source_target_pairs={{0,1},{1,0},{2,3},{3,2},{4,5},{5,4},{6,7},{7,6},{8,9},{9,8},{10,11... | collective-permute-start | bytes 2359304 | tf_op jit(solution)/shard_map/ppermute | solution.py:264
  76.8 1.4 %queries.3.refs_0_ = bf16[544,768]{1,0:T(8,128)(2,1)S(1)} custom-call(bf16[48,768]{1,0:T(8,128)(2,1)S(1)} %get-tuple-element.23.normed_ref, bf16[2,768,2304]{2,1,0:T(8,128)(2,1)S(1)} %bitcast.3, bf16[2,768,2304]{2,1,0:T(8,128)(2,1)S(1)} %bitcast.3), custom_call_target="tpu_custom_call" | custom-call | flops 1000000000 | bytes 5242880 | tf_op jit(solution)/shard_map/queries/pallas_call | solution.py:330
  78.7 4.4 %block_and_broadcast.1 = (bf16[256,128]{1,0:T(8,128)(2,1)}, bf16[32,768]{1,0:T(8,128)(2,1)}) custom-call(bf16[544,768]{1,0:T(8,128)(2,1)S(1)} %queries.3.refs_0_, bf16[512,768]{1,0:T(8,128)(2,1)S(1)} %constant_dynamic-update-slice_fusion.15.refs_1_, bf16[512,768]{1,0:T(8,128)(2,1)S(1)} %collective-permute-done.17.refs_2_, ...), custom_call_target="tpu_custom_call" | custom-call | tf_op jit(solution)/shard_map/block_and_broadcast/pallas_call | solution.py:367
  (72 shorter events, 10.7 us)
Async XLA Ops:
  0.6 49.8 %slice-start = ((s8[7077888]{0:T(1024)(128)(4,1)}), s8[4194304]{0:T(1024)(128)(4,1)S(1)}, s32[]{:S(2)}) async-start(s8[7077888]{0:T(1024)(128)(4,1)} %bitcast.2), calls=%async_computation | async-start | bytes 8388608
  7.5 10.6 %copy-start.12 = (bf16[128,128]{1,0:T(8,128)(2,1)S(1)}, bf16[128,128]{1,0:T(8,128)(2,1)}, u32[]{:S(2)}) copy-start(bf16[128,128]{1,0:T(8,128)(2,1)} %out_w_ref.1) | copy-start | bytes 98308
  7.5 10.6 %copy-start.14 = (s32[256]{0:T(256)S(1)}, s32[256]{0:T(256)}, u32[]{:S(2)}) copy-start(s32[256]{0:T(256)} %param.14) | copy-start | bytes 3076
  7.5 39.1 %copy-start.1 = (bf16[32,1024,128]{2,1,0:T(8,128)(2,1)S(1)}, bf16[32,1024,128]{2,1,0:T(8,128)(2,1)}, u32[]{:S(2)}) copy-start(bf16[32,1024,128]{2,1,0:T(8,128)(2,1)} %pair_ref.1) | copy-start | bytes 25165828
  7.5 39.1 %copy-start.11 = (bf16[128,32]{0,1:T(8,128)(2,1)S(1)}, bf16[128,32]{0,1:T(8,128)(2,1)}, u32[]{:S(2)}) copy-start(bf16[128,32]{0,1:T(8,128)(2,1)} %param.21) | copy-start | bytes 24580
  7.5 43.0 %slice-start.1 = ((s8[7077888]{0:T(1024)(128)(4,1)}), s8[2883584]{0:T(1024)(128)(4,1)S(1)}, s32[]{:S(2)}) async-start(s8[7077888]{0:T(1024)(128)(4,1)} %bitcast.2), calls=%async_computation.1 | async-start | bytes 5767168
  7.9 6.8 %collective-permute-start = (bf16[160,128]{1,0:T(8,128)(2,1)S(1)}, bf16[160,128]{1,0:T(8,128)(2,1)S(1)}, u32[]{:S(2)}, u32[]{:S(2)}) collective-permute-start(bf16[160,128]{1,0:T(8,128)(2,1)S(1)} %get-tuple-element.15), channel_id=1, source_target_pairs={{0,1},{1,2},{2,3},{3,4},{4,5},{5,6},{6,7},{7,8},{8,9},{9,10},{10,1... | collective-permute-start | bytes 122888 | tf_op jit(solution)/shard_map/ppermute | solution.py:296
  12.7 5.3 %collective-permute-start.1 = (bf16[160,128]{1,0:T(8,128)(2,1)S(1)}, bf16[160,128]{1,0:T(8,128)(2,1)S(1)}, u32[]{:S(2)}, u32[]{:S(2)}) collective-permute-start(bf16[160,128]{1,0:T(8,128)(2,1)S(1)} %get-tuple-element.16), channel_id=1, source_target_pairs={{1,0},{2,1},{3,2},{4,3},{5,4},{6,5},{7,6},{8,7},{9,8},{10,9},{11,1... | collective-permute-start | bytes 122888 | tf_op jit(solution)/shard_map/ppermute | solution.py:295
  21.4 7.2 %collective-permute-start.4 = (bf16[32,768]{1,0:T(8,128)(2,1)S(1)}, bf16[32,768]{1,0:T(8,128)(2,1)S(1)}, u32[]{:S(2)}, u32[]{:S(2)}) collective-permute-start(bf16[32,768]{1,0:T(8,128)(2,1)S(1)} %get-tuple-element.18), channel_id=1, source_target_pairs={{0,6},{1,25},{2,4},{3,27},{4,2},{5,29},{6,0},{7,31},{8,14},{9,17},... | collective-permute-start | bytes 147464 | tf_op jit(solution)/shard_map/ppermute | solution.py:262
  24.0 4.7 %collective-permute-start.3 = (bf16[32,768]{1,0:T(8,128)(2,1)S(1)}, bf16[32,768]{1,0:T(8,128)(2,1)S(1)}, u32[]{:S(2)}, u32[]{:S(2)}) collective-permute-start(bf16[32,768]{1,0:T(8,128)(2,1)S(1)} %get-tuple-element.18), channel_id=1, source_target_pairs={{0,4},{1,17},{2,6},{3,19},{4,0},{5,21},{6,2},{7,23},{8,12},{9,25},... | collective-permute-start | bytes 147464 | tf_op jit(solution)/shard_map/ppermute | solution.py:262
  24.5 3.2 %collective-permute-start.2 = (bf16[32,768]{1,0:T(8,128)(2,1)S(1)}, bf16[32,768]{1,0:T(8,128)(2,1)S(1)}, u32[]{:S(2)}, u32[]{:S(2)}) collective-permute-start(bf16[32,768]{1,0:T(8,128)(2,1)S(1)} %get-tuple-element.18), channel_id=1, source_target_pairs={{0,2},{1,9},{2,0},{3,11},{4,6},{5,13},{6,4},{7,15},{8,10},{9,1},{1... | collective-permute-start | bytes 147464 | tf_op jit(solution)/shard_map/ppermute | solution.py:262
  28.7 4.9 %collective-permute-start.5 = (bf16[128,768]{1,0:T(8,128)(2,1)S(1)}, bf16[128,768]{1,0:T(8,128)(2,1)S(1)}, u32[]{:S(2)}, u32[]{:S(2)}) collective-permute-start(bf16[128,768]{1,0:T(8,128)(2,1)S(1)} %get-tuple-element.40), channel_id=1, source_target_pairs={{0,8},{1,3},{2,10},{3,1},{4,12},{5,7},{6,14},{7,5},{8,0},{9,11},{1... | collective-permute-start | bytes 589832 | tf_op jit(solution)/shard_map/ppermute | solution.py:262
  29.9 8.9 %collective-permute-start.6 = (bf16[128,768]{1,0:T(8,128)(2,1)S(1)}, bf16[128,768]{1,0:T(8,128)(2,1)S(1)}, u32[]{:S(2)}, u32[]{:S(2)}) collective-permute-start(bf16[128,768]{1,0:T(8,128)(2,1)S(1)} %get-tuple-element.40), channel_id=1, source_target_pairs={{0,16},{1,5},{2,18},{3,7},{4,20},{5,1},{6,22},{7,3},{8,24},{9,13},... | collective-permute-start | bytes 589832 | tf_op jit(solution)/shard_map/ppermute | solution.py:262
  33.3 7.6 %collective-permute-start.7 = (bf16[128,768]{1,0:T(8,128)(2,1)S(1)}, bf16[128,768]{1,0:T(8,128)(2,1)S(1)}, u32[]{:S(2)}, u32[]{:S(2)}) collective-permute-start(bf16[128,768]{1,0:T(8,128)(2,1)S(1)} %get-tuple-element.40), channel_id=1, source_target_pairs={{0,24},{1,7},{2,26},{3,5},{4,28},{5,3},{6,30},{7,1},{8,16},{9,15},... | collective-permute-start | bytes 589832 | tf_op jit(solution)/shard_map/ppermute | solution.py:262
  40.9 11.1 %collective-permute-start.8 = (bf16[512,768]{1,0:T(8,128)(2,1)S(1)}, bf16[512,768]{1,0:T(8,128)(2,1)S(1)}, u32[]{:S(2)}, u32[]{:S(2)}) collective-permute-start(bf16[512,768]{1,0:T(8,128)(2,1)S(1)} %constant_dynamic-update-slice_fusion.4.refs_1_), channel_id=1, source_target_pairs={{0,1},{1,0},{2,3},{3,2},{4,5},{5,4},{6,7},{7,6},{8,9},{9,8},{10,11... | collective-permute-start | bytes 2359304 | tf_op jit(solution)/shard_map/ppermute | solution.py:264
  41.6 10.4 %collective-permute-start.9 = (bf16[32,1024]{1,0:T(8,128)(2,1)S(1)}, bf16[32,1024]{1,0:T(8,128)(2,1)S(1)}, u32[]{:S(2)}, u32[]{:S(2)}) collective-permute-start(bf16[32,1024]{1,0:T(8,128)(2,1)S(1)} %get-tuple-element.20), channel_id=1, source_target_pairs={{0,1},{1,2},{2,3},{3,4},{4,5},{5,6},{6,7},{7,8},{8,9},{9,10},{10,1... | collective-permute-start | bytes 196616 | tf_op jit(solution)/shard_map/ppermute | solution.py:298
  44.6 7.4 %collective-permute-start.10 = (bf16[32,1024]{1,0:T(8,128)(2,1)S(1)}, bf16[32,1024]{1,0:T(8,128)(2,1)S(1)}, u32[]{:S(2)}, u32[]{:S(2)}) collective-permute-start(bf16[32,1024]{1,0:T(8,128)(2,1)S(1)} %get-tuple-element.21), channel_id=1, source_target_pairs={{1,0},{2,1},{3,2},{4,3},{5,4},{6,5},{7,6},{8,7},{9,8},{10,9},{11,1... | collective-permute-start | bytes 196616 | tf_op jit(solution)/shard_map/ppermute | solution.py:297
  55.9 5.4 %collective-permute-start.13 = (bf16[32,768]{1,0:T(8,128)(2,1)S(1)}, bf16[32,768]{1,0:T(8,128)(2,1)S(1)}, u32[]{:S(2)}, u32[]{:S(2)}) collective-permute-start(bf16[32,768]{1,0:T(8,128)(2,1)S(1)} %get-tuple-element.24), channel_id=1, source_target_pairs={{0,6},{1,25},{2,4},{3,27},{4,2},{5,29},{6,0},{7,31},{8,14},{9,17},... | collective-permute-start | bytes 147464 | tf_op jit(solution)/shard_map/ppermute | solution.py:262
  56.4 4.8 %collective-permute-start.12 = (bf16[32,768]{1,0:T(8,128)(2,1)S(1)}, bf16[32,768]{1,0:T(8,128)(2,1)S(1)}, u32[]{:S(2)}, u32[]{:S(2)}) collective-permute-start(bf16[32,768]{1,0:T(8,128)(2,1)S(1)} %get-tuple-element.24), channel_id=1, source_target_pairs={{0,4},{1,17},{2,6},{3,19},{4,0},{5,21},{6,2},{7,23},{8,12},{9,25},... | collective-permute-start | bytes 147464 | tf_op jit(solution)/shard_map/ppermute | solution.py:262
  57.6 3.6 %collective-permute-start.11 = (bf16[32,768]{1,0:T(8,128)(2,1)S(1)}, bf16[32,768]{1,0:T(8,128)(2,1)S(1)}, u32[]{:S(2)}, u32[]{:S(2)}) collective-permute-start(bf16[32,768]{1,0:T(8,128)(2,1)S(1)} %get-tuple-element.24), channel_id=1, source_target_pairs={{0,2},{1,9},{2,0},{3,11},{4,6},{5,13},{6,4},{7,15},{8,10},{9,1},{1... | collective-permute-start | bytes 147464 | tf_op jit(solution)/shard_map/ppermute | solution.py:262
  61.3 4.6 %collective-permute-start.14 = (bf16[128,768]{1,0:T(8,128)(2,1)S(1)}, bf16[128,768]{1,0:T(8,128)(2,1)S(1)}, u32[]{:S(2)}, u32[]{:S(2)}) collective-permute-start(bf16[128,768]{1,0:T(8,128)(2,1)S(1)} %get-tuple-element.32), channel_id=1, source_target_pairs={{0,8},{1,3},{2,10},{3,1},{4,12},{5,7},{6,14},{7,5},{8,0},{9,11},{1... | collective-permute-start | bytes 589832 | tf_op jit(solution)/shard_map/ppermute | solution.py:262
  61.9 8.0 %collective-permute-start.15 = (bf16[128,768]{1,0:T(8,128)(2,1)S(1)}, bf16[128,768]{1,0:T(8,128)(2,1)S(1)}, u32[]{:S(2)}, u32[]{:S(2)}) collective-permute-start(bf16[128,768]{1,0:T(8,128)(2,1)S(1)} %get-tuple-element.32), channel_id=1, source_target_pairs={{0,16},{1,5},{2,18},{3,7},{4,20},{5,1},{6,22},{7,3},{8,24},{9,13},... | collective-permute-start | bytes 589832 | tf_op jit(solution)/shard_map/ppermute | solution.py:262
  64.7 7.6 %collective-permute-start.16 = (bf16[128,768]{1,0:T(8,128)(2,1)S(1)}, bf16[128,768]{1,0:T(8,128)(2,1)S(1)}, u32[]{:S(2)}, u32[]{:S(2)}) collective-permute-start(bf16[128,768]{1,0:T(8,128)(2,1)S(1)} %get-tuple-element.32), channel_id=1, source_target_pairs={{0,24},{1,7},{2,26},{3,5},{4,28},{5,3},{6,30},{7,1},{8,16},{9,15},... | collective-permute-start | bytes 589832 | tf_op jit(solution)/shard_map/ppermute | solution.py:262
  72.3 6.4 %collective-permute-start.17 = (bf16[512,768]{1,0:T(8,128)(2,1)S(1)}, bf16[512,768]{1,0:T(8,128)(2,1)S(1)}, u32[]{:S(2)}, u32[]{:S(2)}) collective-permute-start(bf16[512,768]{1,0:T(8,128)(2,1)S(1)} %constant_dynamic-update-slice_fusion.15.refs_1_), channel_id=1, source_target_pairs={{0,1},{1,0},{2,3},{3,2},{4,5},{5,4},{6,7},{7,6},{8,9},{9,8},{10,11... | collective-permute-start | bytes 2359304 | tf_op jit(solution)/shard_map/ppermute | solution.py:264
  (11 other events, 52.8 us)

commit v2 on v1

v2 whole, which is shorter than its diff:
```python
import functools

import jax
import jax.numpy as jnp
from jax import lax
from jax.experimental import pallas as pl
from jax.experimental.pallas import tpu as pltpu
from jax.sharding import PartitionSpec as P

C = 768
H = 16
HEAD = C // H
CA = 128
AH = 4
QW = 32
KW = 128
HALO = 48
EDGE = 16
REACH = EDGE + 64
TOKD = 32
ATOMD = 256
ROWS = 48
QROWS = 34 * H
KEYS = 1024
HALF = 512
CHUNK = 32
INFO = REACH + AH * EDGE
PAIR = INFO + 16
PACK = PAIR + 8 * 32
F32 = jnp.float32
BF16 = jnp.bfloat16

NT = (((1,), (1,)), ((), ()))


def params(mib):
    return pltpu.CompilerParams(vmem_limit_bytes=mib * 1024 * 1024)


VMEM = pl.BlockSpec(memory_space=pltpu.VMEM)


def layer_norm(values):
    average = jnp.mean(values, axis=-1, keepdims=True)
    centred = values - average
    variance = jnp.mean(centred * centred, axis=-1, keepdims=True)
    return centred * lax.rsqrt(variance + 1e-05)


def chunk_starts(tok):
    core, y, x = lax.rem(tok, 2), lax.rem(tok // 2, 4), tok // 8
    starts = []
    for j in range(32):
        slow, fast = (j % 16) // 4, j % 4
        plane = core if j < 16 else 1 - core
        kx = jnp.where(plane == 0, slow, fast)
        ky = jnp.where(plane == 0, fast, slow)
        starts.append((((x ^ kx) * 4 + (y ^ ky)) * 2 + plane) * CHUNK)
    return starts


def ordered(pair_ref, t, starts):
    return jnp.concatenate(
        [pair_ref[t, pl.ds(pl.multiple_of(s, CHUNK), CHUNK), :] for s in starts], axis=0
    )


def pack_kernel(single_hbm, bias_hbm, token_hbm, pair_hbm, pair_w_hbm, down_ref, up_ref,
                single_ref, edge_ref, token_ref, pair_ref, pair_w_ref, sems):
    copies = [
        pltpu.make_async_copy(pair_hbm.at[0], pair_ref.at[0], sems.at[0]),
        pltpu.make_async_copy(pair_hbm.at[TOKD - 1], pair_ref.at[1], sems.at[1]),
        pltpu.make_async_copy(pair_w_hbm, pair_w_ref, sems.at[2]),
        pltpu.make_async_copy(single_hbm.at[pl.ds(0, REACH)], single_ref.at[0], sems.at[3]),
        pltpu.make_async_copy(single_hbm.at[pl.ds(ATOMD - REACH, REACH)], single_ref.at[1], sems.at[4]),
        pltpu.make_async_copy(bias_hbm.at[pl.ds(0, EDGE)], edge_ref.at[0], sems.at[5]),
        pltpu.make_async_copy(bias_hbm.at[pl.ds(ATOMD - EDGE, EDGE)], edge_ref.at[1], sems.at[6]),
        pltpu.make_async_copy(token_hbm, token_ref, sems.at[7]),
    ]
    for copy in copies:
        copy.start()
    tok = lax.axis_index("tok")
    base = tok * TOKD
    orders = [chunk_starts(jnp.maximum(tok - 1, 0)), chunk_starts(jnp.minimum(tok + 1, 31))]
    for copy in copies[3:]:
        copy.wait()
    for side, out_ref in enumerate((down_ref, up_ref)):
        out_ref[:REACH] = single_ref[side]
        for h in range(AH):
            out_ref[REACH + EDGE * h : REACH + EDGE * (h + 1)] = edge_ref[side, :, h * KW : (h + 1) * KW]
        relative = (token_ref[:, side * 128 : (side + 1) * 128] - base).astype(F32)
        out_ref[INFO : INFO + 16] = jnp.broadcast_to(relative, (16, 128)).astype(BF16)
    copies[2].wait()
    weights = pair_w_ref[...]
    for side, out_ref in enumerate((down_ref, up_ref)):
        copies[side].wait()
        rows = ordered(pair_ref, side, orders[side])
        out = lax.dot_general(weights, rows, NT, preferred_element_type=F32).astype(BF16)
        for k in range(8):
            out_ref[PAIR + 32 * k : PAIR + 32 * (k + 1)] = out[:, 128 * k : 128 * (k + 1)]


def bias_kernel(pair_ref, pair_w_ref, bias0_ref, bias1_ref):
    starts = chunk_starts(lax.axis_index("tok"))
    weights = pair_w_ref[...]
    for t in range(TOKD):
        rows = ordered(pair_ref, t, starts)
        out = lax.dot_general(weights, rows, NT, preferred_element_type=F32).astype(BF16)
        bias0_ref[t * H : (t + 1) * H] = out[:H]
        bias1_ref[t * H : (t + 1) * H] = out[H:]


def windowed(proj_ref, k_row, q_row, count, bias, first_atom):
    head_of_lane = lax.broadcasted_iota(jnp.int32, (1, CA), 1) // (CA // AH)
    queries = proj_ref[q_row : q_row + count, :CA]
    keys = proj_ref[k_row : k_row + KW, CA : 2 * CA]
    values = proj_ref[k_row : k_row + KW, 2 * CA :]
    stacked = jnp.concatenate(
        [jnp.where(head_of_lane == h, queries, jnp.zeros_like(queries)) for h in range(AH)], axis=0
    )
    scores = lax.dot_general(stacked, keys, NT, preferred_element_type=F32) * (CA // AH) ** (-0.5)
    scores = scores + jnp.concatenate(bias, axis=0).astype(F32)
    position = first_atom + k_row + lax.broadcasted_iota(jnp.int32, (1, KW), 1)
    inside = (position >= 0) & (position < 32 * ATOMD)
    scores = jnp.where(inside, scores, -1000000000.0)
    powers = jnp.exp(scores - jnp.max(scores, axis=-1, keepdims=True))
    total = jnp.sum(powers, axis=-1, keepdims=True)
    mixed = jnp.dot(powers.astype(BF16), values, preferred_element_type=F32) / total
    merged = jnp.where(head_of_lane == 0, mixed[:count], 0.0)
    for h in range(1, AH):
        merged = jnp.where(head_of_lane == h, mixed[h * count : (h + 1) * count], merged)
    return merged.astype(BF16)


def projected(rows, qkv_ref):
    normed = layer_norm(rows.astype(F32)).astype(BF16)
    return jnp.dot(normed, qkv_ref[...], preferred_element_type=F32).astype(BF16)


def own_bias(bias_ref, w):
    return [bias_ref[QW * w : QW * (w + 1), h * KW : (h + 1) * KW] for h in range(AH)]


def wanted_tokens():
    row = lax.broadcasted_iota(jnp.int32, (ROWS, 1), 0)
    return jnp.where(row < TOKD, row, jnp.where(row == TOKD, -1, jnp.where(row == TOKD + 1, TOKD, -200)))


def hidden_and_sums(hidden_in, mixed, relative, out_w_ref, agg_ref):
    hidden = (
        hidden_in.astype(F32) + jnp.dot(mixed, out_w_ref[...], preferred_element_type=F32)
    ).astype(BF16)
    lifted = jnp.maximum(jnp.dot(hidden, agg_ref[...], preferred_element_type=F32), 0.0)
    member = (relative == wanted_tokens()).astype(F32)
    counts = jnp.sum(member, axis=-1, keepdims=True)
    picker = member.astype(BF16)
    upper = lifted.astype(BF16)
    lower = (lifted - upper.astype(F32)).astype(BF16)
    sums = jnp.dot(picker, upper, preferred_element_type=F32)
    sums = sums + jnp.dot(picker, lower, preferred_element_type=F32)
    return hidden, sums, counts


def inner_atom_kernel(*refs):
    sources, refs = refs[:6], refs[6:]
    single_ref, bias_ref, token_ref, qkv_ref, out_w_ref, agg_ref = refs[:6]
    proj_ref, hidden_ref, sums_ref, counts_ref, mixed_ref, sems = refs[6:]
    copies = [
        pltpu.make_async_copy(source, ref, sems.at[i]) for i, (source, ref) in enumerate(zip(sources, refs))
    ]
    for copy in copies:
        copy.start()
    tok = lax.axis_index("tok")
    for copy in copies:
        copy.wait()
    proj_ref[...] = projected(single_ref[...], qkv_ref)
    for i, w in enumerate((4, 5, 2, 3)):
        mixed_ref[QW * i : QW * (i + 1)] = windowed(
            proj_ref, QW * w - HALO, QW * w, QW, own_bias(bias_ref, w), tok * ATOMD
        )
    lane = lax.broadcasted_iota(jnp.int32, (1, 128), 1)
    relative = jnp.where(lane < 64, token_ref[:, 128:], token_ref[:, :128]) - tok * TOKD
    hidden_in = jnp.concatenate([single_ref[128:192], single_ref[64:128]], axis=0)
    hidden, sums, counts = hidden_and_sums(hidden_in, mixed_ref[...], relative, out_w_ref, agg_ref)
    hidden_ref[:64] = hidden[64:]
    hidden_ref[64:] = hidden[:64]
    sums_ref[...] = sums
    counts_ref[...] = jnp.broadcast_to(counts, counts_ref.shape)


def atom_kernel(single_ref, lower_ref, upper_ref, bias_ref, token_ref, qkv_ref, out_w_ref, agg_ref,
                inner_ref, inner_hidden_ref, inner_sums_ref, inner_counts_ref,
                hidden_ref, stream_ref, normed_ref, own_ref, edge0_ref, edge1_ref, proj_ref, mixed_ref):
    tok = lax.axis_index("tok")
    first_atom = tok * ATOMD - REACH
    beside = projected(jnp.concatenate([lower_ref[:REACH], upper_ref[:REACH]], axis=0), qkv_ref)
    proj_ref[:REACH] = beside[:REACH]
    proj_ref[REACH : REACH + ATOMD] = inner_ref[...]
    proj_ref[REACH + ATOMD :] = beside[REACH:]
    mixed_ref[128 + EDGE : 256 - EDGE] = jnp.zeros((128 - 2 * EDGE, CA), BF16)
    for i, w in enumerate((0, 1, 6, 7)):
        mixed_ref[QW * i : QW * (i + 1)] = windowed(
            proj_ref, 32 + QW * w, REACH + QW * w, QW, own_bias(bias_ref, w), first_atom
        )
    for out_row, q_row, k_row, ref in (
        (128, REACH + ATOMD, 288, upper_ref), (256 - EDGE, REACH - EDGE, 0, lower_ref)
    ):
        bias = [ref[REACH + EDGE * h : REACH + EDGE * (h + 1)] for h in range(AH)]
        mixed_ref[out_row : out_row + EDGE] = windowed(proj_ref, k_row, q_row, EDGE, bias, first_atom)
    hidden_in = jnp.concatenate(
        [
            single_ref[:64],
            single_ref[192:],
            upper_ref[:EDGE],
            jnp.zeros((128 - 2 * EDGE, CA), BF16),
            lower_ref[REACH - EDGE : REACH],
        ],
        axis=0,
    )
    lane = lax.broadcasted_iota(jnp.int32, (1, 128), 1)
    after = upper_ref[INFO : INFO + 16][:1].astype(F32).astype(jnp.int32) + TOKD
    before = lower_ref[INFO : INFO + 16][:1].astype(F32).astype(jnp.int32) - TOKD
    near = jnp.where(lane < EDGE, after, jnp.where(lane >= 128 - EDGE, before, -100))
    outer = jnp.where(lane < 64, token_ref[:, :128], token_ref[:, 128:]) - tok * TOKD
    hidden, sums, counts = hidden_and_sums(
        hidden_in, mixed_ref[...], jnp.concatenate([outer, near], axis=1), out_w_ref, agg_ref
    )
    hidden_ref[:64] = hidden[:64]
    hidden_ref[64:192] = inner_hidden_ref[...]
    hidden_ref[192:] = hidden[64:128]
    stream = (sums + inner_sums_ref[...]) / jnp.maximum(counts + inner_counts_ref[:, :1], 1.0)
    stream_ref[...] = stream
    out = layer_norm(stream).astype(BF16)
    normed_ref[...] = out
    own_ref[...] = out[:TOKD]
    for block, ref in enumerate((edge0_ref, edge1_ref)):
        for side, source in enumerate((lower_ref, upper_ref)):
            for k in range(8):
                first = PAIR + 32 * k + H * block
                ref[H * side : H * (side + 1), 128 * k : 128 * (k + 1)] = source[first : first + H]


def head_mask():
    row = lax.broadcasted_iota(jnp.int32, (QROWS, 1), 0)
    lane = lax.broadcasted_iota(jnp.int32, (1, C), 1)
    start = (row & (H - 1)) * HEAD
    return (lane >= start) & (lane < start + HEAD)


def query_kernel(layer, normed_ref, qkv_ref, out_ref):
    queries = jnp.dot(normed_ref[...], qkv_ref[layer, :, :C], preferred_element_type=F32).astype(BF16)
    row = lax.broadcasted_iota(jnp.int32, (QROWS, ROWS), 0)
    column = lax.broadcasted_iota(jnp.int32, (QROWS, ROWS), 1)
    spread = ((row >> 4) == column).astype(F32).astype(BF16)
    repeated = jnp.dot(spread, queries, preferred_element_type=F32)
    repeated = jnp.where(head_mask(), repeated, 0.0).astype(BF16)
    lifted = lax.dot_general(repeated, qkv_ref[layer, :, C : 2 * C], NT, preferred_element_type=F32)
    out_ref[...] = (lifted * HEAD ** (-0.5)).astype(BF16)


def join_kernel(count, *refs):
    out_ref = refs[-1]
    rows = out_ref.shape[0] // 4
    for i, place in enumerate((0, 1, 3, 2)):
        out_ref[place * rows : (place + 1) * rows] = refs[i][...]


def scored(query_ref, rows_ref, bias_ref, edge_bias_ref, half):
    lanes = slice(half * HALF, (half + 1) * HALF)
    scores = lax.dot_general(query_ref[...], rows_ref[...], NT, preferred_element_type=F32)
    return scores + jnp.concatenate([bias_ref[:, lanes], edge_bias_ref[:, lanes]], axis=0).astype(F32)


def near_kernel(query_ref, near_ref, bias_ref, edge_bias_ref, mixed_ref, maximum_ref, total_ref):
    scores = scored(query_ref, near_ref, bias_ref, edge_bias_ref, 0)
    maximum = jnp.max(scores, axis=-1, keepdims=True)
    powers = jnp.exp(scores - maximum)
    maximum_ref[...] = jnp.broadcast_to(maximum, maximum_ref.shape)
    total_ref[...] = jnp.broadcast_to(jnp.sum(powers, axis=-1, keepdims=True), total_ref.shape)
    mixed_ref[...] = jnp.dot(powers.astype(BF16), near_ref[...], preferred_element_type=F32)


def attend(layer, query_ref, far_ref, bias_ref, edge_bias_ref, mixed_ref, maximum_ref, total_ref,
           qkv_ref, out_w_ref, stream_ref):
    scores = scored(query_ref, far_ref, bias_ref, edge_bias_ref, 1)
    near_maximum = maximum_ref[:, :1]
    maximum = jnp.maximum(near_maximum, jnp.max(scores, axis=-1, keepdims=True))
    powers = jnp.exp(scores - maximum)
    fade = jnp.exp(near_maximum - maximum)
    total = total_ref[:, :1] * fade + jnp.sum(powers, axis=-1, keepdims=True)
    mixed = mixed_ref[...] * fade + jnp.dot(powers.astype(BF16), far_ref[...], preferred_element_type=F32)
    mixed = (mixed / total).astype(BF16)
    valued = jnp.dot(mixed, qkv_ref[layer, :, 2 * C :], preferred_element_type=F32)
    valued = jnp.where(head_mask(), valued, 0.0).astype(BF16)
    row = lax.broadcasted_iota(jnp.int32, (ROWS, QROWS), 0)
    column = lax.broadcasted_iota(jnp.int32, (ROWS, QROWS), 1)
    gather = ((column >> 4) == row).astype(F32).astype(BF16)
    heads = jnp.dot(gather, valued, preferred_element_type=F32).astype(BF16)
    return stream_ref[...] + jnp.dot(heads, out_w_ref[layer], preferred_element_type=F32)


def middle_kernel(*refs):
    stream_ref, normed_ref, own_ref = refs[10:]
    stream = attend(0, *refs[:10])
    stream_ref[...] = stream
    out = layer_norm(stream).astype(BF16)
    normed_ref[...] = out
    own_ref[...] = out[:TOKD]


def last_kernel(*refs):
    bcast_ref, token_ref, hidden_ref, atom_out_ref, token_out_ref = refs[10:]
    token_out = attend(1, *refs[:10]).astype(BF16)
    token_out_ref[...] = token_out[:TOKD]
    carry = jnp.dot(token_out, bcast_ref[...], preferred_element_type=F32).astype(BF16)
    relative = token_ref[...] - lax.axis_index("tok") * TOKD
    member = (relative == wanted_tokens()).astype(F32).astype(BF16)
    picked = lax.dot_general(member, carry, (((0,), (0,)), ((), ())), preferred_element_type=F32)
    atom_out_ref[...] = (hidden_ref[...].astype(F32) + picked).astype(BF16)


def flips(dx, dy, dc):
    pairs = []
    for tok in range(32):
        core, y, x = tok % 2, (tok // 2) % 4, tok // 8
        pairs.append((tok, ((x ^ dx) * 4 + (y ^ dy)) * 2 + (core ^ dc)))
    return pairs


def crossed(k, first):
    along_y, along_x = flips(0, k, 0), flips(k, 0, 0)
    return [
        (along_y if (tok % 2 == 0) == first else along_x)[tok] for tok in range(32)
    ]


def join(pieces, after):
    return pl.pallas_call(
        functools.partial(join_kernel, len(after)),
        in_specs=[VMEM] * 4 + [pl.BlockSpec(memory_space=pl.ANY)] * len(after),
        out_specs=VMEM,
        out_shape=shape(4 * pieces[0].shape[0], C),
        compiler_params=params(4),
        name="join",
    )(*pieces, *after)


def exchange(rows, first):
    return [rows] + [lax.ppermute(rows, "tok", crossed(k, first)) for k in (1, 3, 2)]


def in_hbm(*arrays):
    return [pltpu.with_memory_space_constraint(x, pltpu.HBM) for x in arrays]


def shape(rows, columns, dtype=BF16):
    return jax.ShapeDtypeStruct((rows, columns), dtype)


def local(atom_single, atom_bias, atom_token, atom_counts, pair_rep, atom_qkv_w, atom_out_w, agg_w,
          tok_qkv_w, tok_out_w, pair_w, bcast_w):
    tokens = atom_token.reshape(1, ATOMD)
    pair_wt = pair_w.T
    hbm = pl.BlockSpec(memory_space=pltpu.HBM)

    to_down, to_up = pl.pallas_call(
        pack_kernel,
        in_specs=[hbm] * 5,
        out_specs=[VMEM] * 2,
        out_shape=[shape(PACK, CA)] * 2,
        scratch_shapes=[
            pltpu.VMEM((2, REACH, CA), BF16),
            pltpu.VMEM((2, EDGE, AH * KW), BF16),
            pltpu.VMEM((1, ATOMD), jnp.int32),
            pltpu.VMEM((2, KEYS, 128), BF16),
            pltpu.VMEM((32, 128), BF16),
            pltpu.SemaphoreType.DMA((8,)),
        ],
        compiler_params=params(8),
        name="pack",
    )(*in_hbm(atom_single, atom_bias, tokens, pair_rep, pair_wt))
    from_upper = lax.ppermute(to_down, "tok", [((i + 1) % 32, i) for i in range(32)])
    from_lower = lax.ppermute(to_up, "tok", [(i, (i + 1) % 32) for i in range(32)])

    bias = pl.pallas_call(
        bias_kernel,
        in_specs=[VMEM] * 2,
        out_specs=[VMEM] * 2,
        out_shape=[shape(TOKD * H, KEYS)] * 2,
        compiler_params=params(12),
        cost_estimate=pl.CostEstimate(flops=2 * 32 * 1024 * 128 * 32, bytes_accessed=10 * 2**20, transcendentals=0),
        name="bias",
    )(pair_rep, pair_wt)

    small = (atom_single, atom_bias, tokens, atom_qkv_w, atom_out_w, agg_w)
    inner = pl.pallas_call(
        inner_atom_kernel,
        in_specs=[hbm] * 6,
        out_specs=[VMEM] * 10,
        out_shape=[jax.ShapeDtypeStruct(x.shape, x.dtype) for x in small]
        + [
            shape(ATOMD, 3 * CA),
            shape(4 * QW, CA),
            shape(ROWS, C, F32),
            shape(ROWS, 128, F32),
        ],
        scratch_shapes=[pltpu.VMEM((4 * QW, CA), BF16), pltpu.SemaphoreType.DMA((6,))],
        compiler_params=params(8),
        cost_estimate=pl.CostEstimate(flops=10**9, bytes_accessed=5 * 2**20, transcendentals=0),
        name="inner_atoms",
    )(*in_hbm(*small))
    single, *rest = inner
    hidden, stream, normed, own, *edge_bias = pl.pallas_call(
        atom_kernel,
        in_specs=[VMEM] * 12,
        out_specs=[VMEM] * 6,
        out_shape=[shape(ATOMD, CA), shape(ROWS, C, F32), shape(ROWS, C), shape(TOKD, C)] + [shape(2 * H, KEYS)] * 2,
        scratch_shapes=[pltpu.VMEM((2 * REACH + ATOMD, 3 * CA), BF16), pltpu.VMEM((256, CA), BF16)],
        compiler_params=params(8),
        name="atoms",
    )(single, from_lower, from_upper, *rest)

    for layer in range(2):
        pieces = exchange(own, True)
        queries = pl.pallas_call(
            functools.partial(query_kernel, layer),
            in_specs=[VMEM] * 2,
            out_specs=VMEM,
            out_shape=shape(QROWS, C),
            compiler_params=params(16),
            cost_estimate=pl.CostEstimate(flops=10**9, bytes_accessed=5 * 2**20, transcendentals=0),
            name="queries",
        )(normed, tok_qkv_w)
        pieces = exchange(join(pieces, [queries]), False)
        near = join(pieces, [bias[0]] if layer == 0 else [])
        far = lax.ppermute(near, "tok", flips(0, 0, 1))
        partial = pl.pallas_call(
            near_kernel,
            in_specs=[VMEM] * 4,
            out_specs=[VMEM] * 3,
            out_shape=[shape(QROWS, C, F32)] + [shape(QROWS, 128, F32)] * 2,
            compiler_params=params(16),
            cost_estimate=pl.CostEstimate(flops=2 * 10**9, bytes_accessed=5 * 2**20, transcendentals=300000),
            name="near",
        )(queries, near, bias[layer], edge_bias[layer])
        operands = (queries, far, bias[layer], edge_bias[layer], *partial, tok_qkv_w, tok_out_w, stream)
        if layer == 0:
            stream, normed, own = pl.pallas_call(
                middle_kernel,
                in_specs=[VMEM] * 10,
                out_specs=[VMEM] * 3,
                out_shape=[shape(ROWS, C, F32), shape(ROWS, C), shape(TOKD, C)],
                compiler_params=params(16),
                name="block",
            )(*operands)
        else:
            atom_out, token_out = pl.pallas_call(
                last_kernel,
                in_specs=[VMEM] * 13,
                out_specs=[VMEM] * 2,
                out_shape=[shape(ATOMD, CA), shape(TOKD, C)],
                compiler_params=params(16),
                name="block_and_broadcast",
            )(*operands, bcast_w, rest[1], hidden)
    return (atom_out, token_out)


def solution(mesh):
    placed = (
        P(("seed", "tok"), None),
        P("tok", None),
        P("tok"),
        P("tok"),
        P("tok", None, None),
        P(),
        P(),
        P(),
        P(),
        P(),
        P(),
        P(),
    )
    return jax.shard_map(
        local,
        mesh=mesh,
        in_specs=placed,
        out_specs=(P(("seed", "tok"), None), P(("seed", "tok"), None)),
        check_vma=False,
    )
```

time: 83.4 us -> 58.9 us (0.71)
  starting transfers between devices: 32.1 us -> 20.5 us
  waiting for transfers between devices: 24.3 us -> 15 us
  local copies, waits for them, and re-layouts: 7.16 us -> 0.03 us
  Pallas kernels: 18.6 us -> 22.4 us
    ppermute x18 -> x16, starting transfers between devices: 32.1 us -> 20.5 us  [the longest x12 13.7 us: exchange(): lax.ppermute(rows, 'tok', crossed(k, first))]
    ppermute x18 -> x16, waiting for transfers between devices: 24.3 us -> 15 us  [the longest x12 12.5 us: exchange(): lax.ppermute(rows, 'tok', crossed(k, first))]
    unnamed x44 -> x14, local copies, waits for them, and re-layouts: 7.1 us -> 0.03 us
    pallas_call x7 -> x14, Pallas kernels: 18.6 us -> 22.4 us  [the longest x1 3.82 us: local(): pl.pallas_call(last_kernel, in_specs=[VMEM] * 13, out_specs=[VMEM] * 2, o...]
  transfers between devices with their start and end apart: 18 -> 16, of which waited for: 11 -> 10; matrix products, arithmetic and copies ran while one was open for 0% -> 0% of each run, Pallas kernels for 8% -> 19%
where the time goes in v2:
time: 58.9 us; the launch traced here: 58.7 us
  Pallas kernels  22.4 us (38%)
  starting transfers between devices  20.5 us (35%)
  waiting for transfers between devices  15 us (25%)
  between operations  0.8 us (1%)
    ppermute x12, starting transfers between devices, exchange(): lax.ppermute(rows, 'tok', crossed(k, first))  13.7 us
    ppermute x12, waiting for transfers between devices, exchange(): lax.ppermute(rows, 'tok', crossed(k, first))  12.5 us
    ppermute x2, starting transfers between devices, local(): far = lax.ppermute(near, 'tok', flips(0, 0, 1))  3.96 us
    pallas_call x1, Pallas kernels, local(): pl.pallas_call(last_kernel, in_specs=[VMEM] * 13, out_specs=[VMEM] * 2, o...  3.82 us
    pallas_call x1, Pallas kernels, local(): pl.pallas_call(middle_kernel, in_specs=[VMEM] * 10, out_specs=[VMEM] * 3,...  3.1 us
    pallas_call x2, Pallas kernels, local(): pl.pallas_call(near_kernel, in_specs=[VMEM] * 4, out_specs=[VMEM] * 3, ou...  2.95 us
    pallas_call x2, Pallas kernels, local(): pl.pallas_call(functools.partial(query_kernel, layer), in_specs=[VMEM] *...  2.84 us
    pallas_call x1, Pallas kernels, local(): pl.pallas_call(inner_atom_kernel, in_specs=[hbm] * 6, out_specs=[VMEM] *...  2.77 us
  transfers between devices with their start and end apart: 16, of which 10 were waited for; matrix products, arithmetic and copies ran while one was open for 0% of the time, Pallas kernels for 19%

profile of v2, /device:TPU:1, one launch (start us, length us, event | category | flops | bytes accessed | tf_op | source)
XLA Modules:
  0.0 58.7 jit_solution(7885556195635485010)
XLA Ops:
  0.7 1.6 %pack.1 = (bf16[416,128]{1,0:T(8,128)(2,1)S(1)}, bf16[416,128]{1,0:T(8,128)(2,1)S(1)}) custom-call(bf16[256,128]{1,0:T(8,128)(2,1)} %single_hbm.1, bf16[256,512]{1,0:T(8,128)(2,1)} %bias_hbm.1, s32[1,256]{1,0:T(1,128)} %bitcast.8, bf16[32,1024,128]{2,1,0:T(8,128)(2,1)} %pair_ref.1, bf16[32,128]{1,0:T(8,128)(2,1)} %bitcast.6), custom_call_target="tpu_custom_call" | custom-call | tf_op jit(solution)/shard_map/pack/pallas_call | solution.py:366
  2.2 2.8 %collective-permute-start = (bf16[416,128]{1,0:T(8,128)(2,1)S(1)}, bf16[416,128]{1,0:T(8,128)(2,1)S(1)}, u32[]{:S(2)}, u32[]{:S(2)}) collective-permute-start(bf16[416,128]{1,0:T(8,128)(2,1)S(1)} %get-tuple-element.32), channel_id=1, source_target_pairs={{0,1},{1,2},{2,3},{3,4},{4,5},{5,6},{6,7},{7,8},{8,9},{9,10},{10,1... | collective-permute-start | bytes 319496 | tf_op jit(solution)/shard_map/ppermute | solution.py:383
  5.0 2.8 %inner_atoms.1 = (bf16[256,128]{1,0:T(8,128)(2,1)S(1)}, bf16[256,512]{1,0:T(8,128)(2,1)S(1)}, s32[1,256]{1,0:T(1,128)S(1)}, bf16[128,384]{1,0:T(8,128)(2,1)S(1)}...) custom-call(bf16[256,128]{1,0:T(8,128)(2,1)} %single_hbm.1, ...), custom_call_target="tpu_custom_call" | custom-call | flops 1000000000 | bytes 5242880 | tf_op jit(solution)/shard_map/inner_atoms/pallas_call | solution.py:396
  7.8 1.6 %collective-permute-done.1.upper_ref = bf16[416,128]{1,0:T(8,128)(2,1)S(1)} collective-permute-done((bf16[416,128]{1,0:T(8,128)(2,1)S(1)}, bf16[416,128]{1,0:T(8,128)(2,1)S(1)}, u32[]{:S(2)}, u32[]{:S(2)}) %collective-permute-start.1) | collective-permute-done | bytes 106528 | tf_op jit(solution)/shard_map/ppermute | solution.py:382
  9.4 2.6 %atoms.1 = (bf16[256,128]{1,0:T(8,128)(2,1)S(1)}, f32[48,768]{1,0:T(8,128)S(1)}, bf16[48,768]{1,0:T(8,128)(2,1)S(1)}, bf16[32,768]{1,0:T(8,128)(2,1)S(1)}, bf16[...) custom-call(bf16[256,128]{1,0:T(8,128)(2,1)S(1)} %get-tuple-element.31.single_ref, ...), custom_call_target="tpu_custom_call" | custom-call | tf_op jit(solution)/shard_map/atoms/pallas_call | solution.py:413
  12.0 2.8 %collective-permute-start.4 = (bf16[32,768]{1,0:T(8,128)(2,1)S(1)}, bf16[32,768]{1,0:T(8,128)(2,1)S(1)}, u32[]{:S(2)}, u32[]{:S(2)}) collective-permute-start(bf16[32,768]{1,0:T(8,128)(2,1)S(1)} %get-tuple-element.44.refs_0_), channel_id=1, source_target_pairs={{0,4},{1,17},{2,6},{3,19},{4,0},{5,21},{6,2},{7,23},{8,12},{9,25},... | collective-permute-start | bytes 147464 | tf_op jit(solution)/shard_map/ppermute | solution.py:349
  15.7 1.4 %queries.2.refs_4_.query_ref.refs_0_ = bf16[544,768]{1,0:T(8,128)(2,1)S(1)} custom-call(bf16[48,768]{1,0:T(8,128)(2,1)S(1)} %get-tuple-element.43.normed_ref, bf16[2,768,2304]{2,1,0:T(8,128)(2,1)S(1)} %bitcast.3), custom_call_target="tpu_custom_call" | custom-call | flops 1000000000 | bytes 5242880 | tf_op jit(solution)/shard_map/queries/pallas_call | solution.py:425
  17.2 2.1 %collective-permute-done.3.refs_2_ = bf16[32,768]{1,0:T(8,128)(2,1)S(1)} collective-permute-done((bf16[32,768]{1,0:T(8,128)(2,1)S(1)}, bf16[32,768]{1,0:T(8,128)(2,1)S(1)}, u32[]{:S(2)}, u32[]{:S(2)}) %collective-permute-start.3) | collective-permute-done | bytes 49184 | tf_op jit(solution)/shard_map/ppermute | solution.py:349
  19.3 2.1 %collective-permute-start.7 = (bf16[128,768]{1,0:T(8,128)(2,1)S(1)}, bf16[128,768]{1,0:T(8,128)(2,1)S(1)}, u32[]{:S(2)}, u32[]{:S(2)}) collective-permute-start(bf16[128,768]{1,0:T(8,128)(2,1)S(1)} %join.4.refs_0_), channel_id=1, source_target_pairs={{0,16},{1,5},{2,18},{3,7},{4,20},{5,1},{6,22},{7,3},{8,24},{9,13},... | collective-permute-start | bytes 589832 | tf_op jit(solution)/shard_map/ppermute | solution.py:349
  21.4 1.6 %collective-permute-start.6 = (bf16[128,768]{1,0:T(8,128)(2,1)S(1)}, bf16[128,768]{1,0:T(8,128)(2,1)S(1)}, u32[]{:S(2)}, u32[]{:S(2)}) collective-permute-start(bf16[128,768]{1,0:T(8,128)(2,1)S(1)} %join.4.refs_0_), channel_id=1, source_target_pairs={{0,24},{1,7},{2,26},{3,5},{4,28},{5,3},{6,30},{7,1},{8,16},{9,15},... | collective-permute-start | bytes 589832 | tf_op jit(solution)/shard_map/ppermute | solution.py:349
  23.5 2.6 %bias.1 = (bf16[512,1024]{1,0:T(8,128)(2,1)S(1)}, bf16[512,1024]{1,0:T(8,128)(2,1)S(1)}) custom-call(bf16[32,1024,128]{2,1,0:T(8,128)(2,1)S(1)} %bitcast.5, bf16[32,128]{1,0:T(8,128)(2,1)S(1)} %bitcast.7), custom_call_target="tpu_custom_call" | custom-call | flops 268435456 | bytes 10485760 | tf_op jit(solution)/shard_map/bias/pallas_call | solution.py:385
  26.2 1.6 %collective-permute-done.6.refs_2_ = bf16[128,768]{1,0:T(8,128)(2,1)S(1)} collective-permute-done((bf16[128,768]{1,0:T(8,128)(2,1)S(1)}, bf16[128,768]{1,0:T(8,128)(2,1)S(1)}, u32[]{:S(2)}, u32[]{:S(2)}) %collective-permute-start.6) | collective-permute-done | bytes 196640 | tf_op jit(solution)/shard_map/ppermute | solution.py:349
  29.1 1.3 %collective-permute-start.8 = (bf16[512,768]{1,0:T(8,128)(2,1)S(1)}, bf16[512,768]{1,0:T(8,128)(2,1)S(1)}, u32[]{:S(2)}, u32[]{:S(2)}) collective-permute-start(bf16[512,768]{1,0:T(8,128)(2,1)S(1)} %join.5.near_ref), channel_id=1, source_target_pairs={{0,1},{1,0},{2,3},{3,2},{4,5},{5,4},{6,7},{7,6},{8,9},{9,8},{10,11... | collective-permute-start | bytes 2359304 | tf_op jit(solution)/shard_map/ppermute | solution.py:436
  30.3 1.5 %near.2 = (f32[544,768]{1,0:T(8,128)S(1)}, f32[544,128]{1,0:T(8,128)S(1)}, f32[544,128]{1,0:T(8,128)S(1)}) custom-call(bf16[544,768]{1,0:T(8,128)(2,1)S(1)} %queries.2.refs_4_.query_ref.refs_0_, bf16[512,768]{1,0:T(8,128)(2,1)S(1)} %join.5.near_ref, bf16[512,1024]{1,0:T(8,128)(2,1)S(1)} %get-tuple-element.45.refs_4_.bias_ref.refs_2_, ...), custom_call_target="tpu_custom_call" | custom-call | flops 2000000000 | bytes 5242880 | tf_op jit(solution)/shard_map/near/pallas_call | solution.py:437
  32.2 3.1 %block.1 = (f32[48,768]{1,0:T(8,128)S(1)}, bf16[48,768]{1,0:T(8,128)(2,1)S(1)}, bf16[32,768]{1,0:T(8,128)(2,1)S(1)}) custom-call(bf16[544,768]{1,0:T(8,128)(2,1)S(1)} %queries.2.refs_4_.query_ref.refs_0_, bf16[512,768]{1,0:T(8,128)(2,1)S(1)} %collective-permute-done.8.refs_1_, bf16[512,1024]{1,0:T(8,128)(2,1)S(1)} %get-tuple-element.45.refs_4_.bias_ref.refs_2_, ...), custom_call_target="tpu_custom_call" | custom-call | tf_op jit(solution)/shard_map/block/pallas_call | solution.py:448
  35.4 1.3 %collective-permute-start.11 = (bf16[32,768]{1,0:T(8,128)(2,1)S(1)}, bf16[32,768]{1,0:T(8,128)(2,1)S(1)}, u32[]{:S(2)}, u32[]{:S(2)}) collective-permute-start(bf16[32,768]{1,0:T(8,128)(2,1)S(1)} %get-tuple-element.52.refs_0_), channel_id=1, source_target_pairs={{0,4},{1,17},{2,6},{3,19},{4,0},{5,21},{6,2},{7,23},{8,12},{9,25},... | collective-permute-start | bytes 147464 | tf_op jit(solution)/shard_map/ppermute | solution.py:349
  36.7 1.8 %collective-permute-start.10 = (bf16[32,768]{1,0:T(8,128)(2,1)S(1)}, bf16[32,768]{1,0:T(8,128)(2,1)S(1)}, u32[]{:S(2)}, u32[]{:S(2)}) collective-permute-start(bf16[32,768]{1,0:T(8,128)(2,1)S(1)} %get-tuple-element.52.refs_0_), channel_id=1, source_target_pairs={{0,6},{1,25},{2,4},{3,27},{4,2},{5,29},{6,0},{7,31},{8,14},{9,17},... | collective-permute-start | bytes 147464 | tf_op jit(solution)/shard_map/ppermute | solution.py:349
  38.5 1.4 %queries.3.refs_4_.query_ref.refs_0_ = bf16[544,768]{1,0:T(8,128)(2,1)S(1)} custom-call(bf16[48,768]{1,0:T(8,128)(2,1)S(1)} %get-tuple-element.51.normed_ref, bf16[2,768,2304]{2,1,0:T(8,128)(2,1)S(1)} %bitcast.3), custom_call_target="tpu_custom_call" | custom-call | flops 1000000000 | bytes 5242880 | tf_op jit(solution)/shard_map/queries/pallas_call | solution.py:425
  42.9 1.5 %collective-permute-start.13 = (bf16[128,768]{1,0:T(8,128)(2,1)S(1)}, bf16[128,768]{1,0:T(8,128)(2,1)S(1)}, u32[]{:S(2)}, u32[]{:S(2)}) collective-permute-start(bf16[128,768]{1,0:T(8,128)(2,1)S(1)} %join.6.refs_0_), channel_id=1, source_target_pairs={{0,24},{1,7},{2,26},{3,5},{4,28},{5,3},{6,30},{7,1},{8,16},{9,15},... | collective-permute-start | bytes 589832 | tf_op jit(solution)/shard_map/ppermute | solution.py:349
  44.5 3.5 %collective-permute-done.14.refs_3_ = bf16[128,768]{1,0:T(8,128)(2,1)S(1)} collective-permute-done((bf16[128,768]{1,0:T(8,128)(2,1)S(1)}, bf16[128,768]{1,0:T(8,128)(2,1)S(1)}, u32[]{:S(2)}, u32[]{:S(2)}) %collective-permute-start.14) | collective-permute-done | bytes 196640 | tf_op jit(solution)/shard_map/ppermute | solution.py:349
  47.9 2.3 %collective-permute-done.13.refs_2_ = bf16[128,768]{1,0:T(8,128)(2,1)S(1)} collective-permute-done((bf16[128,768]{1,0:T(8,128)(2,1)S(1)}, bf16[128,768]{1,0:T(8,128)(2,1)S(1)}, u32[]{:S(2)}, u32[]{:S(2)}) %collective-permute-start.13) | collective-permute-done | bytes 196640 | tf_op jit(solution)/shard_map/ppermute | solution.py:349
  50.3 2.7 %collective-permute-start.15 = (bf16[512,768]{1,0:T(8,128)(2,1)S(1)}, bf16[512,768]{1,0:T(8,128)(2,1)S(1)}, u32[]{:S(2)}, u32[]{:S(2)}) collective-permute-start(bf16[512,768]{1,0:T(8,128)(2,1)S(1)} %join.7.near_ref), channel_id=1, source_target_pairs={{0,1},{1,0},{2,3},{3,2},{4,5},{5,4},{6,7},{7,6},{8,9},{9,8},{10,11... | collective-permute-start | bytes 2359304 | tf_op jit(solution)/shard_map/ppermute | solution.py:436
  53.0 1.5 %near.3 = (f32[544,768]{1,0:T(8,128)S(1)}, f32[544,128]{1,0:T(8,128)S(1)}, f32[544,128]{1,0:T(8,128)S(1)}) custom-call(bf16[544,768]{1,0:T(8,128)(2,1)S(1)} %queries.3.refs_4_.query_ref.refs_0_, bf16[512,768]{1,0:T(8,128)(2,1)S(1)} %join.7.near_ref, bf16[512,1024]{1,0:T(8,128)(2,1)S(1)} %get-tuple-element.53.bias_ref.refs_2_, ...), custom_call_target="tpu_custom_call" | custom-call | flops 2000000000 | bytes 5242880 | tf_op jit(solution)/shard_map/near/pallas_call | solution.py:437
  54.9 3.8 %block_and_broadcast.1 = (bf16[256,128]{1,0:T(8,128)(2,1)}, bf16[32,768]{1,0:T(8,128)(2,1)}) custom-call(bf16[544,768]{1,0:T(8,128)(2,1)S(1)} %queries.3.refs_4_.query_ref.refs_0_, bf16[512,768]{1,0:T(8,128)(2,1)S(1)} %collective-permute-done.15.refs_1_, bf16[512,1024]{1,0:T(8,128)(2,1)S(1)} %get-tuple-element.53.bias_ref.refs_2_, ...), custom_call_target="tpu_custom_call" | custom-call | tf_op jit(solution)/shard_map/block_and_broadcast/pallas_call | solution.py:457
  (38 shorter events, 6.7 us)
Async XLA Ops:
  0.6 15.1 %slice-start = ((s8[7077888]{0:T(1024)(128)(4,1)}), s8[4194304]{0:T(1024)(128)(4,1)S(1)}, s32[]{:S(2)}) async-start(s8[7077888]{0:T(1024)(128)(4,1)} %bitcast.2), calls=%async_computation | async-start | bytes 8388608
  0.6 15.1 %slice-start.1 = ((s8[7077888]{0:T(1024)(128)(4,1)}), s8[2883584]{0:T(1024)(128)(4,1)S(1)}, s32[]{:S(2)}) async-start(s8[7077888]{0:T(1024)(128)(4,1)} %bitcast.2), calls=%async_computation.1 | async-start | bytes 5767168
  0.7 22.9 %slice-start.2 = ((s8[8388608]{0:T(1024)(128)(4,1)}), s8[4194304]{0:T(1024)(128)(4,1)S(1)}, s32[]{:S(2)}) async-start(s8[8388608]{0:T(1024)(128)(4,1)} %bitcast.4), calls=%async_computation.2 | async-start | bytes 8388608
  2.2 5.5 %collective-permute-start = (bf16[416,128]{1,0:T(8,128)(2,1)S(1)}, bf16[416,128]{1,0:T(8,128)(2,1)S(1)}, u32[]{:S(2)}, u32[]{:S(2)}) collective-permute-start(bf16[416,128]{1,0:T(8,128)(2,1)S(1)} %get-tuple-element.32), channel_id=1, source_target_pairs={{0,1},{1,2},{2,3},{3,4},{4,5},{5,6},{6,7},{7,8},{8,9},{9,10},{10,1... | collective-permute-start | bytes 319496 | tf_op jit(solution)/shard_map/ppermute | solution.py:383
  5.0 18.5 %slice-start.3 = ((s8[8388608]{0:T(1024)(128)(4,1)}), s8[4194304]{0:T(1024)(128)(4,1)S(1)}, s32[]{:S(2)}) async-start(s8[8388608]{0:T(1024)(128)(4,1)} %bitcast.4), calls=%async_computation.3 | async-start | bytes 8388608
  5.0 4.4 %collective-permute-start.1 = (bf16[416,128]{1,0:T(8,128)(2,1)S(1)}, bf16[416,128]{1,0:T(8,128)(2,1)S(1)}, u32[]{:S(2)}, u32[]{:S(2)}) collective-permute-start(bf16[416,128]{1,0:T(8,128)(2,1)S(1)} %get-tuple-element.33), channel_id=1, source_target_pairs={{1,0},{2,1},{3,2},{4,3},{5,4},{6,5},{7,6},{8,7},{9,8},{10,9},{11,1... | collective-permute-start | bytes 319496 | tf_op jit(solution)/shard_map/ppermute | solution.py:382
  12.0 5.1 %collective-permute-start.4 = (bf16[32,768]{1,0:T(8,128)(2,1)S(1)}, bf16[32,768]{1,0:T(8,128)(2,1)S(1)}, u32[]{:S(2)}, u32[]{:S(2)}) collective-permute-start(bf16[32,768]{1,0:T(8,128)(2,1)S(1)} %get-tuple-element.44.refs_0_), channel_id=1, source_target_pairs={{0,4},{1,17},{2,6},{3,19},{4,0},{5,21},{6,2},{7,23},{8,12},{9,25},... | collective-permute-start | bytes 147464 | tf_op jit(solution)/shard_map/ppermute | solution.py:349
  14.9 4.4 %collective-permute-start.3 = (bf16[32,768]{1,0:T(8,128)(2,1)S(1)}, bf16[32,768]{1,0:T(8,128)(2,1)S(1)}, u32[]{:S(2)}, u32[]{:S(2)}) collective-permute-start(bf16[32,768]{1,0:T(8,128)(2,1)S(1)} %get-tuple-element.44.refs_0_), channel_id=1, source_target_pairs={{0,6},{1,25},{2,4},{3,27},{4,2},{5,29},{6,0},{7,31},{8,14},{9,17},... | collective-permute-start | bytes 147464 | tf_op jit(solution)/shard_map/ppermute | solution.py:349
  15.7 3.6 %collective-permute-start.2 = (bf16[32,768]{1,0:T(8,128)(2,1)S(1)}, bf16[32,768]{1,0:T(8,128)(2,1)S(1)}, u32[]{:S(2)}, u32[]{:S(2)}) collective-permute-start(bf16[32,768]{1,0:T(8,128)(2,1)S(1)} %get-tuple-element.44.refs_0_), channel_id=1, source_target_pairs={{0,2},{1,9},{2,0},{3,11},{4,6},{5,13},{6,4},{7,15},{8,10},{9,1},{1... | collective-permute-start | bytes 147464 | tf_op jit(solution)/shard_map/ppermute | solution.py:349
  15.7 7.8 %copy-start.2 = (bf16[128,32]{0,1:T(8,128)(2,1)S(1)}, bf16[128,32]{0,1:T(8,128)(2,1)}, u32[]{:S(2)}) copy-start(bf16[128,32]{0,1:T(8,128)(2,1)} %param.21) | copy-start | bytes 24580
  19.3 6.9 %collective-permute-start.7 = (bf16[128,768]{1,0:T(8,128)(2,1)S(1)}, bf16[128,768]{1,0:T(8,128)(2,1)S(1)}, u32[]{:S(2)}, u32[]{:S(2)}) collective-permute-start(bf16[128,768]{1,0:T(8,128)(2,1)S(1)} %join.4.refs_0_), channel_id=1, source_target_pairs={{0,16},{1,5},{2,18},{3,7},{4,20},{5,1},{6,22},{7,3},{8,24},{9,13},... | collective-permute-start | bytes 589832 | tf_op jit(solution)/shard_map/ppermute | solution.py:349
  21.4 6.4 %collective-permute-start.6 = (bf16[128,768]{1,0:T(8,128)(2,1)S(1)}, bf16[128,768]{1,0:T(8,128)(2,1)S(1)}, u32[]{:S(2)}, u32[]{:S(2)}) collective-permute-start(bf16[128,768]{1,0:T(8,128)(2,1)S(1)} %join.4.refs_0_), channel_id=1, source_target_pairs={{0,24},{1,7},{2,26},{3,5},{4,28},{5,3},{6,30},{7,1},{8,16},{9,15},... | collective-permute-start | bytes 589832 | tf_op jit(solution)/shard_map/ppermute | solution.py:349
  23.0 6.0 %collective-permute-start.5 = (bf16[128,768]{1,0:T(8,128)(2,1)S(1)}, bf16[128,768]{1,0:T(8,128)(2,1)S(1)}, u32[]{:S(2)}, u32[]{:S(2)}) collective-permute-start(bf16[128,768]{1,0:T(8,128)(2,1)S(1)} %join.4.refs_0_), channel_id=1, source_target_pairs={{0,8},{1,3},{2,10},{3,1},{4,12},{5,7},{6,14},{7,5},{8,0},{9,11},{1... | collective-permute-start | bytes 589832 | tf_op jit(solution)/shard_map/ppermute | solution.py:349
  29.1 3.2 %collective-permute-start.8 = (bf16[512,768]{1,0:T(8,128)(2,1)S(1)}, bf16[512,768]{1,0:T(8,128)(2,1)S(1)}, u32[]{:S(2)}, u32[]{:S(2)}) collective-permute-start(bf16[512,768]{1,0:T(8,128)(2,1)S(1)} %join.5.near_ref), channel_id=1, source_target_pairs={{0,1},{1,0},{2,3},{3,2},{4,5},{5,4},{6,7},{7,6},{8,9},{9,8},{10,11... | collective-permute-start | bytes 2359304 | tf_op jit(solution)/shard_map/ppermute | solution.py:436
  30.3 1.9 %copy-start = (bf16[2,768,768]{2,1,0:T(8,128)(2,1)S(1)}, bf16[2,768,768]{2,1,0:T(8,128)(2,1)}, u32[]{:S(2)}) copy-start(bf16[2,768,768]{2,1,0:T(8,128)(2,1)} %refs_8_.3) | copy-start | bytes 7077892
  35.4 4.6 %collective-permute-start.11 = (bf16[32,768]{1,0:T(8,128)(2,1)S(1)}, bf16[32,768]{1,0:T(8,128)(2,1)S(1)}, u32[]{:S(2)}, u32[]{:S(2)}) collective-permute-start(bf16[32,768]{1,0:T(8,128)(2,1)S(1)} %get-tuple-element.52.refs_0_), channel_id=1, source_target_pairs={{0,4},{1,17},{2,6},{3,19},{4,0},{5,21},{6,2},{7,23},{8,12},{9,25},... | collective-permute-start | bytes 147464 | tf_op jit(solution)/shard_map/ppermute | solution.py:349
  36.7 4.3 %collective-permute-start.10 = (bf16[32,768]{1,0:T(8,128)(2,1)S(1)}, bf16[32,768]{1,0:T(8,128)(2,1)S(1)}, u32[]{:S(2)}, u32[]{:S(2)}) collective-permute-start(bf16[32,768]{1,0:T(8,128)(2,1)S(1)} %get-tuple-element.52.refs_0_), channel_id=1, source_target_pairs={{0,6},{1,25},{2,4},{3,27},{4,2},{5,29},{6,0},{7,31},{8,14},{9,17},... | collective-permute-start | bytes 147464 | tf_op jit(solution)/shard_map/ppermute | solution.py:349
  38.5 3.2 %collective-permute-start.9 = (bf16[32,768]{1,0:T(8,128)(2,1)S(1)}, bf16[32,768]{1,0:T(8,128)(2,1)S(1)}, u32[]{:S(2)}, u32[]{:S(2)}) collective-permute-start(bf16[32,768]{1,0:T(8,128)(2,1)S(1)} %get-tuple-element.52.refs_0_), channel_id=1, source_target_pairs={{0,2},{1,9},{2,0},{3,11},{4,6},{5,13},{6,4},{7,15},{8,10},{9,1},{1... | collective-permute-start | bytes 147464 | tf_op jit(solution)/shard_map/ppermute | solution.py:349
  41.7 6.2 %collective-permute-start.14 = (bf16[128,768]{1,0:T(8,128)(2,1)S(1)}, bf16[128,768]{1,0:T(8,128)(2,1)S(1)}, u32[]{:S(2)}, u32[]{:S(2)}) collective-permute-start(bf16[128,768]{1,0:T(8,128)(2,1)S(1)} %join.6.refs_0_), channel_id=1, source_target_pairs={{0,16},{1,5},{2,18},{3,7},{4,20},{5,1},{6,22},{7,3},{8,24},{9,13},... | collective-permute-start | bytes 589832 | tf_op jit(solution)/shard_map/ppermute | solution.py:349
  42.9 7.4 %collective-permute-start.13 = (bf16[128,768]{1,0:T(8,128)(2,1)S(1)}, bf16[128,768]{1,0:T(8,128)(2,1)S(1)}, u32[]{:S(2)}, u32[]{:S(2)}) collective-permute-start(bf16[128,768]{1,0:T(8,128)(2,1)S(1)} %join.6.refs_0_), channel_id=1, source_target_pairs={{0,24},{1,7},{2,26},{3,5},{4,28},{5,3},{6,30},{7,1},{8,16},{9,15},... | collective-permute-start | bytes 589832 | tf_op jit(solution)/shard_map/ppermute | solution.py:349
  44.3 5.9 %collective-permute-start.12 = (bf16[128,768]{1,0:T(8,128)(2,1)S(1)}, bf16[128,768]{1,0:T(8,128)(2,1)S(1)}, u32[]{:S(2)}, u32[]{:S(2)}) collective-permute-start(bf16[128,768]{1,0:T(8,128)(2,1)S(1)} %join.6.refs_0_), channel_id=1, source_target_pairs={{0,8},{1,3},{2,10},{3,1},{4,12},{5,7},{6,14},{7,5},{8,0},{9,11},{1... | collective-permute-start | bytes 589832 | tf_op jit(solution)/shard_map/ppermute | solution.py:349
  50.3 4.6 %collective-permute-start.15 = (bf16[512,768]{1,0:T(8,128)(2,1)S(1)}, bf16[512,768]{1,0:T(8,128)(2,1)S(1)}, u32[]{:S(2)}, u32[]{:S(2)}) collective-permute-start(bf16[512,768]{1,0:T(8,128)(2,1)S(1)} %join.7.near_ref), channel_id=1, source_target_pairs={{0,1},{1,0},{2,3},{3,2},{4,5},{5,4},{6,7},{7,6},{8,9},{9,8},{10,11... | collective-permute-start | bytes 2359304 | tf_op jit(solution)/shard_map/ppermute | solution.py:436
  53.0 1.9 %copy-start.1 = (bf16[768,128]{1,0:T(8,128)(2,1)S(1)}, bf16[768,128]{1,0:T(8,128)(2,1)}, u32[]{:S(2)}) copy-start(bf16[768,128]{1,0:T(8,128)(2,1)} %refs_10_.1) | copy-start | bytes 589828

commit v3 on v2

--- a/solution.py
+++ b/solution.py
@@ -65,42 +65,52 @@
     )
 
 
-def pack_kernel(single_hbm, bias_hbm, token_hbm, pair_hbm, pair_w_hbm, down_ref, up_ref,
-                single_ref, edge_ref, token_ref, pair_ref, pair_w_ref, sems):
+def pack_kernel(*refs):
+    sources, refs = refs[:8], refs[8:]
+    down_ref, up_ref, single_ref, edge_ref, token_ref = refs[:5]
+    pair_ref, pair_w_ref, sems = refs[8:]
+    pair_hbm, pair_w_hbm = sources[6:]
     copies = [
-        pltpu.make_async_copy(pair_hbm.at[0], pair_ref.at[0], sems.at[0]),
-        pltpu.make_async_copy(pair_hbm.at[TOKD - 1], pair_ref.at[1], sems.at[1]),
-        pltpu.make_async_copy(pair_w_hbm, pair_w_ref, sems.at[2]),
-        pltpu.make_async_copy(single_hbm.at[pl.ds(0, REACH)], single_ref.at[0], sems.at[3]),
-        pltpu.make_async_copy(single_hbm.at[pl.ds(ATOMD - REACH, REACH)], single_ref.at[1], sems.at[4]),
-        pltpu.make_async_copy(bias_hbm.at[pl.ds(0, EDGE)], edge_ref.at[0], sems.at[5]),
-        pltpu.make_async_copy(bias_hbm.at[pl.ds(ATOMD - EDGE, EDGE)], edge_ref.at[1], sems.at[6]),
-        pltpu.make_async_copy(token_hbm, token_ref, sems.at[7]),
+        pltpu.make_async_copy(source, ref, sems.at[i])
+        for i, (source, ref) in enumerate(zip(sources[:3], refs[2:5]))
+    ]
+    copies += [
+        pltpu.make_async_copy(pair_w_hbm, pair_w_ref, sems.at[3]),
+        pltpu.make_async_copy(pair_hbm.at[0], pair_ref.at[0], sems.at[4]),
+        pltpu.make_async_copy(pair_hbm.at[TOKD - 1], pair_ref.at[1], sems.at[5]),
+    ]
+    copies += [
+        pltpu.make_async_copy(source, ref, sems.at[6 + i])
+        for i, (source, ref) in enumerate(zip(sources[3:6], refs[5:8]))
     ]
     for copy in copies:
         copy.start()
     tok = lax.axis_index("tok")
     base = tok * TOKD
     orders = [chunk_starts(jnp.maximum(tok - 1, 0)), chunk_starts(jnp.minimum(tok + 1, 31))]
-    for copy in copies[3:]:
+    for copy in copies[:3]:
         copy.wait()
     for side, out_ref in enumerate((down_ref, up_ref)):
-        out_ref[:REACH] = single_ref[side]
+        atoms = slice(0, REACH) if side == 0 else slice(ATOMD - REACH, ATOMD)
+        edge = slice(0, EDGE) if side == 0 else slice(ATOMD - EDGE, ATOMD)
+        out_ref[:REACH] = single_ref[atoms]
         for h in range(AH):
-            out_ref[REACH + EDGE * h : REACH + EDGE * (h + 1)] = edge_ref[side, :, h * KW : (h + 1) * KW]
+            out_ref[REACH + EDGE * h : REACH + EDGE * (h + 1)] = edge_ref[edge, h * KW : (h + 1) * KW]
         relative = (token_ref[:, side * 128 : (side + 1) * 128] - base).astype(F32)
         out_ref[INFO : INFO + 16] = jnp.broadcast_to(relative, (16, 128)).astype(BF16)
-    copies[2].wait()
+    copies[3].wait()
     weights = pair_w_ref[...]
     for side, out_ref in enumerate((down_ref, up_ref)):
-        copies[side].wait()
+        copies[4 + side].wait()
         rows = ordered(pair_ref, side, orders[side])
         out = lax.dot_general(weights, rows, NT, preferred_element_type=F32).astype(BF16)
         for k in range(8):
             out_ref[PAIR + 32 * k : PAIR + 32 * (k + 1)] = out[:, 128 * k : 128 * (k + 1)]
-
-
-def bias_kernel(pair_ref, pair_w_ref, bias0_ref, bias1_ref):
+    for copy in copies[6:]:
+        copy.wait()
+
+
+def bias_kernel(pair_ref, pair_w_ref, token_ref, bias0_ref, bias1_ref, pick_ref, mask_ref):
     starts = chunk_starts(lax.axis_index("tok"))
     weights = pair_w_ref[...]
     for t in range(TOKD):
@@ -108,6 +118,10 @@
         out = lax.dot_general(weights, rows, NT, preferred_element_type=F32).astype(BF16)
         bias0_ref[t * H : (t + 1) * H] = out[:H]
         bias1_ref[t * H : (t + 1) * H] = out[H:]
+    member = (token_ref[...] - lax.axis_index("tok") * TOKD == wanted_tokens()).astype(F32)
+    member = jnp.concatenate([member, jnp.zeros((128 - ROWS, ATOMD), F32)], axis=0)
+    pick_ref[...] = member.T.astype(BF16)
+    mask_ref[...] = head_mask().astype(F32).astype(BF16)
 
 
 def windowed(proj_ref, k_row, q_row, count, bias, first_atom):
@@ -161,18 +175,9 @@
     return hidden, sums, counts
 
 
-def inner_atom_kernel(*refs):
-    sources, refs = refs[:6], refs[6:]
-    single_ref, bias_ref, token_ref, qkv_ref, out_w_ref, agg_ref = refs[:6]
-    proj_ref, hidden_ref, sums_ref, counts_ref, mixed_ref, sems = refs[6:]
-    copies = [
-        pltpu.make_async_copy(source, ref, sems.at[i]) for i, (source, ref) in enumerate(zip(sources, refs))
-    ]
-    for copy in copies:
-        copy.start()
+def inner_atom_kernel(single_ref, bias_ref, token_ref, qkv_ref, out_w_ref, agg_ref,
+                      proj_ref, hidden_ref, sums_ref, counts_ref, mixed_ref):
     tok = lax.axis_index("tok")
-    for copy in copies:
-        copy.wait()
     proj_ref[...] = projected(single_ref[...], qkv_ref)
     for i, w in enumerate((4, 5, 2, 3)):
         mixed_ref[QW * i : QW * (i + 1)] = windowed(
@@ -265,33 +270,57 @@
         out_ref[place * rows : (place + 1) * rows] = refs[i][...]
 
 
+def tree(combine, parts):
+    while len(parts) > 1:
+        parts = [combine(*parts[i : i + 2]) if len(parts[i : i + 2]) == 2 else parts[i] for i in range(0, len(parts), 2)]
+    return parts[0]
+
+
+def along(reduce, values):
+    return jnp.broadcast_to(reduce(values, axis=-1, keepdims=True), values.shape)
+
+
 def scored(query_ref, rows_ref, bias_ref, edge_bias_ref, half):
-    lanes = slice(half * HALF, (half + 1) * HALF)
     scores = lax.dot_general(query_ref[...], rows_ref[...], NT, preferred_element_type=F32)
-    return scores + jnp.concatenate([bias_ref[:, lanes], edge_bias_ref[:, lanes]], axis=0).astype(F32)
+    parts = []
+    for k in range(HALF // 128):
+        lanes = slice(half * HALF + 128 * k, half * HALF + 128 * (k + 1))
+        bias = jnp.concatenate([bias_ref[:, lanes], edge_bias_ref[:, lanes]], axis=0)
+        parts.append(scores[:, 128 * k : 128 * (k + 1)] + bias.astype(F32))
+    return parts
+
+
+def weighted(powers, rows_ref):
+    weights = jnp.concatenate([part.astype(BF16) for part in powers], axis=1)
+    return jnp.dot(weights, rows_ref[...], preferred_element_type=F32)
 
 
 def near_kernel(query_ref, near_ref, bias_ref, edge_bias_ref, mixed_ref, maximum_ref, total_ref):
     scores = scored(query_ref, near_ref, bias_ref, edge_bias_ref, 0)
-    maximum = jnp.max(scores, axis=-1, keepdims=True)
-    powers = jnp.exp(scores - maximum)
-    maximum_ref[...] = jnp.broadcast_to(maximum, maximum_ref.shape)
-    total_ref[...] = jnp.broadcast_to(jnp.sum(powers, axis=-1, keepdims=True), total_ref.shape)
-    mixed_ref[...] = jnp.dot(powers.astype(BF16), near_ref[...], preferred_element_type=F32)
-
-
-def attend(layer, query_ref, far_ref, bias_ref, edge_bias_ref, mixed_ref, maximum_ref, total_ref,
+    maximum = along(jnp.max, tree(jnp.maximum, scores))
+    powers = [jnp.exp(part - maximum) for part in scores]
+    maximum_ref[...] = maximum
+    total_ref[...] = tree(jnp.add, powers)
+    mixed_ref[...] = weighted(powers, near_ref)
+
+
+def attend(layer, query_ref, far_ref, bias_ref, edge_bias_ref, mixed_ref, maximum_ref, total_ref, mask_ref,
            qkv_ref, out_w_ref, stream_ref):
     scores = scored(query_ref, far_ref, bias_ref, edge_bias_ref, 1)
-    near_maximum = maximum_ref[:, :1]
-    maximum = jnp.maximum(near_maximum, jnp.max(scores, axis=-1, keepdims=True))
-    powers = jnp.exp(scores - maximum)
-    fade = jnp.exp(near_maximum - maximum)
-    total = total_ref[:, :1] * fade + jnp.sum(powers, axis=-1, keepdims=True)
-    mixed = mixed_ref[...] * fade + jnp.dot(powers.astype(BF16), far_ref[...], preferred_element_type=F32)
-    mixed = (mixed / total).astype(BF16)
-    valued = jnp.dot(mixed, qkv_ref[layer, :, 2 * C :], preferred_element_type=F32)
-    valued = jnp.where(head_mask(), valued, 0.0).astype(BF16)
+    maximum = jnp.maximum(maximum_ref[...], along(jnp.max, tree(jnp.maximum, scores)))
+    powers = [jnp.exp(part - maximum) for part in scores]
+    fade = jnp.exp(maximum_ref[...] - maximum)
+    share = 1.0 / along(jnp.sum, total_ref[...] * fade + tree(jnp.add, powers))
+    fade = fade * share
+    new = weighted(powers, far_ref)
+    mixed = jnp.concatenate(
+        [
+            (mixed_ref[:, 128 * k : 128 * (k + 1)] * fade + new[:, 128 * k : 128 * (k + 1)] * share).astype(BF16)
+            for k in range(C // 128)
+        ],
+        axis=1,
+    )
+    valued = jnp.dot(mixed, qkv_ref[layer, :, 2 * C :], preferred_element_type=F32).astype(BF16) * mask_ref[...]
     row = lax.broadcasted_iota(jnp.int32, (ROWS, QROWS), 0)
     column = lax.broadcasted_iota(jnp.int32, (ROWS, QROWS), 1)
     gather = ((column >> 4) == row).astype(F32).astype(BF16)
@@ -300,8 +329,8 @@
 
 
 def middle_kernel(*refs):
-    stream_ref, normed_ref, own_ref = refs[10:]
-    stream = attend(0, *refs[:10])
+    stream_ref, normed_ref, own_ref = refs[11:]
+    stream = attend(0, *refs[:11])
     stream_ref[...] = stream
     out = layer_norm(stream).astype(BF16)
     normed_ref[...] = out
@@ -309,13 +338,11 @@
 
 
 def last_kernel(*refs):
-    bcast_ref, token_ref, hidden_ref, atom_out_ref, token_out_ref = refs[10:]
-    token_out = attend(1, *refs[:10]).astype(BF16)
+    bcast_ref, pick_ref, hidden_ref, atom_out_ref, token_out_ref = refs[11:]
+    token_out = attend(1, *refs[:11]).astype(BF16)
     token_out_ref[...] = token_out[:TOKD]
     carry = jnp.dot(token_out, bcast_ref[...], preferred_element_type=F32).astype(BF16)
-    relative = token_ref[...] - lax.axis_index("tok") * TOKD
-    member = (relative == wanted_tokens()).astype(F32).astype(BF16)
-    picked = lax.dot_general(member, carry, (((0,), (0,)), ((), ())), preferred_element_type=F32)
+    picked = jnp.dot(pick_ref[:, :ROWS], carry, preferred_element_type=F32)
     atom_out_ref[...] = (hidden_ref[...].astype(F32) + picked).astype(BF16)
 
 
@@ -363,53 +390,48 @@
     pair_wt = pair_w.T
     hbm = pl.BlockSpec(memory_space=pltpu.HBM)
 
-    to_down, to_up = pl.pallas_call(
+    small = (atom_single, atom_bias, tokens, atom_qkv_w, atom_out_w, agg_w)
+    to_down, to_up, *small = pl.pallas_call(
         pack_kernel,
-        in_specs=[hbm] * 5,
-        out_specs=[VMEM] * 2,
-        out_shape=[shape(PACK, CA)] * 2,
+        in_specs=[hbm] * 8,
+        out_specs=[VMEM] * 8,
+        out_shape=[shape(PACK, CA)] * 2 + [jax.ShapeDtypeStruct(x.shape, x.dtype) for x in small],
         scratch_shapes=[
-            pltpu.VMEM((2, REACH, CA), BF16),
-            pltpu.VMEM((2, EDGE, AH * KW), BF16),
-            pltpu.VMEM((1, ATOMD), jnp.int32),
             pltpu.VMEM((2, KEYS, 128), BF16),
             pltpu.VMEM((32, 128), BF16),
-            pltpu.SemaphoreType.DMA((8,)),
+            pltpu.SemaphoreType.DMA((9,)),
         ],
         compiler_params=params(8),
         name="pack",
-    )(*in_hbm(atom_single, atom_bias, tokens, pair_rep, pair_wt))
+    )(*in_hbm(*small, pair_rep, pair_wt))
     from_upper = lax.ppermute(to_down, "tok", [((i + 1) % 32, i) for i in range(32)])
     from_lower = lax.ppermute(to_up, "tok", [(i, (i + 1) % 32) for i in range(32)])
 
-    bias = pl.pallas_call(
+    *bias, pick, mask = pl.pallas_call(
         bias_kernel,
-        in_specs=[VMEM] * 2,
-        out_specs=[VMEM] * 2,
-        out_shape=[shape(TOKD * H, KEYS)] * 2,
+        in_specs=[VMEM] * 3,
+        out_specs=[VMEM] * 4,
+        out_shape=[shape(TOKD * H, KEYS)] * 2 + [shape(ATOMD, 128), shape(QROWS, C)],
         compiler_params=params(12),
         cost_estimate=pl.CostEstimate(flops=2 * 32 * 1024 * 128 * 32, bytes_accessed=10 * 2**20, transcendentals=0),
         name="bias",
-    )(pair_rep, pair_wt)
-
-    small = (atom_single, atom_bias, tokens, atom_qkv_w, atom_out_w, agg_w)
+    )(pair_rep, pair_wt, small[2])
+
     inner = pl.pallas_call(
         inner_atom_kernel,
-        in_specs=[hbm] * 6,
-        out_specs=[VMEM] * 10,
-        out_shape=[jax.ShapeDtypeStruct(x.shape, x.dtype) for x in small]
-        + [
+        in_specs=[VMEM] * 6,
+        out_specs=[VMEM] * 4,
+        out_shape=[
             shape(ATOMD, 3 * CA),
             shape(4 * QW, CA),
             shape(ROWS, C, F32),
             shape(ROWS, 128, F32),
         ],
-        scratch_shapes=[pltpu.VMEM((4 * QW, CA), BF16), pltpu.SemaphoreType.DMA((6,))],
+        scratch_shapes=[pltpu.VMEM((4 * QW, CA), BF16)],
         compiler_params=params(8),
         cost_estimate=pl.CostEstimate(flops=10**9, bytes_accessed=5 * 2**20, transcendentals=0),
         name="inner_atoms",
-    )(*in_hbm(*small))
-    single, *rest = inner
+    )(*small)
     hidden, stream, normed, own, *edge_bias = pl.pallas_call(
         atom_kernel,
         in_specs=[VMEM] * 12,
@@ -418,7 +440,7 @@
         scratch_shapes=[pltpu.VMEM((2 * REACH + ATOMD, 3 * CA), BF16), pltpu.VMEM((256, CA), BF16)],
         compiler_params=params(8),
         name="atoms",
-    )(single, from_lower, from_upper, *rest)
+    )(small[0], from_lower, from_upper, *small[1:], *inner)
 
     for layer in range(2):
         pieces = exchange(own, True)
@@ -443,11 +465,11 @@
             cost_estimate=pl.CostEstimate(flops=2 * 10**9, bytes_accessed=5 * 2**20, transcendentals=300000),
             name="near",
         )(queries, near, bias[layer], edge_bias[layer])
-        operands = (queries, far, bias[layer], edge_bias[layer], *partial, tok_qkv_w, tok_out_w, stream)
+        operands = (queries, far, bias[layer], edge_bias[layer], *partial, mask, tok_qkv_w, tok_out_w, stream)
         if layer == 0:
             stream, normed, own = pl.pallas_call(
                 middle_kernel,
-                in_specs=[VMEM] * 10,
+                in_specs=[VMEM] * 11,
                 out_specs=[VMEM] * 3,
                 out_shape=[shape(ROWS, C, F32), shape(ROWS, C), shape(TOKD, C)],
                 compiler_params=params(16),
@@ -456,12 +478,12 @@
         else:
             atom_out, token_out = pl.pallas_call(
                 last_kernel,
-                in_specs=[VMEM] * 13,
+                in_specs=[VMEM] * 14,
                 out_specs=[VMEM] * 2,
                 out_shape=[shape(ATOMD, CA), shape(TOKD, C)],
                 compiler_params=params(16),
                 name="block_and_broadcast",
-            )(*operands, bcast_w, rest[1], hidden)
+            )(*operands, bcast_w, pick, hidden)
     return (atom_out, token_out)
 
 

time: 58.9 us -> 57.8 us (0.981)
  Pallas kernels: 22.4 us -> 20.8 us
  starting transfers between devices: 20.5 us -> 21.8 us
  waiting for transfers between devices: 15 us -> 14.3 us
    ppermute x12, waiting for transfers between devices: 12.5 us -> 10.5 us  [exchange(): lax.ppermute(rows, 'tok', crossed(k, first))]
    pallas_call x5, Pallas kernels: 13.9 us -> 12.3 us  [the longest x1 3.28 us: local(): pl.pallas_call(bias_kernel, in_specs=[VMEM] * 3, out_specs=[VMEM] * 4, ou...]
    ppermute x12, starting transfers between devices: 13.7 us -> 14.8 us  [exchange(): lax.ppermute(rows, 'tok', crossed(k, first))]
    ppermute x1, waiting for transfers between devices: 1.63 us -> 2.71 us  [local(): lax.ppermute(to_down, 'tok', [((i + 1) % 32, i) for i in range(32)])]
  transfers between devices with their start and end apart: 16 -> 16, of which waited for: 10 -> 11; matrix products, arithmetic and copies ran while one was open for 0% -> 0% of each run, Pallas kernels for 19% -> 18%
where the time goes in v3:
time: 57.8 us; the launch traced here: 57.7 us
  starting transfers between devices  21.8 us (38%)
  Pallas kernels  20.8 us (36%)
  waiting for transfers between devices  14.3 us (25%)
  between operations  0.78 us (1%)
    ppermute x12, starting transfers between devices, exchange(): lax.ppermute(rows, 'tok', crossed(k, first))  14.8 us
    ppermute x12, waiting for transfers between devices, exchange(): lax.ppermute(rows, 'tok', crossed(k, first))  10.5 us
    ppermute x2, starting transfers between devices, local(): far = lax.ppermute(near, 'tok', flips(0, 0, 1))  4.25 us
    pallas_call x1, Pallas kernels, local(): pl.pallas_call(bias_kernel, in_specs=[VMEM] * 3, out_specs=[VMEM] * 4, ou...  3.28 us
    pallas_call x1, Pallas kernels, local(): pl.pallas_call(last_kernel, in_specs=[VMEM] * 14, out_specs=[VMEM] * 2, o...  3.27 us
    pallas_call x2, Pallas kernels, local(): pl.pallas_call(near_kernel, in_specs=[VMEM] * 4, out_specs=[VMEM] * 3, ou...  2.98 us
    pallas_call x2, Pallas kernels, local(): pl.pallas_call(functools.partial(query_kernel, layer), in_specs=[VMEM] *...  2.8 us
    ppermute x1, starting transfers between devices, local(): lax.ppermute(to_up, 'tok', [(i, (i + 1) % 32) for i in range(32)])  2.76 us
  transfers between devices with their start and end apart: 16, of which 11 were waited for; matrix products, arithmetic and copies ran while one was open for 0% of the time, Pallas kernels for 18%

profile of v3, /device:TPU:1, one launch (start us, length us, event | category | flops | bytes accessed | tf_op | source)
XLA Modules:
  0.0 57.7 jit_solution(11251920077744672945)
XLA Ops:
  0.7 1.7 %pack.1 = (bf16[416,128]{1,0:T(8,128)(2,1)S(1)}, bf16[416,128]{1,0:T(8,128)(2,1)S(1)}, bf16[256,128]{1,0:T(8,128)(2,1)S(1)}, bf16[256,512]{1,0:T(8,128)(2,1)S(1)...) custom-call(bf16[256,128]{1,0:T(8,128)(2,1)} %refs_0_.1, ...), custom_call_target="tpu_custom_call" | custom-call | tf_op jit(solution)/shard_map/pack/pallas_call | solution.py:394
  2.4 2.8 %collective-permute-start = (bf16[416,128]{1,0:T(8,128)(2,1)S(1)}, bf16[416,128]{1,0:T(8,128)(2,1)S(1)}, u32[]{:S(2)}, u32[]{:S(2)}) collective-permute-start(bf16[416,128]{1,0:T(8,128)(2,1)S(1)} %get-tuple-element.34), channel_id=1, source_target_pairs={{0,1},{1,2},{2,3},{3,4},{4,5},{5,6},{6,7},{7,8},{8,9},{9,10},{10,1... | collective-permute-start | bytes 319496 | tf_op jit(solution)/shard_map/ppermute | solution.py:408
  5.2 1.4 %inner_atoms.1 = (bf16[256,384]{1,0:T(8,128)(2,1)S(1)}, bf16[128,128]{1,0:T(8,128)(2,1)S(1)}, f32[48,768]{1,0:T(8,128)S(1)}, f32[48,128]{1,0:T(8,128)S(1)}) custom-call(bf16[256,128]{1,0:T(8,128)(2,1)S(1)} %get-tuple-element.33.single_ref, bf16[256,512]{1,0:T(8,128)(2,1)S(1)} %get-tuple-element.36.bias_ref, s32[1,256]{1,0:T(1,128)S(1)} %get-tuple-element.37.token_ref, ...), custom_call_target="tpu_custom_call" | custom-call | flops 1000000000 | bytes 5242880 | tf_op jit(solution)/shard_map/inner_atoms/pallas_call | solution.py:420
  6.9 2.7 %collective-permute-done.1.upper_ref = bf16[416,128]{1,0:T(8,128)(2,1)S(1)} collective-permute-done((bf16[416,128]{1,0:T(8,128)(2,1)S(1)}, bf16[416,128]{1,0:T(8,128)(2,1)S(1)}, u32[]{:S(2)}, u32[]{:S(2)}) %collective-permute-start.1) | collective-permute-done | bytes 106528 | tf_op jit(solution)/shard_map/ppermute | solution.py:407
  9.6 2.6 %atoms.1 = (bf16[256,128]{1,0:T(8,128)(2,1)S(1)}, f32[48,768]{1,0:T(8,128)S(1)}, bf16[48,768]{1,0:T(8,128)(2,1)S(1)}, bf16[32,768]{1,0:T(8,128)(2,1)S(1)}, bf16[...) custom-call(bf16[256,128]{1,0:T(8,128)(2,1)S(1)} %get-tuple-element.33.single_ref, ...), custom_call_target="tpu_custom_call" | custom-call | tf_op jit(solution)/shard_map/atoms/pallas_call | solution.py:435
  12.2 2.8 %collective-permute-start.4 = (bf16[32,768]{1,0:T(8,128)(2,1)S(1)}, bf16[32,768]{1,0:T(8,128)(2,1)S(1)}, u32[]{:S(2)}, u32[]{:S(2)}) collective-permute-start(bf16[32,768]{1,0:T(8,128)(2,1)S(1)} %get-tuple-element.46.refs_0_), channel_id=1, source_target_pairs={{0,4},{1,17},{2,6},{3,19},{4,0},{5,21},{6,2},{7,23},{8,12},{9,25},... | collective-permute-start | bytes 147464 | tf_op jit(solution)/shard_map/ppermute | solution.py:376
  15.9 1.4 %queries.2.refs_4_.query_ref.refs_0_ = bf16[544,768]{1,0:T(8,128)(2,1)S(1)} custom-call(bf16[48,768]{1,0:T(8,128)(2,1)S(1)} %get-tuple-element.45.normed_ref, bf16[2,768,2304]{2,1,0:T(8,128)(2,1)S(1)} %bitcast.3), custom_call_target="tpu_custom_call" | custom-call | flops 1000000000 | bytes 5242880 | tf_op jit(solution)/shard_map/queries/pallas_call | solution.py:447
  17.3 2.1 %collective-permute-done.3.refs_2_ = bf16[32,768]{1,0:T(8,128)(2,1)S(1)} collective-permute-done((bf16[32,768]{1,0:T(8,128)(2,1)S(1)}, bf16[32,768]{1,0:T(8,128)(2,1)S(1)}, u32[]{:S(2)}, u32[]{:S(2)}) %collective-permute-start.3) | collective-permute-done | bytes 49184 | tf_op jit(solution)/shard_map/ppermute | solution.py:376
  19.5 2.1 %collective-permute-start.7 = (bf16[128,768]{1,0:T(8,128)(2,1)S(1)}, bf16[128,768]{1,0:T(8,128)(2,1)S(1)}, u32[]{:S(2)}, u32[]{:S(2)}) collective-permute-start(bf16[128,768]{1,0:T(8,128)(2,1)S(1)} %join.4.refs_0_), channel_id=1, source_target_pairs={{0,16},{1,5},{2,18},{3,7},{4,20},{5,1},{6,22},{7,3},{8,24},{9,13},... | collective-permute-start | bytes 589832 | tf_op jit(solution)/shard_map/ppermute | solution.py:376
  21.6 1.6 %collective-permute-start.6 = (bf16[128,768]{1,0:T(8,128)(2,1)S(1)}, bf16[128,768]{1,0:T(8,128)(2,1)S(1)}, u32[]{:S(2)}, u32[]{:S(2)}) collective-permute-start(bf16[128,768]{1,0:T(8,128)(2,1)S(1)} %join.4.refs_0_), channel_id=1, source_target_pairs={{0,24},{1,7},{2,26},{3,5},{4,28},{5,3},{6,30},{7,1},{8,16},{9,15},... | collective-permute-start | bytes 589832 | tf_op jit(solution)/shard_map/ppermute | solution.py:376
  23.7 3.3 %bias.1 = (bf16[512,1024]{1,0:T(8,128)(2,1)S(1)}, bf16[512,1024]{1,0:T(8,128)(2,1)S(1)}, bf16[256,128]{1,0:T(8,128)(2,1)S(1)}, bf16[544,768]{1,0:T(8,128)(2,1)S(1)}) custom-call(bf16[32,1024,128]{2,1,0:T(8,128)(2,1)S(1)} %bitcast.5, bf16[32,128]{1,0:T(8,128)(2,1)S(1)} %bitcast.7, s32[1,256]{1,0:T(1,128)S(1)} %get-tuple-element.37.token_ref), custom_call_target="tpu_custom_call" | custom-call | flops 268435456 | bytes 10485760 | tf_op jit(solution)/shard_map/bias/pallas_call | solution.py:410
  29.5 1.5 %near.2 = (f32[544,768]{1,0:T(8,128)S(1)}, f32[544,128]{1,0:T(8,128)S(1)}, f32[544,128]{1,0:T(8,128)S(1)}) custom-call(bf16[544,768]{1,0:T(8,128)(2,1)S(1)} %queries.2.refs_4_.query_ref.refs_0_, bf16[512,768]{1,0:T(8,128)(2,1)S(1)} %join.5.near_ref, bf16[512,1024]{1,0:T(8,128)(2,1)S(1)} %get-tuple-element.47.refs_4_.bias_ref.refs_2_, ...), custom_call_target="tpu_custom_call" | custom-call | flops 2000000000 | bytes 5242880 | tf_op jit(solution)/shard_map/near/pallas_call | solution.py:459
  31.4 2.5 %block.1 = (f32[48,768]{1,0:T(8,128)S(1)}, bf16[48,768]{1,0:T(8,128)(2,1)S(1)}, bf16[32,768]{1,0:T(8,128)(2,1)S(1)}) custom-call(bf16[544,768]{1,0:T(8,128)(2,1)S(1)} %queries.2.refs_4_.query_ref.refs_0_, bf16[512,768]{1,0:T(8,128)(2,1)S(1)} %collective-permute-done.8.refs_1_, bf16[512,1024]{1,0:T(8,128)(2,1)S(1)} %get-tuple-element.47.refs_4_.bias_ref.refs_2_, ...), custom_call_target="tpu_custom_call" | custom-call | tf_op jit(solution)/shard_map/block/pallas_call | solution.py:470
  33.9 2.0 %collective-permute-start.11 = (bf16[32,768]{1,0:T(8,128)(2,1)S(1)}, bf16[32,768]{1,0:T(8,128)(2,1)S(1)}, u32[]{:S(2)}, u32[]{:S(2)}) collective-permute-start(bf16[32,768]{1,0:T(8,128)(2,1)S(1)} %get-tuple-element.55.refs_0_), channel_id=1, source_target_pairs={{0,4},{1,17},{2,6},{3,19},{4,0},{5,21},{6,2},{7,23},{8,12},{9,25},... | collective-permute-start | bytes 147464 | tf_op jit(solution)/shard_map/ppermute | solution.py:376
  35.9 1.3 %collective-permute-start.10 = (bf16[32,768]{1,0:T(8,128)(2,1)S(1)}, bf16[32,768]{1,0:T(8,128)(2,1)S(1)}, u32[]{:S(2)}, u32[]{:S(2)}) collective-permute-start(bf16[32,768]{1,0:T(8,128)(2,1)S(1)} %get-tuple-element.55.refs_0_), channel_id=1, source_target_pairs={{0,6},{1,25},{2,4},{3,27},{4,2},{5,29},{6,0},{7,31},{8,14},{9,17},... | collective-permute-start | bytes 147464 | tf_op jit(solution)/shard_map/ppermute | solution.py:376
  37.2 1.4 %queries.3.refs_4_.query_ref.refs_0_ = bf16[544,768]{1,0:T(8,128)(2,1)S(1)} custom-call(bf16[48,768]{1,0:T(8,128)(2,1)S(1)} %get-tuple-element.54.normed_ref, bf16[2,768,2304]{2,1,0:T(8,128)(2,1)S(1)} %bitcast.3), custom_call_target="tpu_custom_call" | custom-call | flops 1000000000 | bytes 5242880 | tf_op jit(solution)/shard_map/queries/pallas_call | solution.py:447
  38.6 1.5 %collective-permute-done.10.refs_2_ = bf16[32,768]{1,0:T(8,128)(2,1)S(1)} collective-permute-done((bf16[32,768]{1,0:T(8,128)(2,1)S(1)}, bf16[32,768]{1,0:T(8,128)(2,1)S(1)}, u32[]{:S(2)}, u32[]{:S(2)}) %collective-permute-start.10) | collective-permute-done | bytes 49184 | tf_op jit(solution)/shard_map/ppermute | solution.py:376
  40.2 1.6 %collective-permute-start.14 = (bf16[128,768]{1,0:T(8,128)(2,1)S(1)}, bf16[128,768]{1,0:T(8,128)(2,1)S(1)}, u32[]{:S(2)}, u32[]{:S(2)}) collective-permute-start(bf16[128,768]{1,0:T(8,128)(2,1)S(1)} %join.6.refs_0_), channel_id=1, source_target_pairs={{0,16},{1,5},{2,18},{3,7},{4,20},{5,1},{6,22},{7,3},{8,24},{9,13},... | collective-permute-start | bytes 589832 | tf_op jit(solution)/shard_map/ppermute | solution.py:376
  41.8 2.1 %collective-permute-start.13 = (bf16[128,768]{1,0:T(8,128)(2,1)S(1)}, bf16[128,768]{1,0:T(8,128)(2,1)S(1)}, u32[]{:S(2)}, u32[]{:S(2)}) collective-permute-start(bf16[128,768]{1,0:T(8,128)(2,1)S(1)} %join.6.refs_0_), channel_id=1, source_target_pairs={{0,24},{1,7},{2,26},{3,5},{4,28},{5,3},{6,30},{7,1},{8,16},{9,15},... | collective-permute-start | bytes 589832 | tf_op jit(solution)/shard_map/ppermute | solution.py:376
  43.9 2.5 %collective-permute-done.14.refs_3_ = bf16[128,768]{1,0:T(8,128)(2,1)S(1)} collective-permute-done((bf16[128,768]{1,0:T(8,128)(2,1)S(1)}, bf16[128,768]{1,0:T(8,128)(2,1)S(1)}, u32[]{:S(2)}, u32[]{:S(2)}) %collective-permute-start.14) | collective-permute-done | bytes 196640 | tf_op jit(solution)/shard_map/ppermute | solution.py:376
  46.4 2.3 %collective-permute-done.13.refs_2_ = bf16[128,768]{1,0:T(8,128)(2,1)S(1)} collective-permute-done((bf16[128,768]{1,0:T(8,128)(2,1)S(1)}, bf16[128,768]{1,0:T(8,128)(2,1)S(1)}, u32[]{:S(2)}, u32[]{:S(2)}) %collective-permute-start.13) | collective-permute-done | bytes 196640 | tf_op jit(solution)/shard_map/ppermute | solution.py:376
  48.7 3.8 %collective-permute-start.15 = (bf16[512,768]{1,0:T(8,128)(2,1)S(1)}, bf16[512,768]{1,0:T(8,128)(2,1)S(1)}, u32[]{:S(2)}, u32[]{:S(2)}) collective-permute-start(bf16[512,768]{1,0:T(8,128)(2,1)S(1)} %join.7.near_ref), channel_id=1, source_target_pairs={{0,1},{1,0},{2,3},{3,2},{4,5},{5,4},{6,7},{7,6},{8,9},{9,8},{10,11... | collective-permute-start | bytes 2359304 | tf_op jit(solution)/shard_map/ppermute | solution.py:458
  52.5 1.5 %near.3 = (f32[544,768]{1,0:T(8,128)S(1)}, f32[544,128]{1,0:T(8,128)S(1)}, f32[544,128]{1,0:T(8,128)S(1)}) custom-call(bf16[544,768]{1,0:T(8,128)(2,1)S(1)} %queries.3.refs_4_.query_ref.refs_0_, bf16[512,768]{1,0:T(8,128)(2,1)S(1)} %join.7.near_ref, bf16[512,1024]{1,0:T(8,128)(2,1)S(1)} %get-tuple-element.56.bias_ref.refs_2_, ...), custom_call_target="tpu_custom_call" | custom-call | flops 2000000000 | bytes 5242880 | tf_op jit(solution)/shard_map/near/pallas_call | solution.py:459
  54.4 3.3 %block_and_broadcast.1 = (bf16[256,128]{1,0:T(8,128)(2,1)}, bf16[32,768]{1,0:T(8,128)(2,1)}) custom-call(bf16[544,768]{1,0:T(8,128)(2,1)S(1)} %queries.3.refs_4_.query_ref.refs_0_, bf16[512,768]{1,0:T(8,128)(2,1)S(1)} %collective-permute-done.15.refs_1_, bf16[512,1024]{1,0:T(8,128)(2,1)S(1)} %get-tuple-element.56.bias_ref.refs_2_, ...), custom_call_target="tpu_custom_call" | custom-call | tf_op jit(solution)/shard_map/block_and_broadcast/pallas_call | solution.py:479
  (38 shorter events, 5.1 us)
Async XLA Ops:
  0.6 15.2 %slice-start = ((s8[7077888]{0:T(1024)(128)(4,1)}), s8[4194304]{0:T(1024)(128)(4,1)S(1)}, s32[]{:S(2)}) async-start(s8[7077888]{0:T(1024)(128)(4,1)} %bitcast.2), calls=%async_computation | async-start | bytes 8388608
  0.6 15.2 %slice-start.1 = ((s8[7077888]{0:T(1024)(128)(4,1)}), s8[2883584]{0:T(1024)(128)(4,1)S(1)}, s32[]{:S(2)}) async-start(s8[7077888]{0:T(1024)(128)(4,1)} %bitcast.2), calls=%async_computation.1 | async-start | bytes 5767168
  0.7 23.0 %slice-start.2 = ((s8[8388608]{0:T(1024)(128)(4,1)}), s8[4194304]{0:T(1024)(128)(4,1)S(1)}, s32[]{:S(2)}) async-start(s8[8388608]{0:T(1024)(128)(4,1)} %bitcast.4), calls=%async_computation.2 | async-start | bytes 8388608
  2.4 4.5 %collective-permute-start = (bf16[416,128]{1,0:T(8,128)(2,1)S(1)}, bf16[416,128]{1,0:T(8,128)(2,1)S(1)}, u32[]{:S(2)}, u32[]{:S(2)}) collective-permute-start(bf16[416,128]{1,0:T(8,128)(2,1)S(1)} %get-tuple-element.34), channel_id=1, source_target_pairs={{0,1},{1,2},{2,3},{3,4},{4,5},{5,6},{6,7},{7,8},{8,9},{9,10},{10,1... | collective-permute-start | bytes 319496 | tf_op jit(solution)/shard_map/ppermute | solution.py:408
  5.2 4.4 %collective-permute-start.1 = (bf16[416,128]{1,0:T(8,128)(2,1)S(1)}, bf16[416,128]{1,0:T(8,128)(2,1)S(1)}, u32[]{:S(2)}, u32[]{:S(2)}) collective-permute-start(bf16[416,128]{1,0:T(8,128)(2,1)S(1)} %get-tuple-element.35), channel_id=1, source_target_pairs={{1,0},{2,1},{3,2},{4,3},{5,4},{6,5},{7,6},{8,7},{9,8},{10,9},{11,1... | collective-permute-start | bytes 319496 | tf_op jit(solution)/shard_map/ppermute | solution.py:407
  5.2 18.5 %slice-start.3 = ((s8[8388608]{0:T(1024)(128)(4,1)}), s8[4194304]{0:T(1024)(128)(4,1)S(1)}, s32[]{:S(2)}) async-start(s8[8388608]{0:T(1024)(128)(4,1)} %bitcast.4), calls=%async_computation.3 | async-start | bytes 8388608
  12.2 5.1 %collective-permute-start.4 = (bf16[32,768]{1,0:T(8,128)(2,1)S(1)}, bf16[32,768]{1,0:T(8,128)(2,1)S(1)}, u32[]{:S(2)}, u32[]{:S(2)}) collective-permute-start(bf16[32,768]{1,0:T(8,128)(2,1)S(1)} %get-tuple-element.46.refs_0_), channel_id=1, source_target_pairs={{0,4},{1,17},{2,6},{3,19},{4,0},{5,21},{6,2},{7,23},{8,12},{9,25},... | collective-permute-start | bytes 147464 | tf_op jit(solution)/shard_map/ppermute | solution.py:376
  15.0 4.4 %collective-permute-start.3 = (bf16[32,768]{1,0:T(8,128)(2,1)S(1)}, bf16[32,768]{1,0:T(8,128)(2,1)S(1)}, u32[]{:S(2)}, u32[]{:S(2)}) collective-permute-start(bf16[32,768]{1,0:T(8,128)(2,1)S(1)} %get-tuple-element.46.refs_0_), channel_id=1, source_target_pairs={{0,6},{1,25},{2,4},{3,27},{4,2},{5,29},{6,0},{7,31},{8,14},{9,17},... | collective-permute-start | bytes 147464 | tf_op jit(solution)/shard_map/ppermute | solution.py:376
  15.9 3.6 %collective-permute-start.2 = (bf16[32,768]{1,0:T(8,128)(2,1)S(1)}, bf16[32,768]{1,0:T(8,128)(2,1)S(1)}, u32[]{:S(2)}, u32[]{:S(2)}) collective-permute-start(bf16[32,768]{1,0:T(8,128)(2,1)S(1)} %get-tuple-element.46.refs_0_), channel_id=1, source_target_pairs={{0,2},{1,9},{2,0},{3,11},{4,6},{5,13},{6,4},{7,15},{8,10},{9,1},{1... | collective-permute-start | bytes 147464 | tf_op jit(solution)/shard_map/ppermute | solution.py:376
  15.9 7.8 %copy-start.2 = (bf16[128,32]{0,1:T(8,128)(2,1)S(1)}, bf16[128,32]{0,1:T(8,128)(2,1)}, u32[]{:S(2)}) copy-start(bf16[128,32]{0,1:T(8,128)(2,1)} %param.21) | copy-start | bytes 24580
  19.5 7.5 %collective-permute-start.7 = (bf16[128,768]{1,0:T(8,128)(2,1)S(1)}, bf16[128,768]{1,0:T(8,128)(2,1)S(1)}, u32[]{:S(2)}, u32[]{:S(2)}) collective-permute-start(bf16[128,768]{1,0:T(8,128)(2,1)S(1)} %join.4.refs_0_), channel_id=1, source_target_pairs={{0,16},{1,5},{2,18},{3,7},{4,20},{5,1},{6,22},{7,3},{8,24},{9,13},... | collective-permute-start | bytes 589832 | tf_op jit(solution)/shard_map/ppermute | solution.py:376
  21.6 6.4 %collective-permute-start.6 = (bf16[128,768]{1,0:T(8,128)(2,1)S(1)}, bf16[128,768]{1,0:T(8,128)(2,1)S(1)}, u32[]{:S(2)}, u32[]{:S(2)}) collective-permute-start(bf16[128,768]{1,0:T(8,128)(2,1)S(1)} %join.4.refs_0_), channel_id=1, source_target_pairs={{0,24},{1,7},{2,26},{3,5},{4,28},{5,3},{6,30},{7,1},{8,16},{9,15},... | collective-permute-start | bytes 589832 | tf_op jit(solution)/shard_map/ppermute | solution.py:376
  23.2 5.8 %collective-permute-start.5 = (bf16[128,768]{1,0:T(8,128)(2,1)S(1)}, bf16[128,768]{1,0:T(8,128)(2,1)S(1)}, u32[]{:S(2)}, u32[]{:S(2)}) collective-permute-start(bf16[128,768]{1,0:T(8,128)(2,1)S(1)} %join.4.refs_0_), channel_id=1, source_target_pairs={{0,8},{1,3},{2,10},{3,1},{4,12},{5,7},{6,14},{7,5},{8,0},{9,11},{1... | collective-permute-start | bytes 589832 | tf_op jit(solution)/shard_map/ppermute | solution.py:376
  29.0 2.4 %collective-permute-start.8 = (bf16[512,768]{1,0:T(8,128)(2,1)S(1)}, bf16[512,768]{1,0:T(8,128)(2,1)S(1)}, u32[]{:S(2)}, u32[]{:S(2)}) collective-permute-start(bf16[512,768]{1,0:T(8,128)(2,1)S(1)} %join.5.near_ref), channel_id=1, source_target_pairs={{0,1},{1,0},{2,3},{3,2},{4,5},{5,4},{6,7},{7,6},{8,9},{9,8},{10,11... | collective-permute-start | bytes 2359304 | tf_op jit(solution)/shard_map/ppermute | solution.py:458
  29.5 1.9 %copy-start = (bf16[2,768,768]{2,1,0:T(8,128)(2,1)S(1)}, bf16[2,768,768]{2,1,0:T(8,128)(2,1)}, u32[]{:S(2)}) copy-start(bf16[2,768,768]{2,1,0:T(8,128)(2,1)} %refs_9_.3) | copy-start | bytes 7077892
  33.9 4.7 %collective-permute-start.11 = (bf16[32,768]{1,0:T(8,128)(2,1)S(1)}, bf16[32,768]{1,0:T(8,128)(2,1)S(1)}, u32[]{:S(2)}, u32[]{:S(2)}) collective-permute-start(bf16[32,768]{1,0:T(8,128)(2,1)S(1)} %get-tuple-element.55.refs_0_), channel_id=1, source_target_pairs={{0,4},{1,17},{2,6},{3,19},{4,0},{5,21},{6,2},{7,23},{8,12},{9,25},... | collective-permute-start | bytes 147464 | tf_op jit(solution)/shard_map/ppermute | solution.py:376
  35.9 4.2 %collective-permute-start.10 = (bf16[32,768]{1,0:T(8,128)(2,1)S(1)}, bf16[32,768]{1,0:T(8,128)(2,1)S(1)}, u32[]{:S(2)}, u32[]{:S(2)}) collective-permute-start(bf16[32,768]{1,0:T(8,128)(2,1)S(1)} %get-tuple-element.55.refs_0_), channel_id=1, source_target_pairs={{0,6},{1,25},{2,4},{3,27},{4,2},{5,29},{6,0},{7,31},{8,14},{9,17},... | collective-permute-start | bytes 147464 | tf_op jit(solution)/shard_map/ppermute | solution.py:376
  37.2 2.9 %collective-permute-start.9 = (bf16[32,768]{1,0:T(8,128)(2,1)S(1)}, bf16[32,768]{1,0:T(8,128)(2,1)S(1)}, u32[]{:S(2)}, u32[]{:S(2)}) collective-permute-start(bf16[32,768]{1,0:T(8,128)(2,1)S(1)} %get-tuple-element.55.refs_0_), channel_id=1, source_target_pairs={{0,2},{1,9},{2,0},{3,11},{4,6},{5,13},{6,4},{7,15},{8,10},{9,1},{1... | collective-permute-start | bytes 147464 | tf_op jit(solution)/shard_map/ppermute | solution.py:376
  40.2 6.2 %collective-permute-start.14 = (bf16[128,768]{1,0:T(8,128)(2,1)S(1)}, bf16[128,768]{1,0:T(8,128)(2,1)S(1)}, u32[]{:S(2)}, u32[]{:S(2)}) collective-permute-start(bf16[128,768]{1,0:T(8,128)(2,1)S(1)} %join.6.refs_0_), channel_id=1, source_target_pairs={{0,16},{1,5},{2,18},{3,7},{4,20},{5,1},{6,22},{7,3},{8,24},{9,13},... | collective-permute-start | bytes 589832 | tf_op jit(solution)/shard_map/ppermute | solution.py:376
  41.8 6.9 %collective-permute-start.13 = (bf16[128,768]{1,0:T(8,128)(2,1)S(1)}, bf16[128,768]{1,0:T(8,128)(2,1)S(1)}, u32[]{:S(2)}, u32[]{:S(2)}) collective-permute-start(bf16[128,768]{1,0:T(8,128)(2,1)S(1)} %join.6.refs_0_), channel_id=1, source_target_pairs={{0,24},{1,7},{2,26},{3,5},{4,28},{5,3},{6,30},{7,1},{8,16},{9,15},... | collective-permute-start | bytes 589832 | tf_op jit(solution)/shard_map/ppermute | solution.py:376
  43.8 4.8 %collective-permute-start.12 = (bf16[128,768]{1,0:T(8,128)(2,1)S(1)}, bf16[128,768]{1,0:T(8,128)(2,1)S(1)}, u32[]{:S(2)}, u32[]{:S(2)}) collective-permute-start(bf16[128,768]{1,0:T(8,128)(2,1)S(1)} %join.6.refs_0_), channel_id=1, source_target_pairs={{0,8},{1,3},{2,10},{3,1},{4,12},{5,7},{6,14},{7,5},{8,0},{9,11},{1... | collective-permute-start | bytes 589832 | tf_op jit(solution)/shard_map/ppermute | solution.py:376
  48.7 5.7 %collective-permute-start.15 = (bf16[512,768]{1,0:T(8,128)(2,1)S(1)}, bf16[512,768]{1,0:T(8,128)(2,1)S(1)}, u32[]{:S(2)}, u32[]{:S(2)}) collective-permute-start(bf16[512,768]{1,0:T(8,128)(2,1)S(1)} %join.7.near_ref), channel_id=1, source_target_pairs={{0,1},{1,0},{2,3},{3,2},{4,5},{5,4},{6,7},{7,6},{8,9},{9,8},{10,11... | collective-permute-start | bytes 2359304 | tf_op jit(solution)/shard_map/ppermute | solution.py:458
  52.5 1.9 %copy-start.1 = (bf16[768,128]{1,0:T(8,128)(2,1)S(1)}, bf16[768,128]{1,0:T(8,128)(2,1)}, u32[]{:S(2)}) copy-start(bf16[768,128]{1,0:T(8,128)(2,1)} %refs_11_.1) | copy-start | bytes 589828

commit v4 on v3

--- a/solution.py
+++ b/solution.py
@@ -15,6 +15,7 @@
 QW = 32
 KW = 128
 HALO = 48
+NB = 2
 EDGE = 16
 REACH = EDGE + 64
 TOKD = 32
@@ -25,8 +26,7 @@
 HALF = 512
 CHUNK = 32
 INFO = REACH + AH * EDGE
-PAIR = INFO + 16
-PACK = PAIR + 8 * 32
+PACK = INFO + 16
 F32 = jnp.float32
 BF16 = jnp.bfloat16
 
@@ -45,6 +45,16 @@
     centred = values - average
     variance = jnp.mean(centred * centred, axis=-1, keepdims=True)
     return centred * lax.rsqrt(variance + 1e-05)
+
+
+def tree(combine, parts):
+    while len(parts) > 1:
+        parts = [combine(*parts[i : i + 2]) if len(parts[i : i + 2]) == 2 else parts[i] for i in range(0, len(parts), 2)]
+    return parts[0]
+
+
+def along(reduce, values):
+    return jnp.broadcast_to(reduce(values, axis=-1, keepdims=True), values.shape)
 
 
 def chunk_starts(tok):
@@ -65,52 +75,43 @@
     )
 
 
+def for_neighbours(core, apart_ref, beside_ref, fill):
+    for first, refs in ((0, (apart_ref, beside_ref)), (1, (beside_ref, apart_ref))):
+        @pl.when(core == first)
+        def _():
+            for side, ref in enumerate(refs):
+                fill(side, ref)
+
+
 def pack_kernel(*refs):
-    sources, refs = refs[:8], refs[8:]
-    down_ref, up_ref, single_ref, edge_ref, token_ref = refs[:5]
-    pair_ref, pair_w_ref, sems = refs[8:]
-    pair_hbm, pair_w_hbm = sources[6:]
+    sources, targets, sems = refs[:6], refs[8:14], refs[14]
+    apart_ref, beside_ref = refs[6:8]
+    single_ref, edge_ref, token_ref = targets[:3]
     copies = [
-        pltpu.make_async_copy(source, ref, sems.at[i])
-        for i, (source, ref) in enumerate(zip(sources[:3], refs[2:5]))
-    ]
-    copies += [
-        pltpu.make_async_copy(pair_w_hbm, pair_w_ref, sems.at[3]),
-        pltpu.make_async_copy(pair_hbm.at[0], pair_ref.at[0], sems.at[4]),
-        pltpu.make_async_copy(pair_hbm.at[TOKD - 1], pair_ref.at[1], sems.at[5]),
-    ]
-    copies += [
-        pltpu.make_async_copy(source, ref, sems.at[6 + i])
-        for i, (source, ref) in enumerate(zip(sources[3:6], refs[5:8]))
+        pltpu.make_async_copy(source, target, sems.at[i])
+        for i, (source, target) in enumerate(zip(sources, targets))
     ]
     for copy in copies:
         copy.start()
     tok = lax.axis_index("tok")
-    base = tok * TOKD
-    orders = [chunk_starts(jnp.maximum(tok - 1, 0)), chunk_starts(jnp.minimum(tok + 1, 31))]
     for copy in copies[:3]:
         copy.wait()
-    for side, out_ref in enumerate((down_ref, up_ref)):
-        atoms = slice(0, REACH) if side == 0 else slice(ATOMD - REACH, ATOMD)
+
+    def fill(side, out_ref):
+        rows = slice(0, REACH) if side == 0 else slice(ATOMD - REACH, ATOMD)
         edge = slice(0, EDGE) if side == 0 else slice(ATOMD - EDGE, ATOMD)
-        out_ref[:REACH] = single_ref[atoms]
+        out_ref[:REACH] = single_ref[rows]
         for h in range(AH):
             out_ref[REACH + EDGE * h : REACH + EDGE * (h + 1)] = edge_ref[edge, h * KW : (h + 1) * KW]
-        relative = (token_ref[:, side * 128 : (side + 1) * 128] - base).astype(F32)
+        relative = (token_ref[:, side * 128 : (side + 1) * 128] - tok * TOKD).astype(F32)
         out_ref[INFO : INFO + 16] = jnp.broadcast_to(relative, (16, 128)).astype(BF16)
-    copies[3].wait()
-    weights = pair_w_ref[...]
-    for side, out_ref in enumerate((down_ref, up_ref)):
-        copies[4 + side].wait()
-        rows = ordered(pair_ref, side, orders[side])
-        out = lax.dot_general(weights, rows, NT, preferred_element_type=F32).astype(BF16)
-        for k in range(8):
-            out_ref[PAIR + 32 * k : PAIR + 32 * (k + 1)] = out[:, 128 * k : 128 * (k + 1)]
-    for copy in copies[6:]:
+
+    for_neighbours(lax.rem(tok, 2), apart_ref, beside_ref, fill)
+    for copy in copies[3:]:
         copy.wait()
 
 
-def bias_kernel(pair_ref, pair_w_ref, token_ref, bias0_ref, bias1_ref, pick_ref, mask_ref):
+def bias_kernel(pair_ref, pair_w_ref, bias0_ref, bias1_ref):
     starts = chunk_starts(lax.axis_index("tok"))
     weights = pair_w_ref[...]
     for t in range(TOKD):
@@ -118,32 +119,42 @@
         out = lax.dot_general(weights, rows, NT, preferred_element_type=F32).astype(BF16)
         bias0_ref[t * H : (t + 1) * H] = out[:H]
         bias1_ref[t * H : (t + 1) * H] = out[H:]
-    member = (token_ref[...] - lax.axis_index("tok") * TOKD == wanted_tokens()).astype(F32)
-    member = jnp.concatenate([member, jnp.zeros((128 - ROWS, ATOMD), F32)], axis=0)
-    pick_ref[...] = member.T.astype(BF16)
-    mask_ref[...] = head_mask().astype(F32).astype(BF16)
-
-
-def windowed(proj_ref, k_row, q_row, count, bias, first_atom):
+
+
+def windowed(proj_ref, windows, first_atom):
     head_of_lane = lax.broadcasted_iota(jnp.int32, (1, CA), 1) // (CA // AH)
-    queries = proj_ref[q_row : q_row + count, :CA]
-    keys = proj_ref[k_row : k_row + KW, CA : 2 * CA]
-    values = proj_ref[k_row : k_row + KW, 2 * CA :]
-    stacked = jnp.concatenate(
-        [jnp.where(head_of_lane == h, queries, jnp.zeros_like(queries)) for h in range(AH)], axis=0
-    )
-    scores = lax.dot_general(stacked, keys, NT, preferred_element_type=F32) * (CA // AH) ** (-0.5)
-    scores = scores + jnp.concatenate(bias, axis=0).astype(F32)
-    position = first_atom + k_row + lax.broadcasted_iota(jnp.int32, (1, KW), 1)
-    inside = (position >= 0) & (position < 32 * ATOMD)
-    scores = jnp.where(inside, scores, -1000000000.0)
-    powers = jnp.exp(scores - jnp.max(scores, axis=-1, keepdims=True))
-    total = jnp.sum(powers, axis=-1, keepdims=True)
-    mixed = jnp.dot(powers.astype(BF16), values, preferred_element_type=F32) / total
-    merged = jnp.where(head_of_lane == 0, mixed[:count], 0.0)
-    for h in range(1, AH):
-        merged = jnp.where(head_of_lane == h, mixed[h * count : (h + 1) * count], merged)
-    return merged.astype(BF16)
+    heads = [head_of_lane == h for h in range(AH)]
+    lane = lax.broadcasted_iota(jnp.int32, (1, KW), 1)
+    products = []
+    for k_row, q_row, count, bias in windows:
+        queries = proj_ref[q_row : q_row + count, :CA]
+        stacked = jnp.concatenate([jnp.where(head, queries, jnp.zeros_like(queries)) for head in heads], axis=0)
+        keys = proj_ref[k_row : k_row + KW, CA : 2 * CA]
+        products.append(lax.dot_general(stacked, keys, NT, preferred_element_type=F32))
+    scores = []
+    for product, (k_row, q_row, count, bias) in zip(products, windows):
+        position = first_atom + k_row + lane
+        inside = (position >= 0) & (position < 32 * ATOMD)
+        score = product * (CA // AH) ** (-0.5) + jnp.concatenate(bias, axis=0).astype(F32)
+        scores.append(jnp.where(inside, score, -1000000000.0))
+    scores = jnp.concatenate(scores, axis=0)
+    powers = jnp.exp(scores - along(jnp.max, scores))
+    share = 1.0 / along(jnp.sum, powers)
+    weights = powers.astype(BF16)
+    mixed = []
+    first = 0
+    for k_row, q_row, count, bias in windows:
+        values = proj_ref[k_row : k_row + KW, 2 * CA :]
+        rows = slice(first, first + AH * count)
+        mixed.append(jnp.dot(weights[rows], values, preferred_element_type=F32) * share[rows])
+        first += AH * count
+    merged = []
+    for rows, (k_row, q_row, count, bias) in zip(mixed, windows):
+        out = jnp.where(heads[0], rows[:count], 0.0)
+        for h in range(1, AH):
+            out = jnp.where(heads[h], rows[h * count : (h + 1) * count], out)
+        merged.append(out.astype(BF16))
+    return merged
 
 
 def projected(rows, qkv_ref):
@@ -176,42 +187,43 @@
 
 
 def inner_atom_kernel(single_ref, bias_ref, token_ref, qkv_ref, out_w_ref, agg_ref,
-                      proj_ref, hidden_ref, sums_ref, counts_ref, mixed_ref):
+                      proj_ref, hidden_ref, sums_ref, counts_ref, pick_ref, mask_ref):
     tok = lax.axis_index("tok")
     proj_ref[...] = projected(single_ref[...], qkv_ref)
-    for i, w in enumerate((4, 5, 2, 3)):
-        mixed_ref[QW * i : QW * (i + 1)] = windowed(
-            proj_ref, QW * w - HALO, QW * w, QW, own_bias(bias_ref, w), tok * ATOMD
-        )
+    windows = [(QW * w - HALO, QW * w, QW, own_bias(bias_ref, w)) for w in (4, 5, 2, 3)]
+    mixed = jnp.concatenate(windowed(proj_ref, windows, tok * ATOMD), axis=0)
     lane = lax.broadcasted_iota(jnp.int32, (1, 128), 1)
     relative = jnp.where(lane < 64, token_ref[:, 128:], token_ref[:, :128]) - tok * TOKD
     hidden_in = jnp.concatenate([single_ref[128:192], single_ref[64:128]], axis=0)
-    hidden, sums, counts = hidden_and_sums(hidden_in, mixed_ref[...], relative, out_w_ref, agg_ref)
+    hidden, sums, counts = hidden_and_sums(hidden_in, mixed, relative, out_w_ref, agg_ref)
     hidden_ref[:64] = hidden[64:]
     hidden_ref[64:] = hidden[:64]
     sums_ref[...] = sums
     counts_ref[...] = jnp.broadcast_to(counts, counts_ref.shape)
-
-
-def atom_kernel(single_ref, lower_ref, upper_ref, bias_ref, token_ref, qkv_ref, out_w_ref, agg_ref,
+    member = (token_ref[...] - tok * TOKD == wanted_tokens()).astype(F32)
+    member = jnp.concatenate([member, jnp.zeros((128 - ROWS, ATOMD), F32)], axis=0)
+    pick_ref[...] = member.T.astype(BF16)
+    mask_ref[...] = head_mask().astype(F32).astype(BF16)
+
+
+def atom_kernel(single_ref, apart_ref, beside_ref, bias_ref, token_ref, qkv_ref, out_w_ref, agg_ref,
                 inner_ref, inner_hidden_ref, inner_sums_ref, inner_counts_ref,
-                hidden_ref, stream_ref, normed_ref, own_ref, edge0_ref, edge1_ref, proj_ref, mixed_ref):
+                hidden_ref, stream_ref, normed_ref, own_ref, proj_ref, both_ref):
     tok = lax.axis_index("tok")
+    core = lax.rem(tok, 2)
+    both_ref[0] = apart_ref[...]
+    both_ref[1] = beside_ref[...]
+    lower_ref, upper_ref = both_ref.at[core], both_ref.at[1 - core]
     first_atom = tok * ATOMD - REACH
     beside = projected(jnp.concatenate([lower_ref[:REACH], upper_ref[:REACH]], axis=0), qkv_ref)
     proj_ref[:REACH] = beside[:REACH]
     proj_ref[REACH : REACH + ATOMD] = inner_ref[...]
     proj_ref[REACH + ATOMD :] = beside[REACH:]
-    mixed_ref[128 + EDGE : 256 - EDGE] = jnp.zeros((128 - 2 * EDGE, CA), BF16)
-    for i, w in enumerate((0, 1, 6, 7)):
-        mixed_ref[QW * i : QW * (i + 1)] = windowed(
-            proj_ref, 32 + QW * w, REACH + QW * w, QW, own_bias(bias_ref, w), first_atom
-        )
-    for out_row, q_row, k_row, ref in (
-        (128, REACH + ATOMD, 288, upper_ref), (256 - EDGE, REACH - EDGE, 0, lower_ref)
-    ):
-        bias = [ref[REACH + EDGE * h : REACH + EDGE * (h + 1)] for h in range(AH)]
-        mixed_ref[out_row : out_row + EDGE] = windowed(proj_ref, k_row, q_row, EDGE, bias, first_atom)
+    windows = [(32 + QW * w, REACH + QW * w, QW, own_bias(bias_ref, w)) for w in (0, 1, 6, 7)]
+    for k_row, q_row, ref in ((288, REACH + ATOMD, upper_ref), (0, REACH - EDGE, lower_ref)):
+        windows.append((k_row, q_row, EDGE, [ref[REACH + EDGE * h : REACH + EDGE * (h + 1)] for h in range(AH)]))
+    mixed = windowed(proj_ref, windows, first_atom)
+    mixed.insert(5, jnp.zeros((128 - 2 * EDGE, CA), BF16))
     hidden_in = jnp.concatenate(
         [
             single_ref[:64],
@@ -228,7 +240,7 @@
     near = jnp.where(lane < EDGE, after, jnp.where(lane >= 128 - EDGE, before, -100))
     outer = jnp.where(lane < 64, token_ref[:, :128], token_ref[:, 128:]) - tok * TOKD
     hidden, sums, counts = hidden_and_sums(
-        hidden_in, mixed_ref[...], jnp.concatenate([outer, near], axis=1), out_w_ref, agg_ref
+        hidden_in, jnp.concatenate(mixed, axis=0), jnp.concatenate([outer, near], axis=1), out_w_ref, agg_ref
     )
     hidden_ref[:64] = hidden[:64]
     hidden_ref[64:192] = inner_hidden_ref[...]
@@ -238,11 +250,6 @@
     out = layer_norm(stream).astype(BF16)
     normed_ref[...] = out
     own_ref[...] = out[:TOKD]
-    for block, ref in enumerate((edge0_ref, edge1_ref)):
-        for side, source in enumerate((lower_ref, upper_ref)):
-            for k in range(8):
-                first = PAIR + 32 * k + H * block
-                ref[H * side : H * (side + 1), 128 * k : 128 * (k + 1)] = source[first : first + H]
 
 
 def head_mask():
@@ -263,21 +270,46 @@
     out_ref[...] = (lifted * HEAD ** (-0.5)).astype(BF16)
 
 
+def first_query_kernel(normed_ref, qkv_ref, pair_hbm, pair_w_hbm, out_ref, apart_ref, beside_ref,
+                       pair_ref, pair_w_ref, sems):
+    copies = [
+        pltpu.make_async_copy(pair_w_hbm, pair_w_ref, sems.at[0]),
+        pltpu.make_async_copy(pair_hbm.at[0], pair_ref.at[0], sems.at[1]),
+        pltpu.make_async_copy(pair_hbm.at[TOKD - 1], pair_ref.at[1], sems.at[2]),
+    ]
+    for copy in copies:
+        copy.start()
+    query_kernel(0, normed_ref, qkv_ref, out_ref)
+    for copy in copies:
+        copy.wait()
+    tok = lax.axis_index("tok")
+    outs = []
+    for side, owner in enumerate((jnp.maximum(tok - 1, 0), jnp.minimum(tok + 1, 31))):
+        rows = ordered(pair_ref, side, chunk_starts(owner))
+        outs.append(lax.dot_general(pair_w_ref[...], rows, NT, preferred_element_type=F32).astype(BF16))
+
+    def fill(side, ref):
+        ref[...] = outs[side]
+
+    for_neighbours(lax.rem(tok, 2), apart_ref, beside_ref, fill)
+
+
+def join_edges_kernel(*refs):
+    join_kernel(0, *refs[:4], refs[7])
+    both_ref = refs[10]
+    both_ref[0] = refs[4][...]
+    both_ref[1] = refs[5][...]
+    core = lax.rem(lax.axis_index("tok"), 2)
+    for block, ref in enumerate(refs[8:10]):
+        for side, index in enumerate((core, 1 - core)):
+            ref[side * H : (side + 1) * H] = both_ref[index, block * H : (block + 1) * H]
+
+
 def join_kernel(count, *refs):
     out_ref = refs[-1]
     rows = out_ref.shape[0] // 4
     for i, place in enumerate((0, 1, 3, 2)):
         out_ref[place * rows : (place + 1) * rows] = refs[i][...]
-
-
-def tree(combine, parts):
-    while len(parts) > 1:
-        parts = [combine(*parts[i : i + 2]) if len(parts[i : i + 2]) == 2 else parts[i] for i in range(0, len(parts), 2)]
-    return parts[0]
-
-
-def along(reduce, values):
-    return jnp.broadcast_to(reduce(values, axis=-1, keepdims=True), values.shape)
 
 
 def scored(query_ref, rows_ref, bias_ref, edge_bias_ref, half):
@@ -391,70 +423,98 @@
     hbm = pl.BlockSpec(memory_space=pltpu.HBM)
 
     small = (atom_single, atom_bias, tokens, atom_qkv_w, atom_out_w, agg_w)
-    to_down, to_up, *small = pl.pallas_call(
+    to_apart, to_beside, *small = pl.pallas_call(
         pack_kernel,
-        in_specs=[hbm] * 8,
+        in_specs=[hbm] * 6,
         out_specs=[VMEM] * 8,
         out_shape=[shape(PACK, CA)] * 2 + [jax.ShapeDtypeStruct(x.shape, x.dtype) for x in small],
-        scratch_shapes=[
-            pltpu.VMEM((2, KEYS, 128), BF16),
-            pltpu.VMEM((32, 128), BF16),
-            pltpu.SemaphoreType.DMA((9,)),
-        ],
+        scratch_shapes=[pltpu.SemaphoreType.DMA((6,))],
         compiler_params=params(8),
+        cost_estimate=pl.CostEstimate(flops=4 * 10**9, bytes_accessed=16 * 2**20, transcendentals=0),
         name="pack",
-    )(*in_hbm(*small, pair_rep, pair_wt))
-    from_upper = lax.ppermute(to_down, "tok", [((i + 1) % 32, i) for i in range(32)])
-    from_lower = lax.ppermute(to_up, "tok", [(i, (i + 1) % 32) for i in range(32)])
-
-    *bias, pick, mask = pl.pallas_call(
+    )(*in_hbm(*small))
+    across = [(i, (i + (1 if i % 2 else -1)) % 32) for i in range(32)]
+    apart = lax.ppermute(to_apart, "tok", across)
+    beside = lax.ppermute(to_beside, "tok", flips(0, 0, 1))
+
+    bias = pl.pallas_call(
         bias_kernel,
-        in_specs=[VMEM] * 3,
-        out_specs=[VMEM] * 4,
-        out_shape=[shape(TOKD * H, KEYS)] * 2 + [shape(ATOMD, 128), shape(QROWS, C)],
+        in_specs=[VMEM] * 2,
+        out_specs=[VMEM] * 2,
+        out_shape=[shape(TOKD * H, KEYS)] * 2,
         compiler_params=params(12),
         cost_estimate=pl.CostEstimate(flops=2 * 32 * 1024 * 128 * 32, bytes_accessed=10 * 2**20, transcendentals=0),
         name="bias",
-    )(pair_rep, pair_wt, small[2])
-
-    inner = pl.pallas_call(
+    )(pair_rep, pair_wt)
+
+    *inner, pick, mask = pl.pallas_call(
         inner_atom_kernel,
         in_specs=[VMEM] * 6,
-        out_specs=[VMEM] * 4,
+        out_specs=[VMEM] * 6,
         out_shape=[
             shape(ATOMD, 3 * CA),
             shape(4 * QW, CA),
             shape(ROWS, C, F32),
             shape(ROWS, 128, F32),
+            shape(ATOMD, 128),
+            shape(QROWS, C),
         ],
-        scratch_shapes=[pltpu.VMEM((4 * QW, CA), BF16)],
         compiler_params=params(8),
-        cost_estimate=pl.CostEstimate(flops=10**9, bytes_accessed=5 * 2**20, transcendentals=0),
+        cost_estimate=pl.CostEstimate(flops=4 * 10**9, bytes_accessed=16 * 2**20, transcendentals=0),
         name="inner_atoms",
     )(*small)
-    hidden, stream, normed, own, *edge_bias = pl.pallas_call(
+    hidden, stream, normed, own = pl.pallas_call(
         atom_kernel,
         in_specs=[VMEM] * 12,
-        out_specs=[VMEM] * 6,
-        out_shape=[shape(ATOMD, CA), shape(ROWS, C, F32), shape(ROWS, C), shape(TOKD, C)] + [shape(2 * H, KEYS)] * 2,
-        scratch_shapes=[pltpu.VMEM((2 * REACH + ATOMD, 3 * CA), BF16), pltpu.VMEM((256, CA), BF16)],
+        out_specs=[VMEM] * 4,
+        out_shape=[shape(ATOMD, CA), shape(ROWS, C, F32), shape(ROWS, C), shape(TOKD, C)],
+        scratch_shapes=[pltpu.VMEM((2 * REACH + ATOMD, 3 * CA), BF16), pltpu.VMEM((2, PACK, CA), BF16)],
         compiler_params=params(8),
+        cost_estimate=pl.CostEstimate(flops=4 * 10**9, bytes_accessed=16 * 2**20, transcendentals=0),
         name="atoms",
-    )(small[0], from_lower, from_upper, *small[1:], *inner)
+    )(small[0], apart, beside, *small[1:], *inner)
 
     for layer in range(2):
         pieces = exchange(own, True)
-        queries = pl.pallas_call(
-            functools.partial(query_kernel, layer),
-            in_specs=[VMEM] * 2,
-            out_specs=VMEM,
-            out_shape=shape(QROWS, C),
-            compiler_params=params(16),
-            cost_estimate=pl.CostEstimate(flops=10**9, bytes_accessed=5 * 2**20, transcendentals=0),
-            name="queries",
-        )(normed, tok_qkv_w)
+        if layer == 0:
+            queries, *edges = pl.pallas_call(
+                first_query_kernel,
+                in_specs=[VMEM] * 2 + [hbm] * 2,
+                out_specs=[VMEM] * 3,
+                out_shape=[shape(QROWS, C)] + [shape(NB * H, KEYS)] * 2,
+                scratch_shapes=[
+                    pltpu.VMEM((2, KEYS, 128), BF16),
+                    pltpu.VMEM((32, 128), BF16),
+                    pltpu.SemaphoreType.DMA((3,)),
+                ],
+                compiler_params=params(16),
+                cost_estimate=pl.CostEstimate(flops=10**9, bytes_accessed=5 * 2**20, transcendentals=0),
+                name="queries",
+            )(normed, tok_qkv_w, *in_hbm(pair_rep, pair_wt))
+            edges = [lax.ppermute(edges[0], "tok", across), lax.ppermute(edges[1], "tok", flips(0, 0, 1))]
+        else:
+            queries = pl.pallas_call(
+                functools.partial(query_kernel, layer),
+                in_specs=[VMEM] * 2,
+                out_specs=VMEM,
+                out_shape=shape(QROWS, C),
+                compiler_params=params(16),
+                cost_estimate=pl.CostEstimate(flops=10**9, bytes_accessed=5 * 2**20, transcendentals=0),
+                name="queries",
+            )(normed, tok_qkv_w)
         pieces = exchange(join(pieces, [queries]), False)
-        near = join(pieces, [bias[0]] if layer == 0 else [])
+        if layer == 0:
+            near, *edge_bias = pl.pallas_call(
+                join_edges_kernel,
+                in_specs=[VMEM] * 6 + [pl.BlockSpec(memory_space=pl.ANY)],
+                out_specs=[VMEM] * 3,
+                out_shape=[shape(HALF, C)] + [shape(2 * H, KEYS)] * 2,
+                scratch_shapes=[pltpu.VMEM((2, NB * H, KEYS), BF16)],
+                compiler_params=params(8),
+                name="join",
+            )(*pieces, *edges, bias[0])
+        else:
+            near = join(pieces, [])
         far = lax.ppermute(near, "tok", flips(0, 0, 1))
         partial = pl.pallas_call(
             near_kernel,

time: 57.8 us -> 55.5 us (0.960)
  waiting for transfers between devices: 14.3 us -> 8.96 us
  starting transfers between devices: 21.8 us -> 26.1 us
  Pallas kernels: 20.8 us -> 19.4 us
    ppermute x2 -> x4, starting transfers between devices: 2.76 us -> 9.98 us  [the longest x1 3.47 us: local(): beside = lax.ppermute(to_beside, 'tok', flips(0, 0, 1))]
    ppermute x12, starting transfers between devices: 14.8 us -> 11.8 us  [exchange(): lax.ppermute(rows, 'tok', crossed(k, first))]
    ppermute x2 -> x4, waiting for transfers between devices: 2.96 us -> 0.01 us  [the longest x1 0.01 us: local(): beside = lax.ppermute(to_beside, 'tok', flips(0, 0, 1))]
    ppermute x12, waiting for transfers between devices: 10.5 us -> 8.11 us  [exchange(): lax.ppermute(rows, 'tok', crossed(k, first))]
    pallas_call x2 -> x1, Pallas kernels: 2.8 us -> 1.4 us  [local(): pl.pallas_call(functools.partial(query_kernel, layer), in_specs=[VMEM] *...]
    pallas_call x3 -> x5, Pallas kernels: 7.61 us -> 7.27 us  [the longest x1 2.64 us: local(): pl.pallas_call(bias_kernel, in_specs=[VMEM] * 2, out_specs=[VMEM] * 2, ou...]
  transfers between devices with their start and end apart: 16 -> 18, of which waited for: 11 -> 8; matrix products, arithmetic and copies ran while one was open for 0% -> 0% of each run, Pallas kernels for 18% -> 19%
where the time goes in v4:
time: 55.5 us; the launch traced here: 55.4 us
  starting transfers between devices  26.1 us (47%)
  Pallas kernels  19.4 us (35%)
  waiting for transfers between devices  8.96 us (16%)
  between operations  0.84 us (2%)
    ppermute x12, starting transfers between devices, exchange(): lax.ppermute(rows, 'tok', crossed(k, first))  11.8 us
    ppermute x12, waiting for transfers between devices, exchange(): lax.ppermute(rows, 'tok', crossed(k, first))  8.11 us
    ppermute x2, starting transfers between devices, local(): far = lax.ppermute(near, 'tok', flips(0, 0, 1))  4.33 us
    ppermute x1, starting transfers between devices, local(): beside = lax.ppermute(to_beside, 'tok', flips(0, 0, 1))  3.47 us
    pallas_call x1, Pallas kernels, local(): pl.pallas_call(last_kernel, in_specs=[VMEM] * 14, out_specs=[VMEM] * 2, o...  3.27 us
    pallas_call x2, Pallas kernels, local(): pl.pallas_call(near_kernel, in_specs=[VMEM] * 4, out_specs=[VMEM] * 3, ou...  2.98 us
    ppermute x1, starting transfers between devices, local(): apart = lax.ppermute(to_apart, 'tok', across)  2.77 us
    pallas_call x1, Pallas kernels, local(): pl.pallas_call(bias_kernel, in_specs=[VMEM] * 2, out_specs=[VMEM] * 2, ou...  2.64 us
  transfers between devices with their start and end apart: 18, of which 8 were waited for; matrix products, arithmetic and copies ran while one was open for 0% of the time, Pallas kernels for 19%

profile of v4, /device:TPU:1, one launch (start us, length us, event | category | flops | bytes accessed | tf_op | source)
XLA Modules:
  0.0 55.4 jit_solution(1986549622162940957)
XLA Ops:
  1.8 2.8 %collective-permute-start = (bf16[160,128]{1,0:T(8,128)(2,1)S(1)}, bf16[160,128]{1,0:T(8,128)(2,1)S(1)}, u32[]{:S(2)}, u32[]{:S(2)}) collective-permute-start(bf16[160,128]{1,0:T(8,128)(2,1)S(1)} %get-tuple-element.38), channel_id=1, source_target_pairs={{0,31},{1,2},{2,1},{3,4},{4,3},{5,6},{6,5},{7,8},{8,7},{9,10},{10,... | collective-permute-start | bytes 122888 | tf_op jit(solution)/shard_map/ppermute | solution.py:437
  4.6 3.5 %collective-permute-start.1 = (bf16[160,128]{1,0:T(8,128)(2,1)S(1)}, bf16[160,128]{1,0:T(8,128)(2,1)S(1)}, u32[]{:S(2)}, u32[]{:S(2)}) collective-permute-start(bf16[160,128]{1,0:T(8,128)(2,1)S(1)} %get-tuple-element.39), channel_id=1, source_target_pairs={{0,1},{1,0},{2,3},{3,2},{4,5},{5,4},{6,7},{7,6},{8,9},{9,8},{10,11... | collective-permute-start | bytes 122888 | tf_op jit(solution)/shard_map/ppermute | solution.py:438
  8.1 1.9 %inner_atoms.1 = (bf16[256,384]{1,0:T(8,128)(2,1)S(1)}, bf16[128,128]{1,0:T(8,128)(2,1)S(1)}, f32[48,768]{1,0:T(8,128)S(1)}, f32[48,128]{1,0:T(8,128)S(1)}, bf16...) custom-call(bf16[256,128]{1,0:T(8,128)(2,1)S(1)} %get-tuple-element.37.single_ref, ...), custom_call_target="tpu_custom_call" | custom-call | flops 4000000000 | bytes 16777216 | tf_op jit(solution)/shard_map/inner_atoms/pallas_call | solution.py:450
  10.0 1.5 %atoms.1 = (bf16[256,128]{1,0:T(8,128)(2,1)S(1)}, f32[48,768]{1,0:T(8,128)S(1)}, bf16[48,768]{1,0:T(8,128)(2,1)S(1)}, bf16[32,768]{1,0:T(8,128)(2,1)S(1)}) custom-call(bf16[256,128]{1,0:T(8,128)(2,1)S(1)} %get-tuple-element.37.single_ref, bf16[160,128]{1,0:T(8,128)(2,1)S(1)} %collective-permute-done.apart_ref, ...), custom_call_target="tpu_custom_call" | custom-call | flops 4000000000 | bytes 16777216 | tf_op jit(solution)/shard_map/atoms/pallas_call | solution.py:466
  13.0 1.3 %collective-permute-start.2 = (bf16[32,768]{1,0:T(8,128)(2,1)S(1)}, bf16[32,768]{1,0:T(8,128)(2,1)S(1)}, u32[]{:S(2)}, u32[]{:S(2)}) collective-permute-start(bf16[32,768]{1,0:T(8,128)(2,1)S(1)} %get-tuple-element.51.refs_0_), channel_id=1, source_target_pairs={{0,2},{1,9},{2,0},{3,11},{4,6},{5,13},{6,4},{7,15},{8,10},{9,1},{1... | collective-permute-start | bytes 147464 | tf_op jit(solution)/shard_map/ppermute | solution.py:408
  14.3 1.9 %queries.2 = (bf16[544,768]{1,0:T(8,128)(2,1)S(1)}, bf16[32,1024]{1,0:T(8,128)(2,1)S(1)}, bf16[32,1024]{1,0:T(8,128)(2,1)S(1)}) custom-call(bf16[48,768]{1,0:T(8,128)(2,1)S(1)} %get-tuple-element.49.normed_ref, bf16[2,768,2304]{2,1,0:T(8,128)(2,1)S(1)} %bitcast.3, bf16[32,1024,128]{2,1,0:T(8,128)(2,1)} %pair_ref.1, bf16[32,128]{1,0:T(8,128)(2,1)} %bitcast.6), custom_call_target="tpu_custom_call" | custom-call | flops 1000000000 | bytes 5242880 | tf_op jit(solution)/shard_map/queries/pallas_call | solution.py:480
  17.9 1.7 %collective-permute-start.6 = (bf16[128,768]{1,0:T(8,128)(2,1)S(1)}, bf16[128,768]{1,0:T(8,128)(2,1)S(1)}, u32[]{:S(2)}, u32[]{:S(2)}) collective-permute-start(bf16[128,768]{1,0:T(8,128)(2,1)S(1)} %join.4.refs_0_), channel_id=1, source_target_pairs={{0,24},{1,7},{2,26},{3,5},{4,28},{5,3},{6,30},{7,1},{8,16},{9,15},... | collective-permute-start | bytes 589832 | tf_op jit(solution)/shard_map/ppermute | solution.py:408
  20.2 2.3 %collective-permute-start.8 = (bf16[32,1024]{1,0:T(8,128)(2,1)S(1)}, bf16[32,1024]{1,0:T(8,128)(2,1)S(1)}, u32[]{:S(2)}, u32[]{:S(2)}) collective-permute-start(bf16[32,1024]{1,0:T(8,128)(2,1)S(1)} %get-tuple-element.52), channel_id=1, source_target_pairs={{0,31},{1,2},{2,1},{3,4},{4,3},{5,6},{6,5},{7,8},{8,7},{9,10},{10,... | collective-permute-start | bytes 196616 | tf_op jit(solution)/shard_map/ppermute | solution.py:494
  22.4 1.5 %collective-permute-start.9 = (bf16[32,1024]{1,0:T(8,128)(2,1)S(1)}, bf16[32,1024]{1,0:T(8,128)(2,1)S(1)}, u32[]{:S(2)}, u32[]{:S(2)}) collective-permute-start(bf16[32,1024]{1,0:T(8,128)(2,1)S(1)} %get-tuple-element.53), channel_id=1, source_target_pairs={{0,1},{1,0},{2,3},{3,2},{4,5},{5,4},{6,7},{7,6},{8,9},{9,8},{10,11... | collective-permute-start | bytes 196616 | tf_op jit(solution)/shard_map/ppermute | solution.py:494
  23.9 2.6 %bias.1 = (bf16[512,1024]{1,0:T(8,128)(2,1)S(1)}, bf16[512,1024]{1,0:T(8,128)(2,1)S(1)}) custom-call(bf16[32,1024,128]{2,1,0:T(8,128)(2,1)S(1)} %bitcast.5, bf16[32,128]{1,0:T(8,128)(2,1)S(1)} %bitcast.7), custom_call_target="tpu_custom_call" | custom-call | flops 268435456 | bytes 10485760 | tf_op jit(solution)/shard_map/bias/pallas_call | solution.py:440
  26.7 2.6 %collective-permute-start.10 = (bf16[512,768]{1,0:T(8,128)(2,1)S(1)}, bf16[512,768]{1,0:T(8,128)(2,1)S(1)}, u32[]{:S(2)}, u32[]{:S(2)}) collective-permute-start(bf16[512,768]{1,0:T(8,128)(2,1)S(1)} %get-tuple-element.55.near_ref), channel_id=1, source_target_pairs={{0,1},{1,0},{2,3},{3,2},{4,5},{5,4},{6,7},{7,6},{8,9},{9,8},{10,11... | collective-permute-start | bytes 2359304 | tf_op jit(solution)/shard_map/ppermute | solution.py:518
  29.4 1.5 %near.2 = (f32[544,768]{1,0:T(8,128)S(1)}, f32[544,128]{1,0:T(8,128)S(1)}, f32[544,128]{1,0:T(8,128)S(1)}) custom-call(bf16[544,768]{1,0:T(8,128)(2,1)S(1)} %get-tuple-element.50.refs_4_.query_ref.refs_0_, bf16[512,768]{1,0:T(8,128)(2,1)S(1)} %get-tuple-element.55.near_ref, bf16[512,1024]{1,0:T(8,128)(2,1)S(1)} %get-tuple-element.54.refs_6_.bias_ref.refs_2_, ...), custom_call_target="tpu_custom_call" | custom-call | flops 2000000000 | bytes 5242880 | tf_op jit(solution)/shard_map/near/pallas_call | solution.py:519
  31.3 2.6 %block.1 = (f32[48,768]{1,0:T(8,128)S(1)}, bf16[48,768]{1,0:T(8,128)(2,1)S(1)}, bf16[32,768]{1,0:T(8,128)(2,1)S(1)}) custom-call(bf16[544,768]{1,0:T(8,128)(2,1)S(1)} %get-tuple-element.50.refs_4_.query_ref.refs_0_, bf16[512,768]{1,0:T(8,128)(2,1)S(1)} %collective-permute-done.10.refs_1_, bf16[512,1024]{1,0:T(8,128)(2,1)S(1)} %get-tuple-element.54.refs_6_.bias_ref.refs_2_, ...), custom_call_target="tpu_custom_call" | custom-call | tf_op jit(solution)/shard_map/block/pallas_call | solution.py:530
  33.8 1.4 %collective-permute-start.13 = (bf16[32,768]{1,0:T(8,128)(2,1)S(1)}, bf16[32,768]{1,0:T(8,128)(2,1)S(1)}, u32[]{:S(2)}, u32[]{:S(2)}) collective-permute-start(bf16[32,768]{1,0:T(8,128)(2,1)S(1)} %get-tuple-element.63.refs_0_), channel_id=1, source_target_pairs={{0,4},{1,17},{2,6},{3,19},{4,0},{5,21},{6,2},{7,23},{8,12},{9,25},... | collective-permute-start | bytes 147464 | tf_op jit(solution)/shard_map/ppermute | solution.py:408
  35.3 1.6 %collective-permute-start.12 = (bf16[32,768]{1,0:T(8,128)(2,1)S(1)}, bf16[32,768]{1,0:T(8,128)(2,1)S(1)}, u32[]{:S(2)}, u32[]{:S(2)}) collective-permute-start(bf16[32,768]{1,0:T(8,128)(2,1)S(1)} %get-tuple-element.63.refs_0_), channel_id=1, source_target_pairs={{0,6},{1,25},{2,4},{3,27},{4,2},{5,29},{6,0},{7,31},{8,14},{9,17},... | collective-permute-start | bytes 147464 | tf_op jit(solution)/shard_map/ppermute | solution.py:408
  36.9 1.4 %queries.3.refs_4_.query_ref.refs_0_ = bf16[544,768]{1,0:T(8,128)(2,1)S(1)} custom-call(bf16[48,768]{1,0:T(8,128)(2,1)S(1)} %get-tuple-element.62.normed_ref, bf16[2,768,2304]{2,1,0:T(8,128)(2,1)S(1)} %bitcast.3), custom_call_target="tpu_custom_call" | custom-call | flops 1000000000 | bytes 5242880 | tf_op jit(solution)/shard_map/queries/pallas_call | solution.py:496
  38.3 1.4 %collective-permute-done.12.refs_2_ = bf16[32,768]{1,0:T(8,128)(2,1)S(1)} collective-permute-done((bf16[32,768]{1,0:T(8,128)(2,1)S(1)}, bf16[32,768]{1,0:T(8,128)(2,1)S(1)}, u32[]{:S(2)}, u32[]{:S(2)}) %collective-permute-start.12) | collective-permute-done | bytes 49184 | tf_op jit(solution)/shard_map/ppermute | solution.py:408
  40.2 1.3 %collective-permute-start.15 = (bf16[128,768]{1,0:T(8,128)(2,1)S(1)}, bf16[128,768]{1,0:T(8,128)(2,1)S(1)}, u32[]{:S(2)}, u32[]{:S(2)}) collective-permute-start(bf16[128,768]{1,0:T(8,128)(2,1)S(1)} %join.6.refs_0_), channel_id=1, source_target_pairs={{0,24},{1,7},{2,26},{3,5},{4,28},{5,3},{6,30},{7,1},{8,16},{9,15},... | collective-permute-start | bytes 589832 | tf_op jit(solution)/shard_map/ppermute | solution.py:408
  41.5 1.3 %collective-permute-start.14 = (bf16[128,768]{1,0:T(8,128)(2,1)S(1)}, bf16[128,768]{1,0:T(8,128)(2,1)S(1)}, u32[]{:S(2)}, u32[]{:S(2)}) collective-permute-start(bf16[128,768]{1,0:T(8,128)(2,1)S(1)} %join.6.refs_0_), channel_id=1, source_target_pairs={{0,8},{1,3},{2,10},{3,1},{4,12},{5,7},{6,14},{7,5},{8,0},{9,11},{1... | collective-permute-start | bytes 589832 | tf_op jit(solution)/shard_map/ppermute | solution.py:408
  42.8 3.7 %collective-permute-done.16.refs_3_ = bf16[128,768]{1,0:T(8,128)(2,1)S(1)} collective-permute-done((bf16[128,768]{1,0:T(8,128)(2,1)S(1)}, bf16[128,768]{1,0:T(8,128)(2,1)S(1)}, u32[]{:S(2)}, u32[]{:S(2)}) %collective-permute-start.16) | collective-permute-done | bytes 196640 | tf_op jit(solution)/shard_map/ppermute | solution.py:408
  46.6 1.9 %collective-permute-done.15.refs_2_ = bf16[128,768]{1,0:T(8,128)(2,1)S(1)} collective-permute-done((bf16[128,768]{1,0:T(8,128)(2,1)S(1)}, bf16[128,768]{1,0:T(8,128)(2,1)S(1)}, u32[]{:S(2)}, u32[]{:S(2)}) %collective-permute-start.15) | collective-permute-done | bytes 196640 | tf_op jit(solution)/shard_map/ppermute | solution.py:408
  48.5 1.7 %collective-permute-start.17 = (bf16[512,768]{1,0:T(8,128)(2,1)S(1)}, bf16[512,768]{1,0:T(8,128)(2,1)S(1)}, u32[]{:S(2)}, u32[]{:S(2)}) collective-permute-start(bf16[512,768]{1,0:T(8,128)(2,1)S(1)} %join.7.near_ref), channel_id=1, source_target_pairs={{0,1},{1,0},{2,3},{3,2},{4,5},{5,4},{6,7},{7,6},{8,9},{9,8},{10,11... | collective-permute-start | bytes 2359304 | tf_op jit(solution)/shard_map/ppermute | solution.py:518
  50.2 1.5 %near.3 = (f32[544,768]{1,0:T(8,128)S(1)}, f32[544,128]{1,0:T(8,128)S(1)}, f32[544,128]{1,0:T(8,128)S(1)}) custom-call(bf16[544,768]{1,0:T(8,128)(2,1)S(1)} %queries.3.refs_4_.query_ref.refs_0_, bf16[512,768]{1,0:T(8,128)(2,1)S(1)} %join.7.near_ref, bf16[512,1024]{1,0:T(8,128)(2,1)S(1)} %get-tuple-element.64.bias_ref.refs_2_, ...), custom_call_target="tpu_custom_call" | custom-call | flops 2000000000 | bytes 5242880 | tf_op jit(solution)/shard_map/near/pallas_call | solution.py:519
  52.1 3.3 %block_and_broadcast.1 = (bf16[256,128]{1,0:T(8,128)(2,1)}, bf16[32,768]{1,0:T(8,128)(2,1)}) custom-call(bf16[544,768]{1,0:T(8,128)(2,1)S(1)} %queries.3.refs_4_.query_ref.refs_0_, bf16[512,768]{1,0:T(8,128)(2,1)S(1)} %collective-permute-done.17.refs_1_, bf16[512,1024]{1,0:T(8,128)(2,1)S(1)} %get-tuple-element.64.bias_ref.refs_2_, ...), custom_call_target="tpu_custom_call" | custom-call | tf_op jit(solution)/shard_map/block_and_broadcast/pallas_call | solution.py:539
  (42 shorter events, 6.5 us)
Async XLA Ops:
  1.8 8.1 %collective-permute-start = (bf16[160,128]{1,0:T(8,128)(2,1)S(1)}, bf16[160,128]{1,0:T(8,128)(2,1)S(1)}, u32[]{:S(2)}, u32[]{:S(2)}) collective-permute-start(bf16[160,128]{1,0:T(8,128)(2,1)S(1)} %get-tuple-element.38), channel_id=1, source_target_pairs={{0,31},{1,2},{2,1},{3,4},{4,3},{5,6},{6,5},{7,8},{8,7},{9,10},{10,... | collective-permute-start | bytes 122888 | tf_op jit(solution)/shard_map/ppermute | solution.py:437
  4.6 5.4 %collective-permute-start.1 = (bf16[160,128]{1,0:T(8,128)(2,1)S(1)}, bf16[160,128]{1,0:T(8,128)(2,1)S(1)}, u32[]{:S(2)}, u32[]{:S(2)}) collective-permute-start(bf16[160,128]{1,0:T(8,128)(2,1)S(1)} %get-tuple-element.39), channel_id=1, source_target_pairs={{0,1},{1,0},{2,3},{3,2},{4,5},{5,4},{6,7},{7,6},{8,9},{9,8},{10,11... | collective-permute-start | bytes 122888 | tf_op jit(solution)/shard_map/ppermute | solution.py:438
  10.0 4.3 %slice-start = ((s8[7077888]{0:T(1024)(128)(4,1)}), s8[4194304]{0:T(1024)(128)(4,1)S(1)}, s32[]{:S(2)}) async-start(s8[7077888]{0:T(1024)(128)(4,1)} %bitcast.2), calls=%async_computation | async-start | bytes 8388608
  10.0 4.3 %slice-start.1 = ((s8[7077888]{0:T(1024)(128)(4,1)}), s8[2883584]{0:T(1024)(128)(4,1)S(1)}, s32[]{:S(2)}) async-start(s8[7077888]{0:T(1024)(128)(4,1)} %bitcast.2), calls=%async_computation.1 | async-start | bytes 5767168
  11.5 4.6 %collective-permute-start.4 = (bf16[32,768]{1,0:T(8,128)(2,1)S(1)}, bf16[32,768]{1,0:T(8,128)(2,1)S(1)}, u32[]{:S(2)}, u32[]{:S(2)}) collective-permute-start(bf16[32,768]{1,0:T(8,128)(2,1)S(1)} %get-tuple-element.51.refs_0_), channel_id=1, source_target_pairs={{0,4},{1,17},{2,6},{3,19},{4,0},{5,21},{6,2},{7,23},{8,12},{9,25},... | collective-permute-start | bytes 147464 | tf_op jit(solution)/shard_map/ppermute | solution.py:408
  12.1 4.7 %collective-permute-start.3 = (bf16[32,768]{1,0:T(8,128)(2,1)S(1)}, bf16[32,768]{1,0:T(8,128)(2,1)S(1)}, u32[]{:S(2)}, u32[]{:S(2)}) collective-permute-start(bf16[32,768]{1,0:T(8,128)(2,1)S(1)} %get-tuple-element.51.refs_0_), channel_id=1, source_target_pairs={{0,6},{1,25},{2,4},{3,27},{4,2},{5,29},{6,0},{7,31},{8,14},{9,17},... | collective-permute-start | bytes 147464 | tf_op jit(solution)/shard_map/ppermute | solution.py:408
  13.0 3.9 %collective-permute-start.2 = (bf16[32,768]{1,0:T(8,128)(2,1)S(1)}, bf16[32,768]{1,0:T(8,128)(2,1)S(1)}, u32[]{:S(2)}, u32[]{:S(2)}) collective-permute-start(bf16[32,768]{1,0:T(8,128)(2,1)S(1)} %get-tuple-element.51.refs_0_), channel_id=1, source_target_pairs={{0,2},{1,9},{2,0},{3,11},{4,6},{5,13},{6,4},{7,15},{8,10},{9,1},{1... | collective-permute-start | bytes 147464 | tf_op jit(solution)/shard_map/ppermute | solution.py:408
  14.2 9.7 %slice-start.2 = ((s8[8388608]{0:T(1024)(128)(4,1)}), s8[4194304]{0:T(1024)(128)(4,1)S(1)}, s32[]{:S(2)}) async-start(s8[8388608]{0:T(1024)(128)(4,1)} %bitcast.4), calls=%async_computation.2 | async-start | bytes 8388608
  14.3 9.7 %slice-start.3 = ((s8[8388608]{0:T(1024)(128)(4,1)}), s8[4194304]{0:T(1024)(128)(4,1)S(1)}, s32[]{:S(2)}) async-start(s8[8388608]{0:T(1024)(128)(4,1)} %bitcast.4), calls=%async_computation.3 | async-start | bytes 8388608
  14.3 9.7 %copy-start.2 = (bf16[128,32]{0,1:T(8,128)(2,1)S(1)}, bf16[128,32]{0,1:T(8,128)(2,1)}, u32[]{:S(2)}) copy-start(bf16[128,32]{0,1:T(8,128)(2,1)} %param.21) | copy-start | bytes 24580
  16.9 9.7 %collective-permute-start.7 = (bf16[128,768]{1,0:T(8,128)(2,1)S(1)}, bf16[128,768]{1,0:T(8,128)(2,1)S(1)}, u32[]{:S(2)}, u32[]{:S(2)}) collective-permute-start(bf16[128,768]{1,0:T(8,128)(2,1)S(1)} %join.4.refs_0_), channel_id=1, source_target_pairs={{0,16},{1,5},{2,18},{3,7},{4,20},{5,1},{6,22},{7,3},{8,24},{9,13},... | collective-permute-start | bytes 589832 | tf_op jit(solution)/shard_map/ppermute | solution.py:408
  17.9 8.7 %collective-permute-start.6 = (bf16[128,768]{1,0:T(8,128)(2,1)S(1)}, bf16[128,768]{1,0:T(8,128)(2,1)S(1)}, u32[]{:S(2)}, u32[]{:S(2)}) collective-permute-start(bf16[128,768]{1,0:T(8,128)(2,1)S(1)} %join.4.refs_0_), channel_id=1, source_target_pairs={{0,24},{1,7},{2,26},{3,5},{4,28},{5,3},{6,30},{7,1},{8,16},{9,15},... | collective-permute-start | bytes 589832 | tf_op jit(solution)/shard_map/ppermute | solution.py:408
  19.7 6.9 %collective-permute-start.5 = (bf16[128,768]{1,0:T(8,128)(2,1)S(1)}, bf16[128,768]{1,0:T(8,128)(2,1)S(1)}, u32[]{:S(2)}, u32[]{:S(2)}) collective-permute-start(bf16[128,768]{1,0:T(8,128)(2,1)S(1)} %join.4.refs_0_), channel_id=1, source_target_pairs={{0,8},{1,3},{2,10},{3,1},{4,12},{5,7},{6,14},{7,5},{8,0},{9,11},{1... | collective-permute-start | bytes 589832 | tf_op jit(solution)/shard_map/ppermute | solution.py:408
  20.2 6.4 %collective-permute-start.8 = (bf16[32,1024]{1,0:T(8,128)(2,1)S(1)}, bf16[32,1024]{1,0:T(8,128)(2,1)S(1)}, u32[]{:S(2)}, u32[]{:S(2)}) collective-permute-start(bf16[32,1024]{1,0:T(8,128)(2,1)S(1)} %get-tuple-element.52), channel_id=1, source_target_pairs={{0,31},{1,2},{2,1},{3,4},{4,3},{5,6},{6,5},{7,8},{8,7},{9,10},{10,... | collective-permute-start | bytes 196616 | tf_op jit(solution)/shard_map/ppermute | solution.py:494
  22.4 4.1 %collective-permute-start.9 = (bf16[32,1024]{1,0:T(8,128)(2,1)S(1)}, bf16[32,1024]{1,0:T(8,128)(2,1)S(1)}, u32[]{:S(2)}, u32[]{:S(2)}) collective-permute-start(bf16[32,1024]{1,0:T(8,128)(2,1)S(1)} %get-tuple-element.53), channel_id=1, source_target_pairs={{0,1},{1,0},{2,3},{3,2},{4,5},{5,4},{6,7},{7,6},{8,9},{9,8},{10,11... | collective-permute-start | bytes 196616 | tf_op jit(solution)/shard_map/ppermute | solution.py:494
  26.7 4.6 %collective-permute-start.10 = (bf16[512,768]{1,0:T(8,128)(2,1)S(1)}, bf16[512,768]{1,0:T(8,128)(2,1)S(1)}, u32[]{:S(2)}, u32[]{:S(2)}) collective-permute-start(bf16[512,768]{1,0:T(8,128)(2,1)S(1)} %get-tuple-element.55.near_ref), channel_id=1, source_target_pairs={{0,1},{1,0},{2,3},{3,2},{4,5},{5,4},{6,7},{7,6},{8,9},{9,8},{10,11... | collective-permute-start | bytes 2359304 | tf_op jit(solution)/shard_map/ppermute | solution.py:518
  29.4 1.9 %copy-start = (bf16[2,768,768]{2,1,0:T(8,128)(2,1)S(1)}, bf16[2,768,768]{2,1,0:T(8,128)(2,1)}, u32[]{:S(2)}) copy-start(bf16[2,768,768]{2,1,0:T(8,128)(2,1)} %refs_9_.3) | copy-start | bytes 7077892
  33.8 4.5 %collective-permute-start.13 = (bf16[32,768]{1,0:T(8,128)(2,1)S(1)}, bf16[32,768]{1,0:T(8,128)(2,1)S(1)}, u32[]{:S(2)}, u32[]{:S(2)}) collective-permute-start(bf16[32,768]{1,0:T(8,128)(2,1)S(1)} %get-tuple-element.63.refs_0_), channel_id=1, source_target_pairs={{0,4},{1,17},{2,6},{3,19},{4,0},{5,21},{6,2},{7,23},{8,12},{9,25},... | collective-permute-start | bytes 147464 | tf_op jit(solution)/shard_map/ppermute | solution.py:408
  35.3 4.4 %collective-permute-start.12 = (bf16[32,768]{1,0:T(8,128)(2,1)S(1)}, bf16[32,768]{1,0:T(8,128)(2,1)S(1)}, u32[]{:S(2)}, u32[]{:S(2)}) collective-permute-start(bf16[32,768]{1,0:T(8,128)(2,1)S(1)} %get-tuple-element.63.refs_0_), channel_id=1, source_target_pairs={{0,6},{1,25},{2,4},{3,27},{4,2},{5,29},{6,0},{7,31},{8,14},{9,17},... | collective-permute-start | bytes 147464 | tf_op jit(solution)/shard_map/ppermute | solution.py:408
  36.9 3.2 %collective-permute-start.11 = (bf16[32,768]{1,0:T(8,128)(2,1)S(1)}, bf16[32,768]{1,0:T(8,128)(2,1)S(1)}, u32[]{:S(2)}, u32[]{:S(2)}) collective-permute-start(bf16[32,768]{1,0:T(8,128)(2,1)S(1)} %get-tuple-element.63.refs_0_), channel_id=1, source_target_pairs={{0,2},{1,9},{2,0},{3,11},{4,6},{5,13},{6,4},{7,15},{8,10},{9,1},{1... | collective-permute-start | bytes 147464 | tf_op jit(solution)/shard_map/ppermute | solution.py:408
  40.1 6.4 %collective-permute-start.16 = (bf16[128,768]{1,0:T(8,128)(2,1)S(1)}, bf16[128,768]{1,0:T(8,128)(2,1)S(1)}, u32[]{:S(2)}, u32[]{:S(2)}) collective-permute-start(bf16[128,768]{1,0:T(8,128)(2,1)S(1)} %join.6.refs_0_), channel_id=1, source_target_pairs={{0,16},{1,5},{2,18},{3,7},{4,20},{5,1},{6,22},{7,3},{8,24},{9,13},... | collective-permute-start | bytes 589832 | tf_op jit(solution)/shard_map/ppermute | solution.py:408
  40.2 8.2 %collective-permute-start.15 = (bf16[128,768]{1,0:T(8,128)(2,1)S(1)}, bf16[128,768]{1,0:T(8,128)(2,1)S(1)}, u32[]{:S(2)}, u32[]{:S(2)}) collective-permute-start(bf16[128,768]{1,0:T(8,128)(2,1)S(1)} %join.6.refs_0_), channel_id=1, source_target_pairs={{0,24},{1,7},{2,26},{3,5},{4,28},{5,3},{6,30},{7,1},{8,16},{9,15},... | collective-permute-start | bytes 589832 | tf_op jit(solution)/shard_map/ppermute | solution.py:408
  41.5 6.9 %collective-permute-start.14 = (bf16[128,768]{1,0:T(8,128)(2,1)S(1)}, bf16[128,768]{1,0:T(8,128)(2,1)S(1)}, u32[]{:S(2)}, u32[]{:S(2)}) collective-permute-start(bf16[128,768]{1,0:T(8,128)(2,1)S(1)} %join.6.refs_0_), channel_id=1, source_target_pairs={{0,8},{1,3},{2,10},{3,1},{4,12},{5,7},{6,14},{7,5},{8,0},{9,11},{1... | collective-permute-start | bytes 589832 | tf_op jit(solution)/shard_map/ppermute | solution.py:408
  48.5 3.6 %collective-permute-start.17 = (bf16[512,768]{1,0:T(8,128)(2,1)S(1)}, bf16[512,768]{1,0:T(8,128)(2,1)S(1)}, u32[]{:S(2)}, u32[]{:S(2)}) collective-permute-start(bf16[512,768]{1,0:T(8,128)(2,1)S(1)} %join.7.near_ref), channel_id=1, source_target_pairs={{0,1},{1,0},{2,3},{3,2},{4,5},{5,4},{6,7},{7,6},{8,9},{9,8},{10,11... | collective-permute-start | bytes 2359304 | tf_op jit(solution)/shard_map/ppermute | solution.py:518
  (1 other events, 1.9 us)

commit v5 on v4

--- a/solution.py
+++ b/solution.py
@@ -294,26 +294,26 @@
     for_neighbours(lax.rem(tok, 2), apart_ref, beside_ref, fill)
 
 
-def join_edges_kernel(*refs):
-    join_kernel(0, *refs[:4], refs[7])
-    both_ref = refs[10]
-    both_ref[0] = refs[4][...]
-    both_ref[1] = refs[5][...]
+def join_edges_kernel(places, *refs):
+    join_kernel(places, *refs[:3], refs[6])
+    both_ref = refs[9]
+    both_ref[0] = refs[3][...]
+    both_ref[1] = refs[4][...]
     core = lax.rem(lax.axis_index("tok"), 2)
-    for block, ref in enumerate(refs[8:10]):
+    for block, ref in enumerate(refs[7:9]):
         for side, index in enumerate((core, 1 - core)):
             ref[side * H : (side + 1) * H] = both_ref[index, block * H : (block + 1) * H]
 
 
-def join_kernel(count, *refs):
+def join_kernel(places, *refs):
     out_ref = refs[-1]
-    rows = out_ref.shape[0] // 4
-    for i, place in enumerate((0, 1, 3, 2)):
+    rows = out_ref.shape[0] // len(places)
+    for i, place in enumerate(places):
         out_ref[place * rows : (place + 1) * rows] = refs[i][...]
 
 
-def scored(query_ref, rows_ref, bias_ref, edge_bias_ref, half):
-    scores = lax.dot_general(query_ref[...], rows_ref[...], NT, preferred_element_type=F32)
+def scored(query_ref, rows, bias_ref, edge_bias_ref, half):
+    scores = lax.dot_general(query_ref[...], rows, NT, preferred_element_type=F32)
     parts = []
     for k in range(HALF // 128):
         lanes = slice(half * HALF + 128 * k, half * HALF + 128 * (k + 1))
@@ -322,29 +322,31 @@
     return parts
 
 
-def weighted(powers, rows_ref):
+def weighted(powers, rows):
     weights = jnp.concatenate([part.astype(BF16) for part in powers], axis=1)
-    return jnp.dot(weights, rows_ref[...], preferred_element_type=F32)
-
-
-def near_kernel(query_ref, near_ref, bias_ref, edge_bias_ref, mixed_ref, maximum_ref, total_ref):
-    scores = scored(query_ref, near_ref, bias_ref, edge_bias_ref, 0)
+    return jnp.dot(weights, rows, preferred_element_type=F32)
+
+
+def near_kernel(query_ref, quad_ref, rest_ref, bias_ref, edge_bias_ref, mixed_ref, maximum_ref, total_ref):
+    rows = jnp.concatenate([quad_ref[...], rest_ref[...]], axis=0)
+    scores = scored(query_ref, rows, bias_ref, edge_bias_ref, 0)
     maximum = along(jnp.max, tree(jnp.maximum, scores))
     powers = [jnp.exp(part - maximum) for part in scores]
     maximum_ref[...] = maximum
     total_ref[...] = tree(jnp.add, powers)
-    mixed_ref[...] = weighted(powers, near_ref)
-
-
-def attend(layer, query_ref, far_ref, bias_ref, edge_bias_ref, mixed_ref, maximum_ref, total_ref, mask_ref,
+    mixed_ref[...] = weighted(powers, rows)
+
+
+def attend(layer, query_ref, quad_ref, rest_ref, bias_ref, edge_bias_ref, mixed_ref, maximum_ref, total_ref, mask_ref,
            qkv_ref, out_w_ref, stream_ref):
-    scores = scored(query_ref, far_ref, bias_ref, edge_bias_ref, 1)
+    rows = jnp.concatenate([quad_ref[...], rest_ref[...]], axis=0)
+    scores = scored(query_ref, rows, bias_ref, edge_bias_ref, 1)
     maximum = jnp.maximum(maximum_ref[...], along(jnp.max, tree(jnp.maximum, scores)))
     powers = [jnp.exp(part - maximum) for part in scores]
     fade = jnp.exp(maximum_ref[...] - maximum)
     share = 1.0 / along(jnp.sum, total_ref[...] * fade + tree(jnp.add, powers))
     fade = fade * share
-    new = weighted(powers, far_ref)
+    new = weighted(powers, rows)
     mixed = jnp.concatenate(
         [
             (mixed_ref[:, 128 * k : 128 * (k + 1)] * fade + new[:, 128 * k : 128 * (k + 1)] * share).astype(BF16)
@@ -361,8 +363,8 @@
 
 
 def middle_kernel(*refs):
-    stream_ref, normed_ref, own_ref = refs[11:]
-    stream = attend(0, *refs[:11])
+    stream_ref, normed_ref, own_ref = refs[12:]
+    stream = attend(0, *refs[:12])
     stream_ref[...] = stream
     out = layer_norm(stream).astype(BF16)
     normed_ref[...] = out
@@ -370,8 +372,8 @@
 
 
 def last_kernel(*refs):
-    bcast_ref, pick_ref, hidden_ref, atom_out_ref, token_out_ref = refs[11:]
-    token_out = attend(1, *refs[:11]).astype(BF16)
+    bcast_ref, pick_ref, hidden_ref, atom_out_ref, token_out_ref = refs[12:]
+    token_out = attend(1, *refs[:12]).astype(BF16)
     token_out_ref[...] = token_out[:TOKD]
     carry = jnp.dot(token_out, bcast_ref[...], preferred_element_type=F32).astype(BF16)
     picked = jnp.dot(pick_ref[:, :ROWS], carry, preferred_element_type=F32)
@@ -393,19 +395,22 @@
     ]
 
 
-def join(pieces, after):
+def join(pieces, places, after=()):
     return pl.pallas_call(
-        functools.partial(join_kernel, len(after)),
-        in_specs=[VMEM] * 4 + [pl.BlockSpec(memory_space=pl.ANY)] * len(after),
+        functools.partial(join_kernel, places),
+        in_specs=[VMEM] * len(pieces) + [pl.BlockSpec(memory_space=pl.ANY)] * len(after),
         out_specs=VMEM,
-        out_shape=shape(4 * pieces[0].shape[0], C),
+        out_shape=shape(len(pieces) * pieces[0].shape[0], C),
         compiler_params=params(4),
         name="join",
     )(*pieces, *after)
 
 
+ORDER = (2, 3, 1)
+
+
 def exchange(rows, first):
-    return [rows] + [lax.ppermute(rows, "tok", crossed(k, first)) for k in (1, 3, 2)]
+    return [lax.ppermute(rows, "tok", crossed(k, first)) for k in ORDER]
 
 
 def in_hbm(*arrays):
@@ -475,7 +480,7 @@
     )(small[0], apart, beside, *small[1:], *inner)
 
     for layer in range(2):
-        pieces = exchange(own, True)
+        pieces = [own] + exchange(own, True)
         if layer == 0:
             queries, *edges = pl.pallas_call(
                 first_query_kernel,
@@ -502,34 +507,37 @@
                 cost_estimate=pl.CostEstimate(flops=10**9, bytes_accessed=5 * 2**20, transcendentals=0),
                 name="queries",
             )(normed, tok_qkv_w)
-        pieces = exchange(join(pieces, [queries]), False)
+        quad = join(pieces, (0, *ORDER), [queries])
+        far_quad = lax.ppermute(quad, "tok", flips(0, 0, 1))
+        pieces = exchange(quad, False)
+        places = tuple(k - 1 for k in ORDER)
         if layer == 0:
-            near, *edge_bias = pl.pallas_call(
-                join_edges_kernel,
-                in_specs=[VMEM] * 6 + [pl.BlockSpec(memory_space=pl.ANY)],
+            rest, *edge_bias = pl.pallas_call(
+                functools.partial(join_edges_kernel, places),
+                in_specs=[VMEM] * 5 + [pl.BlockSpec(memory_space=pl.ANY)],
                 out_specs=[VMEM] * 3,
-                out_shape=[shape(HALF, C)] + [shape(2 * H, KEYS)] * 2,
+                out_shape=[shape(HALF * 3 // 4, C)] + [shape(2 * H, KEYS)] * 2,
                 scratch_shapes=[pltpu.VMEM((2, NB * H, KEYS), BF16)],
                 compiler_params=params(8),
                 name="join",
             )(*pieces, *edges, bias[0])
         else:
-            near = join(pieces, [])
-        far = lax.ppermute(near, "tok", flips(0, 0, 1))
+            rest = join(pieces, places, [far_quad])
+        far_rest = lax.ppermute(rest, "tok", flips(0, 0, 1))
         partial = pl.pallas_call(
             near_kernel,
-            in_specs=[VMEM] * 4,
+            in_specs=[VMEM] * 5,
             out_specs=[VMEM] * 3,
             out_shape=[shape(QROWS, C, F32)] + [shape(QROWS, 128, F32)] * 2,
             compiler_params=params(16),
             cost_estimate=pl.CostEstimate(flops=2 * 10**9, bytes_accessed=5 * 2**20, transcendentals=300000),
             name="near",
-        )(queries, near, bias[layer], edge_bias[layer])
-        operands = (queries, far, bias[layer], edge_bias[layer], *partial, mask, tok_qkv_w, tok_out_w, stream)
+        )(queries, quad, rest, bias[layer], edge_bias[layer])
+        operands = (queries, far_quad, far_rest, bias[layer], edge_bias[layer], *partial, mask, tok_qkv_w, tok_out_w, stream)
         if layer == 0:
             stream, normed, own = pl.pallas_call(
                 middle_kernel,
-                in_specs=[VMEM] * 11,
+                in_specs=[VMEM] * 12,
                 out_specs=[VMEM] * 3,
                 out_shape=[shape(ROWS, C, F32), shape(ROWS, C), shape(TOKD, C)],
                 compiler_params=params(16),
@@ -538,7 +546,7 @@
         else:
             atom_out, token_out = pl.pallas_call(
                 last_kernel,
-                in_specs=[VMEM] * 14,
+                in_specs=[VMEM] * 15,
                 out_specs=[VMEM] * 2,
                 out_shape=[shape(ATOMD, CA), shape(TOKD, C)],
                 compiler_params=params(16),

time: 55.5 us -> 55.1 us (level)
  starting transfers between devices: 26.1 us -> 25.5 us
    ppermute x1, starting transfers between devices: 2.26 us -> 1.2 us  [local(): lax.ppermute(edges[0], 'tok', across)]
    ppermute x14 -> x16, starting transfers between devices: 16.1 us -> 17 us  [the longest x12 12.4 us: exchange(): return [lax.ppermute(rows, 'tok', crossed(k, first)) for k in ORDER]]
    ppermute x1, waiting for transfers between devices: 0.01 us -> 0.88 us  [local(): lax.ppermute(edges[0], 'tok', across)]
    ppermute x14 -> x16, waiting for transfers between devices: 8.95 us -> 8.29 us  [the longest x12 8.01 us: exchange(): return [lax.ppermute(rows, 'tok', crossed(k, first)) for k in ORDER]]
  transfers between devices with their start and end apart: 18 -> 20, of which waited for: 8 -> 10; matrix products, arithmetic and copies ran while one was open for 0% -> 0% of each run, Pallas kernels for 19% -> 20%
where the time goes in v5:
time: 55.1 us; the launch traced here: 55 us
  starting transfers between devices  25.5 us (46%)
  Pallas kernels  19.4 us (35%)
  waiting for transfers between devices  9.18 us (17%)
  between operations  0.8 us (1%)
    ppermute x12, starting transfers between devices, exchange(): return [lax.ppermute(rows, 'tok', crossed(k, first)) for k in ORDER]  12.4 us
    ppermute x12, waiting for transfers between devices, exchange(): return [lax.ppermute(rows, 'tok', crossed(k, first)) for k in ORDER]  8.01 us
    ppermute x2, starting transfers between devices, local(): far_rest = lax.ppermute(rest, 'tok', flips(0, 0, 1))  3.74 us
    ppermute x1, starting transfers between devices, local(): beside = lax.ppermute(to_beside, 'tok', flips(0, 0, 1))  3.47 us
    pallas_call x1, Pallas kernels, local(): pl.pallas_call(last_kernel, in_specs=[VMEM] * 15, out_specs=[VMEM] * 2, o...  3.27 us
    pallas_call x2, Pallas kernels, local(): pl.pallas_call(near_kernel, in_specs=[VMEM] * 5, out_specs=[VMEM] * 3, ou...  2.98 us
    ppermute x1, starting transfers between devices, local(): apart = lax.ppermute(to_apart, 'tok', across)  2.77 us
    pallas_call x1, Pallas kernels, local(): pl.pallas_call(bias_kernel, in_specs=[VMEM] * 2, out_specs=[VMEM] * 2, ou...  2.64 us
  transfers between devices with their start and end apart: 20, of which 10 were waited for; matrix products, arithmetic and copies ran while one was open for 0% of the time, Pallas kernels for 20%

profile of v5, /device:TPU:1, one launch (start us, length us, event | category | flops | bytes accessed | tf_op | source)
XLA Modules:
  0.0 55.0 jit_solution(12464172670115538421)
XLA Ops:
  0.6 1.2 %pack.1 = (bf16[160,128]{1,0:T(8,128)(2,1)S(1)}, bf16[160,128]{1,0:T(8,128)(2,1)S(1)}, bf16[256,128]{1,0:T(8,128)(2,1)S(1)}, bf16[256,512]{1,0:T(8,128)(2,1)S(1)...) custom-call(bf16[256,128]{1,0:T(8,128)(2,1)} %refs_0_.1, ...), custom_call_target="tpu_custom_call" | custom-call | flops 4000000000 | bytes 16777216 | tf_op jit(solution)/shard_map/pack/pallas_call | solution.py:431
  1.8 2.8 %collective-permute-start = (bf16[160,128]{1,0:T(8,128)(2,1)S(1)}, bf16[160,128]{1,0:T(8,128)(2,1)S(1)}, u32[]{:S(2)}, u32[]{:S(2)}) collective-permute-start(bf16[160,128]{1,0:T(8,128)(2,1)S(1)} %get-tuple-element.38), channel_id=1, source_target_pairs={{0,31},{1,2},{2,1},{3,4},{4,3},{5,6},{6,5},{7,8},{8,7},{9,10},{10,... | collective-permute-start | bytes 122888 | tf_op jit(solution)/shard_map/ppermute | solution.py:442
  4.6 3.5 %collective-permute-start.1 = (bf16[160,128]{1,0:T(8,128)(2,1)S(1)}, bf16[160,128]{1,0:T(8,128)(2,1)S(1)}, u32[]{:S(2)}, u32[]{:S(2)}) collective-permute-start(bf16[160,128]{1,0:T(8,128)(2,1)S(1)} %get-tuple-element.39), channel_id=1, source_target_pairs={{0,1},{1,0},{2,3},{3,2},{4,5},{5,4},{6,7},{7,6},{8,9},{9,8},{10,11... | collective-permute-start | bytes 122888 | tf_op jit(solution)/shard_map/ppermute | solution.py:443
  8.1 1.9 %inner_atoms.1 = (bf16[256,384]{1,0:T(8,128)(2,1)S(1)}, bf16[128,128]{1,0:T(8,128)(2,1)S(1)}, f32[48,768]{1,0:T(8,128)S(1)}, f32[48,128]{1,0:T(8,128)S(1)}, bf16...) custom-call(bf16[256,128]{1,0:T(8,128)(2,1)S(1)} %get-tuple-element.37.single_ref, ...), custom_call_target="tpu_custom_call" | custom-call | flops 4000000000 | bytes 16777216 | tf_op jit(solution)/shard_map/inner_atoms/pallas_call | solution.py:455
  10.0 1.5 %atoms.1 = (bf16[256,128]{1,0:T(8,128)(2,1)S(1)}, f32[48,768]{1,0:T(8,128)S(1)}, bf16[48,768]{1,0:T(8,128)(2,1)S(1)}, bf16[32,768]{1,0:T(8,128)(2,1)S(1)}) custom-call(bf16[256,128]{1,0:T(8,128)(2,1)S(1)} %get-tuple-element.37.single_ref, bf16[160,128]{1,0:T(8,128)(2,1)S(1)} %collective-permute-done.apart_ref, ...), custom_call_target="tpu_custom_call" | custom-call | flops 4000000000 | bytes 16777216 | tf_op jit(solution)/shard_map/atoms/pallas_call | solution.py:471
  13.0 1.3 %collective-permute-start.4 = (bf16[32,768]{1,0:T(8,128)(2,1)S(1)}, bf16[32,768]{1,0:T(8,128)(2,1)S(1)}, u32[]{:S(2)}, u32[]{:S(2)}) collective-permute-start(bf16[32,768]{1,0:T(8,128)(2,1)S(1)} %get-tuple-element.51.refs_0_), channel_id=1, source_target_pairs={{0,2},{1,9},{2,0},{3,11},{4,6},{5,13},{6,4},{7,15},{8,10},{9,1},{1... | collective-permute-start | bytes 147464 | tf_op jit(solution)/shard_map/ppermute | solution.py:413
  14.3 1.9 %queries.2 = (bf16[544,768]{1,0:T(8,128)(2,1)S(1)}, bf16[32,1024]{1,0:T(8,128)(2,1)S(1)}, bf16[32,1024]{1,0:T(8,128)(2,1)S(1)}) custom-call(bf16[48,768]{1,0:T(8,128)(2,1)S(1)} %get-tuple-element.49.normed_ref, bf16[2,768,2304]{2,1,0:T(8,128)(2,1)S(1)} %bitcast.3, bf16[32,1024,128]{2,1,0:T(8,128)(2,1)} %pair_ref.1, bf16[32,128]{1,0:T(8,128)(2,1)} %bitcast.6), custom_call_target="tpu_custom_call" | custom-call | flops 1000000000 | bytes 5242880 | tf_op jit(solution)/shard_map/queries/pallas_call | solution.py:485
  16.9 1.1 %collective-permute-start.6 = (bf16[128,768]{1,0:T(8,128)(2,1)S(1)}, bf16[128,768]{1,0:T(8,128)(2,1)S(1)}, u32[]{:S(2)}, u32[]{:S(2)}) collective-permute-start(bf16[128,768]{1,0:T(8,128)(2,1)S(1)} %join.4.quad_ref), channel_id=1, source_target_pairs={{0,16},{1,5},{2,18},{3,7},{4,20},{5,1},{6,22},{7,3},{8,24},{9,13},... | collective-permute-start | bytes 589832 | tf_op jit(solution)/shard_map/ppermute | solution.py:413
  17.9 1.7 %collective-permute-start.7 = (bf16[128,768]{1,0:T(8,128)(2,1)S(1)}, bf16[128,768]{1,0:T(8,128)(2,1)S(1)}, u32[]{:S(2)}, u32[]{:S(2)}) collective-permute-start(bf16[128,768]{1,0:T(8,128)(2,1)S(1)} %join.4.quad_ref), channel_id=1, source_target_pairs={{0,24},{1,7},{2,26},{3,5},{4,28},{5,3},{6,30},{7,1},{8,16},{9,15},... | collective-permute-start | bytes 589832 | tf_op jit(solution)/shard_map/ppermute | solution.py:413
  21.2 1.2 %collective-permute-start.9 = (bf16[32,1024]{1,0:T(8,128)(2,1)S(1)}, bf16[32,1024]{1,0:T(8,128)(2,1)S(1)}, u32[]{:S(2)}, u32[]{:S(2)}) collective-permute-start(bf16[32,1024]{1,0:T(8,128)(2,1)S(1)} %get-tuple-element.52), channel_id=1, source_target_pairs={{0,31},{1,2},{2,1},{3,4},{4,3},{5,6},{6,5},{7,8},{8,7},{9,10},{10,... | collective-permute-start | bytes 196616 | tf_op jit(solution)/shard_map/ppermute | solution.py:499
  22.5 2.6 %bias.1 = (bf16[512,1024]{1,0:T(8,128)(2,1)S(1)}, bf16[512,1024]{1,0:T(8,128)(2,1)S(1)}) custom-call(bf16[32,1024,128]{2,1,0:T(8,128)(2,1)S(1)} %bitcast.5, bf16[32,128]{1,0:T(8,128)(2,1)S(1)} %bitcast.7), custom_call_target="tpu_custom_call" | custom-call | flops 268435456 | bytes 10485760 | tf_op jit(solution)/shard_map/bias/pallas_call | solution.py:445
  26.4 2.7 %collective-permute-start.11 = (bf16[384,768]{1,0:T(8,128)(2,1)S(1)}, bf16[384,768]{1,0:T(8,128)(2,1)S(1)}, u32[]{:S(2)}, u32[]{:S(2)}) collective-permute-start(bf16[384,768]{1,0:T(8,128)(2,1)S(1)} %get-tuple-element.55.rest_ref), channel_id=1, source_target_pairs={{0,1},{1,0},{2,3},{3,2},{4,5},{5,4},{6,7},{7,6},{8,9},{9,8},{10,11... | collective-permute-start | bytes 1769480 | tf_op jit(solution)/shard_map/ppermute | solution.py:526
  29.4 1.5 %near.2 = (f32[544,768]{1,0:T(8,128)S(1)}, f32[544,128]{1,0:T(8,128)S(1)}, f32[544,128]{1,0:T(8,128)S(1)}) custom-call(bf16[544,768]{1,0:T(8,128)(2,1)S(1)} %get-tuple-element.50.refs_4_.query_ref.refs_0_, bf16[128,768]{1,0:T(8,128)(2,1)S(1)} %join.4.quad_ref, bf16[384,768]{1,0:T(8,128)(2,1)S(1)} %get-tuple-element.55.rest_ref, ...), custom_call_target="tpu_custom_call" | custom-call | flops 2000000000 | bytes 5242880 | tf_op jit(solution)/shard_map/near/pallas_call | solution.py:527
  31.1 2.6 %block.1 = (f32[48,768]{1,0:T(8,128)S(1)}, bf16[48,768]{1,0:T(8,128)(2,1)S(1)}, bf16[32,768]{1,0:T(8,128)(2,1)S(1)}) custom-call(bf16[544,768]{1,0:T(8,128)(2,1)S(1)} %get-tuple-element.50.refs_4_.query_ref.refs_0_, bf16[128,768]{1,0:T(8,128)(2,1)S(1)} %collective-permute-done.5.refs_1_, bf16[384,768]{1,0:T(8,128)(2,1)S(1)} %collective-permute-done.11.refs_2_, ...), custom_call_target="tpu_custom_call" | custom-call | tf_op jit(solution)/shard_map/block/pallas_call | solution.py:538
  33.7 1.4 %collective-permute-start.12 = (bf16[32,768]{1,0:T(8,128)(2,1)S(1)}, bf16[32,768]{1,0:T(8,128)(2,1)S(1)}, u32[]{:S(2)}, u32[]{:S(2)}) collective-permute-start(bf16[32,768]{1,0:T(8,128)(2,1)S(1)} %get-tuple-element.63.refs_0_), channel_id=1, source_target_pairs={{0,4},{1,17},{2,6},{3,19},{4,0},{5,21},{6,2},{7,23},{8,12},{9,25},... | collective-permute-start | bytes 147464 | tf_op jit(solution)/shard_map/ppermute | solution.py:413
  35.1 1.6 %collective-permute-start.13 = (bf16[32,768]{1,0:T(8,128)(2,1)S(1)}, bf16[32,768]{1,0:T(8,128)(2,1)S(1)}, u32[]{:S(2)}, u32[]{:S(2)}) collective-permute-start(bf16[32,768]{1,0:T(8,128)(2,1)S(1)} %get-tuple-element.63.refs_0_), channel_id=1, source_target_pairs={{0,6},{1,25},{2,4},{3,27},{4,2},{5,29},{6,0},{7,31},{8,14},{9,17},... | collective-permute-start | bytes 147464 | tf_op jit(solution)/shard_map/ppermute | solution.py:413
  36.7 1.4 %queries.3.refs_4_.query_ref.refs_0_ = bf16[544,768]{1,0:T(8,128)(2,1)S(1)} custom-call(bf16[48,768]{1,0:T(8,128)(2,1)S(1)} %get-tuple-element.62.normed_ref, bf16[2,768,2304]{2,1,0:T(8,128)(2,1)S(1)} %bitcast.3), custom_call_target="tpu_custom_call" | custom-call | flops 1000000000 | bytes 5242880 | tf_op jit(solution)/shard_map/queries/pallas_call | solution.py:501
  38.2 1.4 %collective-permute-done.13.refs_2_ = bf16[32,768]{1,0:T(8,128)(2,1)S(1)} collective-permute-done((bf16[32,768]{1,0:T(8,128)(2,1)S(1)}, bf16[32,768]{1,0:T(8,128)(2,1)S(1)}, u32[]{:S(2)}, u32[]{:S(2)}) %collective-permute-start.13) | collective-permute-done | bytes 49184 | tf_op jit(solution)/shard_map/ppermute | solution.py:413
  40.6 1.1 %collective-permute-start.16 = (bf16[128,768]{1,0:T(8,128)(2,1)S(1)}, bf16[128,768]{1,0:T(8,128)(2,1)S(1)}, u32[]{:S(2)}, u32[]{:S(2)}) collective-permute-start(bf16[128,768]{1,0:T(8,128)(2,1)S(1)} %join.6.quad_ref), channel_id=1, source_target_pairs={{0,16},{1,5},{2,18},{3,7},{4,20},{5,1},{6,22},{7,3},{8,24},{9,13},... | collective-permute-start | bytes 589832 | tf_op jit(solution)/shard_map/ppermute | solution.py:413
  41.7 2.2 %collective-permute-start.17 = (bf16[128,768]{1,0:T(8,128)(2,1)S(1)}, bf16[128,768]{1,0:T(8,128)(2,1)S(1)}, u32[]{:S(2)}, u32[]{:S(2)}) collective-permute-start(bf16[128,768]{1,0:T(8,128)(2,1)S(1)} %join.6.quad_ref), channel_id=1, source_target_pairs={{0,24},{1,7},{2,26},{3,5},{4,28},{5,3},{6,30},{7,1},{8,16},{9,15},... | collective-permute-start | bytes 589832 | tf_op jit(solution)/shard_map/ppermute | solution.py:413
  43.9 3.0 %collective-permute-done.16.refs_0_ = bf16[128,768]{1,0:T(8,128)(2,1)S(1)} collective-permute-done((bf16[128,768]{1,0:T(8,128)(2,1)S(1)}, bf16[128,768]{1,0:T(8,128)(2,1)S(1)}, u32[]{:S(2)}, u32[]{:S(2)}) %collective-permute-start.16) | collective-permute-done | bytes 196640 | tf_op jit(solution)/shard_map/ppermute | solution.py:413
  46.9 2.1 %collective-permute-done.17.refs_1_ = bf16[128,768]{1,0:T(8,128)(2,1)S(1)} collective-permute-done((bf16[128,768]{1,0:T(8,128)(2,1)S(1)}, bf16[128,768]{1,0:T(8,128)(2,1)S(1)}, u32[]{:S(2)}, u32[]{:S(2)}) %collective-permute-start.17) | collective-permute-done | bytes 196640 | tf_op jit(solution)/shard_map/ppermute | solution.py:413
  50.1 1.5 %near.3 = (f32[544,768]{1,0:T(8,128)S(1)}, f32[544,128]{1,0:T(8,128)S(1)}, f32[544,128]{1,0:T(8,128)S(1)}) custom-call(bf16[544,768]{1,0:T(8,128)(2,1)S(1)} %queries.3.refs_4_.query_ref.refs_0_, bf16[128,768]{1,0:T(8,128)(2,1)S(1)} %join.6.quad_ref, bf16[384,768]{1,0:T(8,128)(2,1)S(1)} %join.7.rest_ref, ...), custom_call_target="tpu_custom_call" | custom-call | flops 2000000000 | bytes 5242880 | tf_op jit(solution)/shard_map/near/pallas_call | solution.py:527
  51.7 3.3 %block_and_broadcast.1 = (bf16[256,128]{1,0:T(8,128)(2,1)}, bf16[32,768]{1,0:T(8,128)(2,1)}) custom-call(bf16[544,768]{1,0:T(8,128)(2,1)S(1)} %queries.3.refs_4_.query_ref.refs_0_, bf16[128,768]{1,0:T(8,128)(2,1)S(1)} %collective-permute-done.15.refs_3_.refs_1_, bf16[384,768]{1,0:T(8,128)(2,1)S(1)} %collective-permute-done.19.refs_2_, ...), custom_call_target="tpu_custom_call" | custom-call | tf_op jit(solution)/shard_map/block_and_broadcast/pallas_call | solution.py:547
  (46 shorter events, 7.8 us)
Async XLA Ops:
  1.8 8.1 %collective-permute-start = (bf16[160,128]{1,0:T(8,128)(2,1)S(1)}, bf16[160,128]{1,0:T(8,128)(2,1)S(1)}, u32[]{:S(2)}, u32[]{:S(2)}) collective-permute-start(bf16[160,128]{1,0:T(8,128)(2,1)S(1)} %get-tuple-element.38), channel_id=1, source_target_pairs={{0,31},{1,2},{2,1},{3,4},{4,3},{5,6},{6,5},{7,8},{8,7},{9,10},{10,... | collective-permute-start | bytes 122888 | tf_op jit(solution)/shard_map/ppermute | solution.py:442
  4.6 5.4 %collective-permute-start.1 = (bf16[160,128]{1,0:T(8,128)(2,1)S(1)}, bf16[160,128]{1,0:T(8,128)(2,1)S(1)}, u32[]{:S(2)}, u32[]{:S(2)}) collective-permute-start(bf16[160,128]{1,0:T(8,128)(2,1)S(1)} %get-tuple-element.39), channel_id=1, source_target_pairs={{0,1},{1,0},{2,3},{3,2},{4,5},{5,4},{6,7},{7,6},{8,9},{9,8},{10,11... | collective-permute-start | bytes 122888 | tf_op jit(solution)/shard_map/ppermute | solution.py:443
  10.0 4.3 %slice-start = ((s8[7077888]{0:T(1024)(128)(4,1)}), s8[4194304]{0:T(1024)(128)(4,1)S(1)}, s32[]{:S(2)}) async-start(s8[7077888]{0:T(1024)(128)(4,1)} %bitcast.2), calls=%async_computation | async-start | bytes 8388608
  11.5 4.7 %collective-permute-start.2 = (bf16[32,768]{1,0:T(8,128)(2,1)S(1)}, bf16[32,768]{1,0:T(8,128)(2,1)S(1)}, u32[]{:S(2)}, u32[]{:S(2)}) collective-permute-start(bf16[32,768]{1,0:T(8,128)(2,1)S(1)} %get-tuple-element.51.refs_0_), channel_id=1, source_target_pairs={{0,4},{1,17},{2,6},{3,19},{4,0},{5,21},{6,2},{7,23},{8,12},{9,25},... | collective-permute-start | bytes 147464 | tf_op jit(solution)/shard_map/ppermute | solution.py:413
  12.1 4.7 %collective-permute-start.3 = (bf16[32,768]{1,0:T(8,128)(2,1)S(1)}, bf16[32,768]{1,0:T(8,128)(2,1)S(1)}, u32[]{:S(2)}, u32[]{:S(2)}) collective-permute-start(bf16[32,768]{1,0:T(8,128)(2,1)S(1)} %get-tuple-element.51.refs_0_), channel_id=1, source_target_pairs={{0,6},{1,25},{2,4},{3,27},{4,2},{5,29},{6,0},{7,31},{8,14},{9,17},... | collective-permute-start | bytes 147464 | tf_op jit(solution)/shard_map/ppermute | solution.py:413
  13.0 3.9 %collective-permute-start.4 = (bf16[32,768]{1,0:T(8,128)(2,1)S(1)}, bf16[32,768]{1,0:T(8,128)(2,1)S(1)}, u32[]{:S(2)}, u32[]{:S(2)}) collective-permute-start(bf16[32,768]{1,0:T(8,128)(2,1)S(1)} %get-tuple-element.51.refs_0_), channel_id=1, source_target_pairs={{0,2},{1,9},{2,0},{3,11},{4,6},{5,13},{6,4},{7,15},{8,10},{9,1},{1... | collective-permute-start | bytes 147464 | tf_op jit(solution)/shard_map/ppermute | solution.py:413
  14.2 8.2 %slice-start.2 = ((s8[8388608]{0:T(1024)(128)(4,1)}), s8[4194304]{0:T(1024)(128)(4,1)S(1)}, s32[]{:S(2)}) async-start(s8[8388608]{0:T(1024)(128)(4,1)} %bitcast.4), calls=%async_computation.2 | async-start | bytes 8388608
  14.3 8.2 %slice-start.3 = ((s8[8388608]{0:T(1024)(128)(4,1)}), s8[4194304]{0:T(1024)(128)(4,1)S(1)}, s32[]{:S(2)}) async-start(s8[8388608]{0:T(1024)(128)(4,1)} %bitcast.4), calls=%async_computation.3 | async-start | bytes 8388608
  14.3 8.2 %copy-start.2 = (bf16[128,32]{0,1:T(8,128)(2,1)S(1)}, bf16[128,32]{0,1:T(8,128)(2,1)}, u32[]{:S(2)}) copy-start(bf16[128,32]{0,1:T(8,128)(2,1)} %param.21) | copy-start | bytes 24580
  16.9 9.1 %collective-permute-start.6 = (bf16[128,768]{1,0:T(8,128)(2,1)S(1)}, bf16[128,768]{1,0:T(8,128)(2,1)S(1)}, u32[]{:S(2)}, u32[]{:S(2)}) collective-permute-start(bf16[128,768]{1,0:T(8,128)(2,1)S(1)} %join.4.quad_ref), channel_id=1, source_target_pairs={{0,16},{1,5},{2,18},{3,7},{4,20},{5,1},{6,22},{7,3},{8,24},{9,13},... | collective-permute-start | bytes 589832 | tf_op jit(solution)/shard_map/ppermute | solution.py:413
  17.9 8.1 %collective-permute-start.7 = (bf16[128,768]{1,0:T(8,128)(2,1)S(1)}, bf16[128,768]{1,0:T(8,128)(2,1)S(1)}, u32[]{:S(2)}, u32[]{:S(2)}) collective-permute-start(bf16[128,768]{1,0:T(8,128)(2,1)S(1)} %join.4.quad_ref), channel_id=1, source_target_pairs={{0,24},{1,7},{2,26},{3,5},{4,28},{5,3},{6,30},{7,1},{8,16},{9,15},... | collective-permute-start | bytes 589832 | tf_op jit(solution)/shard_map/ppermute | solution.py:413
  19.7 6.7 %collective-permute-start.8 = (bf16[128,768]{1,0:T(8,128)(2,1)S(1)}, bf16[128,768]{1,0:T(8,128)(2,1)S(1)}, u32[]{:S(2)}, u32[]{:S(2)}) collective-permute-start(bf16[128,768]{1,0:T(8,128)(2,1)S(1)} %join.4.quad_ref), channel_id=1, source_target_pairs={{0,8},{1,3},{2,10},{3,1},{4,12},{5,7},{6,14},{7,5},{8,0},{9,11},{1... | collective-permute-start | bytes 589832 | tf_op jit(solution)/shard_map/ppermute | solution.py:413
  20.2 4.9 %collective-permute-start.10 = (bf16[32,1024]{1,0:T(8,128)(2,1)S(1)}, bf16[32,1024]{1,0:T(8,128)(2,1)S(1)}, u32[]{:S(2)}, u32[]{:S(2)}) collective-permute-start(bf16[32,1024]{1,0:T(8,128)(2,1)S(1)} %get-tuple-element.53), channel_id=1, source_target_pairs={{0,1},{1,0},{2,3},{3,2},{4,5},{5,4},{6,7},{7,6},{8,9},{9,8},{10,11... | collective-permute-start | bytes 196616 | tf_op jit(solution)/shard_map/ppermute | solution.py:499
  21.2 4.8 %collective-permute-start.9 = (bf16[32,1024]{1,0:T(8,128)(2,1)S(1)}, bf16[32,1024]{1,0:T(8,128)(2,1)S(1)}, u32[]{:S(2)}, u32[]{:S(2)}) collective-permute-start(bf16[32,1024]{1,0:T(8,128)(2,1)S(1)} %get-tuple-element.52), channel_id=1, source_target_pairs={{0,31},{1,2},{2,1},{3,4},{4,3},{5,6},{6,5},{7,8},{8,7},{9,10},{10,... | collective-permute-start | bytes 196616 | tf_op jit(solution)/shard_map/ppermute | solution.py:499
  26.4 4.6 %collective-permute-start.11 = (bf16[384,768]{1,0:T(8,128)(2,1)S(1)}, bf16[384,768]{1,0:T(8,128)(2,1)S(1)}, u32[]{:S(2)}, u32[]{:S(2)}) collective-permute-start(bf16[384,768]{1,0:T(8,128)(2,1)S(1)} %get-tuple-element.55.rest_ref), channel_id=1, source_target_pairs={{0,1},{1,0},{2,3},{3,2},{4,5},{5,4},{6,7},{7,6},{8,9},{9,8},{10,11... | collective-permute-start | bytes 1769480 | tf_op jit(solution)/shard_map/ppermute | solution.py:526
  29.2 1.9 %collective-permute-start.5 = (bf16[128,768]{1,0:T(8,128)(2,1)S(1)}, bf16[128,768]{1,0:T(8,128)(2,1)S(1)}, u32[]{:S(2)}, u32[]{:S(2)}) collective-permute-start(bf16[128,768]{1,0:T(8,128)(2,1)S(1)} %join.4.quad_ref), channel_id=1, source_target_pairs={{0,1},{1,0},{2,3},{3,2},{4,5},{5,4},{6,7},{7,6},{8,9},{9,8},{10,11... | collective-permute-start | bytes 589832 | tf_op jit(solution)/shard_map/ppermute | solution.py:511
  33.7 4.5 %collective-permute-start.12 = (bf16[32,768]{1,0:T(8,128)(2,1)S(1)}, bf16[32,768]{1,0:T(8,128)(2,1)S(1)}, u32[]{:S(2)}, u32[]{:S(2)}) collective-permute-start(bf16[32,768]{1,0:T(8,128)(2,1)S(1)} %get-tuple-element.63.refs_0_), channel_id=1, source_target_pairs={{0,4},{1,17},{2,6},{3,19},{4,0},{5,21},{6,2},{7,23},{8,12},{9,25},... | collective-permute-start | bytes 147464 | tf_op jit(solution)/shard_map/ppermute | solution.py:413
  35.1 4.4 %collective-permute-start.13 = (bf16[32,768]{1,0:T(8,128)(2,1)S(1)}, bf16[32,768]{1,0:T(8,128)(2,1)S(1)}, u32[]{:S(2)}, u32[]{:S(2)}) collective-permute-start(bf16[32,768]{1,0:T(8,128)(2,1)S(1)} %get-tuple-element.63.refs_0_), channel_id=1, source_target_pairs={{0,6},{1,25},{2,4},{3,27},{4,2},{5,29},{6,0},{7,31},{8,14},{9,17},... | collective-permute-start | bytes 147464 | tf_op jit(solution)/shard_map/ppermute | solution.py:413
  36.7 3.2 %collective-permute-start.14 = (bf16[32,768]{1,0:T(8,128)(2,1)S(1)}, bf16[32,768]{1,0:T(8,128)(2,1)S(1)}, u32[]{:S(2)}, u32[]{:S(2)}) collective-permute-start(bf16[32,768]{1,0:T(8,128)(2,1)S(1)} %get-tuple-element.63.refs_0_), channel_id=1, source_target_pairs={{0,2},{1,9},{2,0},{3,11},{4,6},{5,13},{6,4},{7,15},{8,10},{9,1},{1... | collective-permute-start | bytes 147464 | tf_op jit(solution)/shard_map/ppermute | solution.py:413
  39.9 3.9 %collective-permute-start.15 = (bf16[128,768]{1,0:T(8,128)(2,1)S(1)}, bf16[128,768]{1,0:T(8,128)(2,1)S(1)}, u32[]{:S(2)}, u32[]{:S(2)}) collective-permute-start(bf16[128,768]{1,0:T(8,128)(2,1)S(1)} %join.6.quad_ref), channel_id=1, source_target_pairs={{0,1},{1,0},{2,3},{3,2},{4,5},{5,4},{6,7},{7,6},{8,9},{9,8},{10,11... | collective-permute-start | bytes 589832 | tf_op jit(solution)/shard_map/ppermute | solution.py:511
  40.6 6.3 %collective-permute-start.16 = (bf16[128,768]{1,0:T(8,128)(2,1)S(1)}, bf16[128,768]{1,0:T(8,128)(2,1)S(1)}, u32[]{:S(2)}, u32[]{:S(2)}) collective-permute-start(bf16[128,768]{1,0:T(8,128)(2,1)S(1)} %join.6.quad_ref), channel_id=1, source_target_pairs={{0,16},{1,5},{2,18},{3,7},{4,20},{5,1},{6,22},{7,3},{8,24},{9,13},... | collective-permute-start | bytes 589832 | tf_op jit(solution)/shard_map/ppermute | solution.py:413
  41.7 7.3 %collective-permute-start.17 = (bf16[128,768]{1,0:T(8,128)(2,1)S(1)}, bf16[128,768]{1,0:T(8,128)(2,1)S(1)}, u32[]{:S(2)}, u32[]{:S(2)}) collective-permute-start(bf16[128,768]{1,0:T(8,128)(2,1)S(1)} %join.6.quad_ref), channel_id=1, source_target_pairs={{0,24},{1,7},{2,26},{3,5},{4,28},{5,3},{6,30},{7,1},{8,16},{9,15},... | collective-permute-start | bytes 589832 | tf_op jit(solution)/shard_map/ppermute | solution.py:413
  43.9 5.1 %collective-permute-start.18 = (bf16[128,768]{1,0:T(8,128)(2,1)S(1)}, bf16[128,768]{1,0:T(8,128)(2,1)S(1)}, u32[]{:S(2)}, u32[]{:S(2)}) collective-permute-start(bf16[128,768]{1,0:T(8,128)(2,1)S(1)} %join.6.quad_ref), channel_id=1, source_target_pairs={{0,8},{1,3},{2,10},{3,1},{4,12},{5,7},{6,14},{7,5},{8,0},{9,11},{1... | collective-permute-start | bytes 589832 | tf_op jit(solution)/shard_map/ppermute | solution.py:413
  49.0 2.7 %collective-permute-start.19 = (bf16[384,768]{1,0:T(8,128)(2,1)S(1)}, bf16[384,768]{1,0:T(8,128)(2,1)S(1)}, u32[]{:S(2)}, u32[]{:S(2)}) collective-permute-start(bf16[384,768]{1,0:T(8,128)(2,1)S(1)} %join.7.rest_ref), channel_id=1, source_target_pairs={{0,1},{1,0},{2,3},{3,2},{4,5},{5,4},{6,7},{7,6},{8,9},{9,8},{10,11... | collective-permute-start | bytes 1769480 | tf_op jit(solution)/shard_map/ppermute | solution.py:526
  (3 other events, 7.6 us)

commit v6 on v5

--- a/solution.py
+++ b/solution.py
@@ -187,7 +187,7 @@
 
 
 def inner_atom_kernel(single_ref, bias_ref, token_ref, qkv_ref, out_w_ref, agg_ref,
-                      proj_ref, hidden_ref, sums_ref, counts_ref, pick_ref, mask_ref):
+                      proj_ref, hidden_ref, sums_ref, counts_ref, pick_ref):
     tok = lax.axis_index("tok")
     proj_ref[...] = projected(single_ref[...], qkv_ref)
     windows = [(QW * w - HALO, QW * w, QW, own_bias(bias_ref, w)) for w in (4, 5, 2, 3)]
@@ -203,7 +203,6 @@
     member = (token_ref[...] - tok * TOKD == wanted_tokens()).astype(F32)
     member = jnp.concatenate([member, jnp.zeros((128 - ROWS, ATOMD), F32)], axis=0)
     pick_ref[...] = member.T.astype(BF16)
-    mask_ref[...] = head_mask().astype(F32).astype(BF16)
 
 
 def atom_kernel(single_ref, apart_ref, beside_ref, bias_ref, token_ref, qkv_ref, out_w_ref, agg_ref,
@@ -327,7 +326,9 @@
     return jnp.dot(weights, rows, preferred_element_type=F32)
 
 
-def near_kernel(query_ref, quad_ref, rest_ref, bias_ref, edge_bias_ref, mixed_ref, maximum_ref, total_ref):
+def near_kernel(query_ref, quad_ref, rest_ref, bias_ref, edge_bias_ref, mixed_ref, maximum_ref, total_ref, *mask_ref):
+    for ref in mask_ref:
+        ref[...] = head_mask().astype(F32).astype(BF16)
     rows = jnp.concatenate([quad_ref[...], rest_ref[...]], axis=0)
     scores = scored(query_ref, rows, bias_ref, edge_bias_ref, 0)
     maximum = along(jnp.max, tree(jnp.maximum, scores))
@@ -452,17 +453,16 @@
         name="bias",
     )(pair_rep, pair_wt)
 
-    *inner, pick, mask = pl.pallas_call(
+    *inner, pick = pl.pallas_call(
         inner_atom_kernel,
         in_specs=[VMEM] * 6,
-        out_specs=[VMEM] * 6,
+        out_specs=[VMEM] * 5,
         out_shape=[
             shape(ATOMD, 3 * CA),
             shape(4 * QW, CA),
             shape(ROWS, C, F32),
             shape(ROWS, 128, F32),
             shape(ATOMD, 128),
-            shape(QROWS, C),
         ],
         compiler_params=params(8),
         cost_estimate=pl.CostEstimate(flops=4 * 10**9, bytes_accessed=16 * 2**20, transcendentals=0),
@@ -524,15 +524,17 @@
         else:
             rest = join(pieces, places, [far_quad])
         far_rest = lax.ppermute(rest, "tok", flips(0, 0, 1))
-        partial = pl.pallas_call(
+        made = pl.pallas_call(
             near_kernel,
             in_specs=[VMEM] * 5,
-            out_specs=[VMEM] * 3,
-            out_shape=[shape(QROWS, C, F32)] + [shape(QROWS, 128, F32)] * 2,
+            out_specs=[VMEM] * (4 - layer),
+            out_shape=[shape(QROWS, C, F32)] + [shape(QROWS, 128, F32)] * 2 + [shape(QROWS, C)] * (1 - layer),
             compiler_params=params(16),
             cost_estimate=pl.CostEstimate(flops=2 * 10**9, bytes_accessed=5 * 2**20, transcendentals=300000),
             name="near",
         )(queries, quad, rest, bias[layer], edge_bias[layer])
+        partial = made[:3]
+        mask = mask if layer else made[3]
         operands = (queries, far_quad, far_rest, bias[layer], edge_bias[layer], *partial, mask, tok_qkv_w, tok_out_w, stream)
         if layer == 0:
             stream, normed, own = pl.pallas_call(

time: 55.1 us -> 55.4 us (level)
    pallas_call x1, Pallas kernels: 1.89 us -> 1.22 us  [local(): pl.pallas_call(inner_atom_kernel, in_specs=[VMEM] * 6, out_specs=[VMEM] *...]
    ppermute x12, starting transfers between devices: 12.4 us -> 13 us  [exchange(): return [lax.ppermute(rows, 'tok', crossed(k, first)) for k in ORDER]]
  transfers between devices with their start and end apart: 20 -> 20, of which waited for: 10 -> 9; matrix products, arithmetic and copies ran while one was open for 0% -> 0% of each run, Pallas kernels for 20% -> 19%
where the time goes in v6:
time: 55.4 us; the launch traced here: 55.3 us
  starting transfers between devices  26 us (47%)
  Pallas kernels  19.3 us (35%)
  waiting for transfers between devices  9.12 us (16%)
  between operations  0.82 us (1%)
    ppermute x12, starting transfers between devices, exchange(): return [lax.ppermute(rows, 'tok', crossed(k, first)) for k in ORDER]  13 us
    ppermute x12, waiting for transfers between devices, exchange(): return [lax.ppermute(rows, 'tok', crossed(k, first)) for k in ORDER]  8.13 us
    ppermute x2, starting transfers between devices, local(): far_rest = lax.ppermute(rest, 'tok', flips(0, 0, 1))  3.68 us
    pallas_call x2, Pallas kernels, local(): pl.pallas_call(near_kernel, in_specs=[VMEM] * 5, out_specs=[VMEM] * (4 -...  3.51 us
    ppermute x1, starting transfers between devices, local(): beside = lax.ppermute(to_beside, 'tok', flips(0, 0, 1))  3.47 us
    pallas_call x1, Pallas kernels, local(): pl.pallas_call(last_kernel, in_specs=[VMEM] * 15, out_specs=[VMEM] * 2, o...  3.27 us
    ppermute x1, starting transfers between devices, local(): apart = lax.ppermute(to_apart, 'tok', across)  2.77 us
    pallas_call x1, Pallas kernels, local(): pl.pallas_call(bias_kernel, in_specs=[VMEM] * 2, out_specs=[VMEM] * 2, ou...  2.64 us
  transfers between devices with their start and end apart: 20, of which 9 were waited for; matrix products, arithmetic and copies ran while one was open for 0% of the time, Pallas kernels for 19%

profile of v6, /device:TPU:1, one launch (start us, length us, event | category | flops | bytes accessed | tf_op | source)
XLA Modules:
  0.0 55.3 jit_solution(1329654978311856549)
XLA Ops:
  0.6 1.2 %pack.1 = (bf16[160,128]{1,0:T(8,128)(2,1)S(1)}, bf16[160,128]{1,0:T(8,128)(2,1)S(1)}, bf16[256,128]{1,0:T(8,128)(2,1)S(1)}, bf16[256,512]{1,0:T(8,128)(2,1)S(1)...) custom-call(bf16[256,128]{1,0:T(8,128)(2,1)} %refs_0_.1, ...), custom_call_target="tpu_custom_call" | custom-call | flops 4000000000 | bytes 16777216 | tf_op jit(solution)/shard_map/pack/pallas_call | solution.py:432
  1.8 2.8 %collective-permute-start = (bf16[160,128]{1,0:T(8,128)(2,1)S(1)}, bf16[160,128]{1,0:T(8,128)(2,1)S(1)}, u32[]{:S(2)}, u32[]{:S(2)}) collective-permute-start(bf16[160,128]{1,0:T(8,128)(2,1)S(1)} %get-tuple-element.38), channel_id=1, source_target_pairs={{0,31},{1,2},{2,1},{3,4},{4,3},{5,6},{6,5},{7,8},{8,7},{9,10},{10,... | collective-permute-start | bytes 122888 | tf_op jit(solution)/shard_map/ppermute | solution.py:443
  4.6 3.5 %collective-permute-start.1 = (bf16[160,128]{1,0:T(8,128)(2,1)S(1)}, bf16[160,128]{1,0:T(8,128)(2,1)S(1)}, u32[]{:S(2)}, u32[]{:S(2)}) collective-permute-start(bf16[160,128]{1,0:T(8,128)(2,1)S(1)} %get-tuple-element.39), channel_id=1, source_target_pairs={{0,1},{1,0},{2,3},{3,2},{4,5},{5,4},{6,7},{7,6},{8,9},{9,8},{10,11... | collective-permute-start | bytes 122888 | tf_op jit(solution)/shard_map/ppermute | solution.py:444
  8.1 1.2 %inner_atoms.1 = (bf16[256,384]{1,0:T(8,128)(2,1)S(1)}, bf16[128,128]{1,0:T(8,128)(2,1)S(1)}, f32[48,768]{1,0:T(8,128)S(1)}, f32[48,128]{1,0:T(8,128)S(1)}, bf16[256,128]{1,0:T(8,128)(2,1)S(1)}) custom-call(bf16[256,128]{1,0:T(8,128)(2,1)S(1)} %get-tuple-element.37.single_ref, bf16[256,512]{1,0:T(8,128)(2,1)S(1)} %get-tuple-element.40.bias_ref, ...), custom_call_target="tpu_custom_call" | custom-call | flops 4000000000 | bytes 16777216 | tf_op jit(solution)/shard_map/inner_atoms/pallas_call | solution.py:456
  9.3 1.5 %atoms.1 = (bf16[256,128]{1,0:T(8,128)(2,1)S(1)}, f32[48,768]{1,0:T(8,128)S(1)}, bf16[48,768]{1,0:T(8,128)(2,1)S(1)}, bf16[32,768]{1,0:T(8,128)(2,1)S(1)}) custom-call(bf16[256,128]{1,0:T(8,128)(2,1)S(1)} %get-tuple-element.37.single_ref, bf16[160,128]{1,0:T(8,128)(2,1)S(1)} %collective-permute-done.apart_ref, ...), custom_call_target="tpu_custom_call" | custom-call | flops 4000000000 | bytes 16777216 | tf_op jit(solution)/shard_map/atoms/pallas_call | solution.py:471
  12.3 1.3 %collective-permute-start.4 = (bf16[32,768]{1,0:T(8,128)(2,1)S(1)}, bf16[32,768]{1,0:T(8,128)(2,1)S(1)}, u32[]{:S(2)}, u32[]{:S(2)}) collective-permute-start(bf16[32,768]{1,0:T(8,128)(2,1)S(1)} %get-tuple-element.51.refs_0_), channel_id=1, source_target_pairs={{0,2},{1,9},{2,0},{3,11},{4,6},{5,13},{6,4},{7,15},{8,10},{9,1},{1... | collective-permute-start | bytes 147464 | tf_op jit(solution)/shard_map/ppermute | solution.py:414
  13.6 1.9 %queries.2 = (bf16[544,768]{1,0:T(8,128)(2,1)S(1)}, bf16[32,1024]{1,0:T(8,128)(2,1)S(1)}, bf16[32,1024]{1,0:T(8,128)(2,1)S(1)}) custom-call(bf16[48,768]{1,0:T(8,128)(2,1)S(1)} %get-tuple-element.49.normed_ref, bf16[2,768,2304]{2,1,0:T(8,128)(2,1)S(1)} %bitcast.3, bf16[32,1024,128]{2,1,0:T(8,128)(2,1)} %pair_ref.1, bf16[32,128]{1,0:T(8,128)(2,1)} %bitcast.6), custom_call_target="tpu_custom_call" | custom-call | flops 1000000000 | bytes 5242880 | tf_op jit(solution)/shard_map/queries/pallas_call | solution.py:485
  16.2 1.7 %collective-permute-start.6 = (bf16[128,768]{1,0:T(8,128)(2,1)S(1)}, bf16[128,768]{1,0:T(8,128)(2,1)S(1)}, u32[]{:S(2)}, u32[]{:S(2)}) collective-permute-start(bf16[128,768]{1,0:T(8,128)(2,1)S(1)} %join.4.quad_ref), channel_id=1, source_target_pairs={{0,16},{1,5},{2,18},{3,7},{4,20},{5,1},{6,22},{7,3},{8,24},{9,13},... | collective-permute-start | bytes 589832 | tf_op jit(solution)/shard_map/ppermute | solution.py:414
  17.9 1.7 %collective-permute-start.7 = (bf16[128,768]{1,0:T(8,128)(2,1)S(1)}, bf16[128,768]{1,0:T(8,128)(2,1)S(1)}, u32[]{:S(2)}, u32[]{:S(2)}) collective-permute-start(bf16[128,768]{1,0:T(8,128)(2,1)S(1)} %join.4.quad_ref), channel_id=1, source_target_pairs={{0,24},{1,7},{2,26},{3,5},{4,28},{5,3},{6,30},{7,1},{8,16},{9,15},... | collective-permute-start | bytes 589832 | tf_op jit(solution)/shard_map/ppermute | solution.py:414
  21.2 1.2 %collective-permute-start.9 = (bf16[32,1024]{1,0:T(8,128)(2,1)S(1)}, bf16[32,1024]{1,0:T(8,128)(2,1)S(1)}, u32[]{:S(2)}, u32[]{:S(2)}) collective-permute-start(bf16[32,1024]{1,0:T(8,128)(2,1)S(1)} %get-tuple-element.52), channel_id=1, source_target_pairs={{0,31},{1,2},{2,1},{3,4},{4,3},{5,6},{6,5},{7,8},{8,7},{9,10},{10,... | collective-permute-start | bytes 196616 | tf_op jit(solution)/shard_map/ppermute | solution.py:499
  22.5 2.6 %bias.1 = (bf16[512,1024]{1,0:T(8,128)(2,1)S(1)}, bf16[512,1024]{1,0:T(8,128)(2,1)S(1)}) custom-call(bf16[32,1024,128]{2,1,0:T(8,128)(2,1)S(1)} %bitcast.5, bf16[32,128]{1,0:T(8,128)(2,1)S(1)} %bitcast.7), custom_call_target="tpu_custom_call" | custom-call | flops 268435456 | bytes 10485760 | tf_op jit(solution)/shard_map/bias/pallas_call | solution.py:446
  26.4 2.7 %collective-permute-start.11 = (bf16[384,768]{1,0:T(8,128)(2,1)S(1)}, bf16[384,768]{1,0:T(8,128)(2,1)S(1)}, u32[]{:S(2)}, u32[]{:S(2)}) collective-permute-start(bf16[384,768]{1,0:T(8,128)(2,1)S(1)} %get-tuple-element.55.rest_ref), channel_id=1, source_target_pairs={{0,1},{1,0},{2,3},{3,2},{4,5},{5,4},{6,7},{7,6},{8,9},{9,8},{10,11... | collective-permute-start | bytes 1769480 | tf_op jit(solution)/shard_map/ppermute | solution.py:526
  29.4 2.0 %near.2 = (f32[544,768]{1,0:T(8,128)S(1)}, f32[544,128]{1,0:T(8,128)S(1)}, f32[544,128]{1,0:T(8,128)S(1)}, bf16[544,768]{1,0:T(8,128)(2,1)S(1)}) custom-call(bf16[544,768]{1,0:T(8,128)(2,1)S(1)} %get-tuple-element.50.refs_4_.query_ref.refs_0_, bf16[128,768]{1,0:T(8,128)(2,1)S(1)} %join.4.quad_ref, bf16[384,768]{1,0:T(8,128)(2,1)S(1)} %get-tuple-element.55.rest_ref, ...), custom_call_target="tpu_custom_call" | custom-call | flops 2000000000 | bytes 5242880 | tf_op jit(solution)/shard_map/near/pallas_call | solution.py:527
  31.4 2.6 %block.1 = (f32[48,768]{1,0:T(8,128)S(1)}, bf16[48,768]{1,0:T(8,128)(2,1)S(1)}, bf16[32,768]{1,0:T(8,128)(2,1)S(1)}) custom-call(bf16[544,768]{1,0:T(8,128)(2,1)S(1)} %get-tuple-element.50.refs_4_.query_ref.refs_0_, bf16[128,768]{1,0:T(8,128)(2,1)S(1)} %collective-permute-done.5.refs_1_, bf16[384,768]{1,0:T(8,128)(2,1)S(1)} %collective-permute-done.11.refs_2_, ...), custom_call_target="tpu_custom_call" | custom-call | tf_op jit(solution)/shard_map/block/pallas_call | solution.py:540
  34.0 1.5 %collective-permute-start.12 = (bf16[32,768]{1,0:T(8,128)(2,1)S(1)}, bf16[32,768]{1,0:T(8,128)(2,1)S(1)}, u32[]{:S(2)}, u32[]{:S(2)}) collective-permute-start(bf16[32,768]{1,0:T(8,128)(2,1)S(1)} %get-tuple-element.63.refs_0_), channel_id=1, source_target_pairs={{0,4},{1,17},{2,6},{3,19},{4,0},{5,21},{6,2},{7,23},{8,12},{9,25},... | collective-permute-start | bytes 147464 | tf_op jit(solution)/shard_map/ppermute | solution.py:414
  35.5 1.5 %collective-permute-start.13 = (bf16[32,768]{1,0:T(8,128)(2,1)S(1)}, bf16[32,768]{1,0:T(8,128)(2,1)S(1)}, u32[]{:S(2)}, u32[]{:S(2)}) collective-permute-start(bf16[32,768]{1,0:T(8,128)(2,1)S(1)} %get-tuple-element.63.refs_0_), channel_id=1, source_target_pairs={{0,6},{1,25},{2,4},{3,27},{4,2},{5,29},{6,0},{7,31},{8,14},{9,17},... | collective-permute-start | bytes 147464 | tf_op jit(solution)/shard_map/ppermute | solution.py:414
  37.0 1.4 %queries.3.refs_4_.query_ref.refs_0_ = bf16[544,768]{1,0:T(8,128)(2,1)S(1)} custom-call(bf16[48,768]{1,0:T(8,128)(2,1)S(1)} %get-tuple-element.62.normed_ref, bf16[2,768,2304]{2,1,0:T(8,128)(2,1)S(1)} %bitcast.3), custom_call_target="tpu_custom_call" | custom-call | flops 1000000000 | bytes 5242880 | tf_op jit(solution)/shard_map/queries/pallas_call | solution.py:501
  38.5 1.3 %collective-permute-done.13.refs_2_ = bf16[32,768]{1,0:T(8,128)(2,1)S(1)} collective-permute-done((bf16[32,768]{1,0:T(8,128)(2,1)S(1)}, bf16[32,768]{1,0:T(8,128)(2,1)S(1)}, u32[]{:S(2)}, u32[]{:S(2)}) %collective-permute-start.13) | collective-permute-done | bytes 49184 | tf_op jit(solution)/shard_map/ppermute | solution.py:414
  40.9 1.2 %collective-permute-start.16 = (bf16[128,768]{1,0:T(8,128)(2,1)S(1)}, bf16[128,768]{1,0:T(8,128)(2,1)S(1)}, u32[]{:S(2)}, u32[]{:S(2)}) collective-permute-start(bf16[128,768]{1,0:T(8,128)(2,1)S(1)} %join.6.quad_ref), channel_id=1, source_target_pairs={{0,16},{1,5},{2,18},{3,7},{4,20},{5,1},{6,22},{7,3},{8,24},{9,13},... | collective-permute-start | bytes 589832 | tf_op jit(solution)/shard_map/ppermute | solution.py:414
  42.0 2.1 %collective-permute-start.17 = (bf16[128,768]{1,0:T(8,128)(2,1)S(1)}, bf16[128,768]{1,0:T(8,128)(2,1)S(1)}, u32[]{:S(2)}, u32[]{:S(2)}) collective-permute-start(bf16[128,768]{1,0:T(8,128)(2,1)S(1)} %join.6.quad_ref), channel_id=1, source_target_pairs={{0,24},{1,7},{2,26},{3,5},{4,28},{5,3},{6,30},{7,1},{8,16},{9,15},... | collective-permute-start | bytes 589832 | tf_op jit(solution)/shard_map/ppermute | solution.py:414
  44.1 3.1 %collective-permute-done.16.refs_0_ = bf16[128,768]{1,0:T(8,128)(2,1)S(1)} collective-permute-done((bf16[128,768]{1,0:T(8,128)(2,1)S(1)}, bf16[128,768]{1,0:T(8,128)(2,1)S(1)}, u32[]{:S(2)}, u32[]{:S(2)}) %collective-permute-start.16) | collective-permute-done | bytes 196640 | tf_op jit(solution)/shard_map/ppermute | solution.py:414
  47.2 2.1 %collective-permute-done.17.refs_1_ = bf16[128,768]{1,0:T(8,128)(2,1)S(1)} collective-permute-done((bf16[128,768]{1,0:T(8,128)(2,1)S(1)}, bf16[128,768]{1,0:T(8,128)(2,1)S(1)}, u32[]{:S(2)}, u32[]{:S(2)}) %collective-permute-start.17) | collective-permute-done | bytes 196640 | tf_op jit(solution)/shard_map/ppermute | solution.py:414
  50.4 1.5 %near.3 = (f32[544,768]{1,0:T(8,128)S(1)}, f32[544,128]{1,0:T(8,128)S(1)}, f32[544,128]{1,0:T(8,128)S(1)}) custom-call(bf16[544,768]{1,0:T(8,128)(2,1)S(1)} %queries.3.refs_4_.query_ref.refs_0_, bf16[128,768]{1,0:T(8,128)(2,1)S(1)} %join.6.quad_ref, bf16[384,768]{1,0:T(8,128)(2,1)S(1)} %join.7.rest_ref, ...), custom_call_target="tpu_custom_call" | custom-call | flops 2000000000 | bytes 5242880 | tf_op jit(solution)/shard_map/near/pallas_call | solution.py:527
  52.0 3.3 %block_and_broadcast.1 = (bf16[256,128]{1,0:T(8,128)(2,1)}, bf16[32,768]{1,0:T(8,128)(2,1)}) custom-call(bf16[544,768]{1,0:T(8,128)(2,1)S(1)} %queries.3.refs_4_.query_ref.refs_0_, bf16[128,768]{1,0:T(8,128)(2,1)S(1)} %collective-permute-done.15.refs_3_.refs_1_, bf16[384,768]{1,0:T(8,128)(2,1)S(1)} %collective-permute-done.19.refs_2_, ...), custom_call_target="tpu_custom_call" | custom-call | tf_op jit(solution)/shard_map/block_and_broadcast/pallas_call | solution.py:549
  (46 shorter events, 7.6 us)
Async XLA Ops:
  1.8 7.5 %collective-permute-start = (bf16[160,128]{1,0:T(8,128)(2,1)S(1)}, bf16[160,128]{1,0:T(8,128)(2,1)S(1)}, u32[]{:S(2)}, u32[]{:S(2)}) collective-permute-start(bf16[160,128]{1,0:T(8,128)(2,1)S(1)} %get-tuple-element.38), channel_id=1, source_target_pairs={{0,31},{1,2},{2,1},{3,4},{4,3},{5,6},{6,5},{7,8},{8,7},{9,10},{10,... | collective-permute-start | bytes 122888 | tf_op jit(solution)/shard_map/ppermute | solution.py:443
  4.6 4.7 %collective-permute-start.1 = (bf16[160,128]{1,0:T(8,128)(2,1)S(1)}, bf16[160,128]{1,0:T(8,128)(2,1)S(1)}, u32[]{:S(2)}, u32[]{:S(2)}) collective-permute-start(bf16[160,128]{1,0:T(8,128)(2,1)S(1)} %get-tuple-element.39), channel_id=1, source_target_pairs={{0,1},{1,0},{2,3},{3,2},{4,5},{5,4},{6,7},{7,6},{8,9},{9,8},{10,11... | collective-permute-start | bytes 122888 | tf_op jit(solution)/shard_map/ppermute | solution.py:444
  9.3 4.3 %slice-start = ((s8[7077888]{0:T(1024)(128)(4,1)}), s8[4194304]{0:T(1024)(128)(4,1)S(1)}, s32[]{:S(2)}) async-start(s8[7077888]{0:T(1024)(128)(4,1)} %bitcast.2), calls=%async_computation | async-start | bytes 8388608
  10.8 4.7 %collective-permute-start.2 = (bf16[32,768]{1,0:T(8,128)(2,1)S(1)}, bf16[32,768]{1,0:T(8,128)(2,1)S(1)}, u32[]{:S(2)}, u32[]{:S(2)}) collective-permute-start(bf16[32,768]{1,0:T(8,128)(2,1)S(1)} %get-tuple-element.51.refs_0_), channel_id=1, source_target_pairs={{0,4},{1,17},{2,6},{3,19},{4,0},{5,21},{6,2},{7,23},{8,12},{9,25},... | collective-permute-start | bytes 147464 | tf_op jit(solution)/shard_map/ppermute | solution.py:414
  11.4 4.7 %collective-permute-start.3 = (bf16[32,768]{1,0:T(8,128)(2,1)S(1)}, bf16[32,768]{1,0:T(8,128)(2,1)S(1)}, u32[]{:S(2)}, u32[]{:S(2)}) collective-permute-start(bf16[32,768]{1,0:T(8,128)(2,1)S(1)} %get-tuple-element.51.refs_0_), channel_id=1, source_target_pairs={{0,6},{1,25},{2,4},{3,27},{4,2},{5,29},{6,0},{7,31},{8,14},{9,17},... | collective-permute-start | bytes 147464 | tf_op jit(solution)/shard_map/ppermute | solution.py:414
  12.3 3.9 %collective-permute-start.4 = (bf16[32,768]{1,0:T(8,128)(2,1)S(1)}, bf16[32,768]{1,0:T(8,128)(2,1)S(1)}, u32[]{:S(2)}, u32[]{:S(2)}) collective-permute-start(bf16[32,768]{1,0:T(8,128)(2,1)S(1)} %get-tuple-element.51.refs_0_), channel_id=1, source_target_pairs={{0,2},{1,9},{2,0},{3,11},{4,6},{5,13},{6,4},{7,15},{8,10},{9,1},{1... | collective-permute-start | bytes 147464 | tf_op jit(solution)/shard_map/ppermute | solution.py:414
  13.6 8.9 %slice-start.2 = ((s8[8388608]{0:T(1024)(128)(4,1)}), s8[4194304]{0:T(1024)(128)(4,1)S(1)}, s32[]{:S(2)}) async-start(s8[8388608]{0:T(1024)(128)(4,1)} %bitcast.4), calls=%async_computation.2 | async-start | bytes 8388608
  13.6 8.9 %slice-start.3 = ((s8[8388608]{0:T(1024)(128)(4,1)}), s8[4194304]{0:T(1024)(128)(4,1)S(1)}, s32[]{:S(2)}) async-start(s8[8388608]{0:T(1024)(128)(4,1)} %bitcast.4), calls=%async_computation.3 | async-start | bytes 8388608
  13.6 8.9 %copy-start.2 = (bf16[128,32]{0,1:T(8,128)(2,1)S(1)}, bf16[128,32]{0,1:T(8,128)(2,1)}, u32[]{:S(2)}) copy-start(bf16[128,32]{0,1:T(8,128)(2,1)} %param.21) | copy-start | bytes 24580
  16.2 9.7 %collective-permute-start.6 = (bf16[128,768]{1,0:T(8,128)(2,1)S(1)}, bf16[128,768]{1,0:T(8,128)(2,1)S(1)}, u32[]{:S(2)}, u32[]{:S(2)}) collective-permute-start(bf16[128,768]{1,0:T(8,128)(2,1)S(1)} %join.4.quad_ref), channel_id=1, source_target_pairs={{0,16},{1,5},{2,18},{3,7},{4,20},{5,1},{6,22},{7,3},{8,24},{9,13},... | collective-permute-start | bytes 589832 | tf_op jit(solution)/shard_map/ppermute | solution.py:414
  17.9 8.0 %collective-permute-start.7 = (bf16[128,768]{1,0:T(8,128)(2,1)S(1)}, bf16[128,768]{1,0:T(8,128)(2,1)S(1)}, u32[]{:S(2)}, u32[]{:S(2)}) collective-permute-start(bf16[128,768]{1,0:T(8,128)(2,1)S(1)} %join.4.quad_ref), channel_id=1, source_target_pairs={{0,24},{1,7},{2,26},{3,5},{4,28},{5,3},{6,30},{7,1},{8,16},{9,15},... | collective-permute-start | bytes 589832 | tf_op jit(solution)/shard_map/ppermute | solution.py:414
  19.7 6.7 %collective-permute-start.8 = (bf16[128,768]{1,0:T(8,128)(2,1)S(1)}, bf16[128,768]{1,0:T(8,128)(2,1)S(1)}, u32[]{:S(2)}, u32[]{:S(2)}) collective-permute-start(bf16[128,768]{1,0:T(8,128)(2,1)S(1)} %join.4.quad_ref), channel_id=1, source_target_pairs={{0,8},{1,3},{2,10},{3,1},{4,12},{5,7},{6,14},{7,5},{8,0},{9,11},{1... | collective-permute-start | bytes 589832 | tf_op jit(solution)/shard_map/ppermute | solution.py:414
  20.2 4.9 %collective-permute-start.10 = (bf16[32,1024]{1,0:T(8,128)(2,1)S(1)}, bf16[32,1024]{1,0:T(8,128)(2,1)S(1)}, u32[]{:S(2)}, u32[]{:S(2)}) collective-permute-start(bf16[32,1024]{1,0:T(8,128)(2,1)S(1)} %get-tuple-element.53), channel_id=1, source_target_pairs={{0,1},{1,0},{2,3},{3,2},{4,5},{5,4},{6,7},{7,6},{8,9},{9,8},{10,11... | collective-permute-start | bytes 196616 | tf_op jit(solution)/shard_map/ppermute | solution.py:499
  21.2 4.8 %collective-permute-start.9 = (bf16[32,1024]{1,0:T(8,128)(2,1)S(1)}, bf16[32,1024]{1,0:T(8,128)(2,1)S(1)}, u32[]{:S(2)}, u32[]{:S(2)}) collective-permute-start(bf16[32,1024]{1,0:T(8,128)(2,1)S(1)} %get-tuple-element.52), channel_id=1, source_target_pairs={{0,31},{1,2},{2,1},{3,4},{4,3},{5,6},{6,5},{7,8},{8,7},{9,10},{10,... | collective-permute-start | bytes 196616 | tf_op jit(solution)/shard_map/ppermute | solution.py:499
  26.4 5.0 %collective-permute-start.11 = (bf16[384,768]{1,0:T(8,128)(2,1)S(1)}, bf16[384,768]{1,0:T(8,128)(2,1)S(1)}, u32[]{:S(2)}, u32[]{:S(2)}) collective-permute-start(bf16[384,768]{1,0:T(8,128)(2,1)S(1)} %get-tuple-element.55.rest_ref), channel_id=1, source_target_pairs={{0,1},{1,0},{2,3},{3,2},{4,5},{5,4},{6,7},{7,6},{8,9},{9,8},{10,11... | collective-permute-start | bytes 1769480 | tf_op jit(solution)/shard_map/ppermute | solution.py:526
  29.1 2.3 %collective-permute-start.5 = (bf16[128,768]{1,0:T(8,128)(2,1)S(1)}, bf16[128,768]{1,0:T(8,128)(2,1)S(1)}, u32[]{:S(2)}, u32[]{:S(2)}) collective-permute-start(bf16[128,768]{1,0:T(8,128)(2,1)S(1)} %join.4.quad_ref), channel_id=1, source_target_pairs={{0,1},{1,0},{2,3},{3,2},{4,5},{5,4},{6,7},{7,6},{8,9},{9,8},{10,11... | collective-permute-start | bytes 589832 | tf_op jit(solution)/shard_map/ppermute | solution.py:511
  34.0 4.5 %collective-permute-start.12 = (bf16[32,768]{1,0:T(8,128)(2,1)S(1)}, bf16[32,768]{1,0:T(8,128)(2,1)S(1)}, u32[]{:S(2)}, u32[]{:S(2)}) collective-permute-start(bf16[32,768]{1,0:T(8,128)(2,1)S(1)} %get-tuple-element.63.refs_0_), channel_id=1, source_target_pairs={{0,4},{1,17},{2,6},{3,19},{4,0},{5,21},{6,2},{7,23},{8,12},{9,25},... | collective-permute-start | bytes 147464 | tf_op jit(solution)/shard_map/ppermute | solution.py:414
  35.5 4.3 %collective-permute-start.13 = (bf16[32,768]{1,0:T(8,128)(2,1)S(1)}, bf16[32,768]{1,0:T(8,128)(2,1)S(1)}, u32[]{:S(2)}, u32[]{:S(2)}) collective-permute-start(bf16[32,768]{1,0:T(8,128)(2,1)S(1)} %get-tuple-element.63.refs_0_), channel_id=1, source_target_pairs={{0,6},{1,25},{2,4},{3,27},{4,2},{5,29},{6,0},{7,31},{8,14},{9,17},... | collective-permute-start | bytes 147464 | tf_op jit(solution)/shard_map/ppermute | solution.py:414
  37.0 3.2 %collective-permute-start.14 = (bf16[32,768]{1,0:T(8,128)(2,1)S(1)}, bf16[32,768]{1,0:T(8,128)(2,1)S(1)}, u32[]{:S(2)}, u32[]{:S(2)}) collective-permute-start(bf16[32,768]{1,0:T(8,128)(2,1)S(1)} %get-tuple-element.63.refs_0_), channel_id=1, source_target_pairs={{0,2},{1,9},{2,0},{3,11},{4,6},{5,13},{6,4},{7,15},{8,10},{9,1},{1... | collective-permute-start | bytes 147464 | tf_op jit(solution)/shard_map/ppermute | solution.py:414
  40.3 3.8 %collective-permute-start.15 = (bf16[128,768]{1,0:T(8,128)(2,1)S(1)}, bf16[128,768]{1,0:T(8,128)(2,1)S(1)}, u32[]{:S(2)}, u32[]{:S(2)}) collective-permute-start(bf16[128,768]{1,0:T(8,128)(2,1)S(1)} %join.6.quad_ref), channel_id=1, source_target_pairs={{0,1},{1,0},{2,3},{3,2},{4,5},{5,4},{6,7},{7,6},{8,9},{9,8},{10,11... | collective-permute-start | bytes 589832 | tf_op jit(solution)/shard_map/ppermute | solution.py:511
  40.9 6.3 %collective-permute-start.16 = (bf16[128,768]{1,0:T(8,128)(2,1)S(1)}, bf16[128,768]{1,0:T(8,128)(2,1)S(1)}, u32[]{:S(2)}, u32[]{:S(2)}) collective-permute-start(bf16[128,768]{1,0:T(8,128)(2,1)S(1)} %join.6.quad_ref), channel_id=1, source_target_pairs={{0,16},{1,5},{2,18},{3,7},{4,20},{5,1},{6,22},{7,3},{8,24},{9,13},... | collective-permute-start | bytes 589832 | tf_op jit(solution)/shard_map/ppermute | solution.py:414
  42.0 7.2 %collective-permute-start.17 = (bf16[128,768]{1,0:T(8,128)(2,1)S(1)}, bf16[128,768]{1,0:T(8,128)(2,1)S(1)}, u32[]{:S(2)}, u32[]{:S(2)}) collective-permute-start(bf16[128,768]{1,0:T(8,128)(2,1)S(1)} %join.6.quad_ref), channel_id=1, source_target_pairs={{0,24},{1,7},{2,26},{3,5},{4,28},{5,3},{6,30},{7,1},{8,16},{9,15},... | collective-permute-start | bytes 589832 | tf_op jit(solution)/shard_map/ppermute | solution.py:414
  44.1 5.2 %collective-permute-start.18 = (bf16[128,768]{1,0:T(8,128)(2,1)S(1)}, bf16[128,768]{1,0:T(8,128)(2,1)S(1)}, u32[]{:S(2)}, u32[]{:S(2)}) collective-permute-start(bf16[128,768]{1,0:T(8,128)(2,1)S(1)} %join.6.quad_ref), channel_id=1, source_target_pairs={{0,8},{1,3},{2,10},{3,1},{4,12},{5,7},{6,14},{7,5},{8,0},{9,11},{1... | collective-permute-start | bytes 589832 | tf_op jit(solution)/shard_map/ppermute | solution.py:414
  49.3 2.7 %collective-permute-start.19 = (bf16[384,768]{1,0:T(8,128)(2,1)S(1)}, bf16[384,768]{1,0:T(8,128)(2,1)S(1)}, u32[]{:S(2)}, u32[]{:S(2)}) collective-permute-start(bf16[384,768]{1,0:T(8,128)(2,1)S(1)} %join.7.rest_ref), channel_id=1, source_target_pairs={{0,1},{1,0},{2,3},{3,2},{4,5},{5,4},{6,7},{7,6},{8,9},{9,8},{10,11... | collective-permute-start | bytes 1769480 | tf_op jit(solution)/shard_map/ppermute | solution.py:526
  (3 other events, 8.0 us)
